TPU v7x, 256 devices: a whole 4x4x8 slice. The times are simulated.
256 devices in a mesh: group: 8 (over z_hi, y), blk: 32 (over x, z_lo, core).
Axes of the slice: x: 4, y: 4, z: 8 (z_hi: 2, z_lo: 4; z = z_hi * 4 + z_lo), core: 2. Of those that a mesh axis runs over, the one named last changes fastest.
Arguments:
- picture_embeddings: float32 [16384, 1152], P('blk'), may hold values from -4 to 4
- caption_embeddings: float32 [16384, 1152], P(('group', 'blk')), may hold values from -4 to 4
- exponent_of_sharpness: float32 [1], replicated, may hold values from 2.2 to 2.8
- offset_shift: float32 [1], replicated, may hold values from -9 to -6
Outputs:
- picture_embedding_slope: float32 [16384, 1152], P('blk')
- text_grad: float32 [16384, 1152], P(('group', 'blk'))
- statistics: float32 [3], replicated
All inputs are finite; a program needn't handle non-finite values.
Results may differ from a plain program's by a relative error of at most 0.0015.
Values may be sent and summed in bfloat16 or wider, within the bound.
No kernel may reach another device: no remote copies, remote signals or barrier semaphores. Data moves between devices by JAX's collectives and lax.ppermute only.
A program may use at most 64 MiB of HBM per device.

v0:
```python
import jax
import jax.numpy as jnp
from jax import lax
from jax.sharding import PartitionSpec as P


def normalize_rows(matrix):
    inverse_norm = lax.rsqrt(jnp.sum(matrix * matrix, axis=1, keepdims=True) + 1e-06)
    return (matrix * inverse_norm, inverse_norm)


def unit_backward(grad, unit_rows, inverse_norm):
    return (grad - unit_rows * jnp.sum(unit_rows * grad, axis=1, keepdims=True)) * inverse_norm


def per_device(picture_embeddings, caption_embeddings, exponent_of_sharpness, offset_shift):
    row_count = picture_embeddings.shape[0]
    unit_image, inv_image = normalize_rows(picture_embeddings)
    unit_text, inv_text = normalize_rows(caption_embeddings)
    image_rows = unit_image.astype(jnp.bfloat16)
    text_matrix_rows = unit_text.astype(jnp.bfloat16)
    sharpness_factor = jnp.exp(exponent_of_sharpness[0])
    bias_scalar = offset_shift[0]
    rows_overall = row_count * lax.axis_size("blk")
    first_row = lax.axis_index("blk") * row_count
    all_texts = lax.all_gather(text_matrix_rows, "blk", axis=0, tiled=True)
    first_column = lax.axis_index("group") * all_texts.shape[0]
    dot_products = jnp.dot(image_rows, all_texts.T, preferred_element_type=jnp.float32)
    row_ids = lax.broadcasted_iota(jnp.int32, dot_products.shape, 0) + first_row
    column_ids = lax.broadcasted_iota(jnp.int32, dot_products.shape, 1) + first_column
    signs = jnp.where(row_ids == column_ids, 1.0, -1.0).astype(jnp.float32)
    logit_matrix = sharpness_factor * dot_products + bias_scalar
    pair_loss = jax.nn.softplus(-signs * logit_matrix)
    coeff = -signs * jax.nn.sigmoid(-signs * logit_matrix)
    coefficient_rows = coeff.astype(jnp.bfloat16)
    local_sums = (jnp.sum(pair_loss), jnp.sum(coeff * dot_products), jnp.sum(coeff))
    image_contribution = sharpness_factor * jnp.dot(
        coefficient_rows, all_texts, preferred_element_type=jnp.float32
    )
    complete_contribution = sharpness_factor * lax.dot_general(
        coefficient_rows, image_rows, (((0,), (0,)), ((), ())), preferred_element_type=jnp.float32
    )
    text_unit_grad = lax.psum_scatter(complete_contribution, "blk", scatter_dimension=0, tiled=True)
    image_unit_grad = lax.psum(image_contribution, "group")
    picture_embedding_slope = unit_backward(image_unit_grad, unit_image, inv_image)
    loss_total, scale_total, bias_total = lax.psum(
        (local_sums[0], local_sums[1], local_sums[2]), ("group", "blk")
    )
    statistics = jnp.stack([loss_total, sharpness_factor * scale_total, bias_total]) / rows_overall
    text_grad = unit_backward(text_unit_grad, unit_text, inv_text)
    return (picture_embedding_slope, text_grad, statistics)


def solution(mesh):
    placed = (P("blk", None), P(("group", "blk"), None), P(), P())
    return jax.shard_map(
        per_device,
        mesh=mesh,
        in_specs=placed,
        out_specs=(P("blk", None), P(("group", "blk"), None), P()),
        check_vma=False,
    )
```

profile of v0, /device:TPU:24, one launch (start us, length us, event | category | flops | bytes accessed | tf_op | source)
XLA Modules:
  0.0 410.7 jit_solution(17088176144387666569)
XLA Ops:
  7.2 0.0 all-gather.2.cloned.1.call-start
  7.2 1.1 multiply_reduce_fusion.4
  8.3 1.7 multiply_convert_fusion.1
  10.0 0.0 all-gather.2.cloned.1.call-update
  10.1 0.0 all-reduce.3.cloned.1.call-start
  11.5 1.9 multiply_reduce_fusion.2
  13.4 63.7 %all-gather.2.cloned.1.call-done = bf16[2048,1152]{1,0:T(8,128)(2,1)} async-done(((bf16[64,1152]{1,0:T(8,128)(2,1)}), bf16[2048,1152]{1,0:T(8,128)(2,1)}) %all-gather.2.cloned.1.call-update) | async-done | bytes 4718608 | tf_op jit(solution)/shard_map/all_gather | solution.py:26
  77.0 0.0 copy-start.3
  77.0 10.4 %fusion = (f32[]{:T(128)}, f32[]{:T(128)}, f32[]{:T(128)}, f32[512,2048]{1,0:T(8,128)S(1)}) fusion(f32[]{:T(128)} %bitcast.8, f32[]{:T(128)} %bitcast, s32[2048]{0:T(1024)S(1)} %iota_add_fusion, s32[512]{0:T(512)S(1)} %iota_add_fusion.1, bf16[2048,1152]{1,0:T(8,128)(2,1)} %all-gather.2.cloned.1.call-done, f32[512,1152]{1,0:T(8,128)} %param.4, ...), kind=kOutput, calls=%fused_computation.2 | convolution fusion | flops 2438070272 | bytes 11284500 | tf_op jit(solution)/shard_map/dot_general | solution.py:28
  87.5 0.0 copy-start.4
  87.5 2.1 copy-done.4
  89.6 0.0 copy-done.3
  89.6 0.0 copy-start
  89.6 5.5 %convolution_multiply_fusion.1 = f32[512,1152]{1,0:T(8,128)} fusion(bf16[2048,1152]{1,0:T(8,128)(2,1)S(1)} %copy-done.3, f32[]{:T(128)} %bitcast, f32[512,2048]{1,0:T(8,128)S(1)} %get-tuple-element.9, f32[]{:T(128)} %bitcast.7, s32[2048]{0:T(1024)S(1)} %iota_add_fusion, s32[512]{0:T(512)S(1)} %iota_add_fusion.1), kind=kOutput, calls=%fused_computation.7 | convolution fusion | flops 2428043264 | bytes 11282440 | tf_op jit(solution)/shard_map/dot_general | solution.py:37
  95.0 0.0 all-reduce.3.cloned.1.call-update
  95.1 0.2 reduce-scatter.2.cloned.1.call-start
  95.3 0.0 copy-done
  95.3 9.8 %convolution_multiply_fusion = f32[2048,1152]{1,0:T(8,128)} fusion(f32[]{:T(128)} %bitcast, f32[512,1152]{1,0:T(8,128)S(1)} %copy-done, f32[512]{0:T(512)S(1)} %add_rsqrt_fusion, f32[512,2048]{1,0:T(8,128)} %copy-done.4, f32[]{:T(128)} %bitcast.9, s32[2048]{0:T(1024)S(1)} %iota_add_fusion, s32[512]{0:T(512)S(1)} %iota_add_fusion.1), kind=kOutput, calls=%fused_computation.1 | convolution fusion | flops 2430992384 | bytes 16003080 | tf_op jit(solution)/shard_map/dot_general | solution.py:40
  105.1 0.0 reduce-scatter.2.cloned.1.call-update
  105.1 89.0 %all-reduce = (f32[1]{0:T(128)}, f32[]{:T(128)}, f32[1]{0:T(128)}) all-reduce(f32[1]{0:T(128)} %bitcast.4, f32[]{:T(128)} %get-tuple-element.5, f32[1]{0:T(128)} %bitcast.2), channel_id=1, replica_groups=mesh['group'=8,'blk'=32] {'group','blk'}, use_global_device_ids=true, to_apply=%region_11.12 | all-reduce | flops 3 | bytes 24 | tf_op jit(solution)/shard_map/psum | solution.py:46
  194.7 1.8 maximum_multiply_fusion
  196.5 39.2 %all-reduce.3.cloned.1.call-done = f32[512,1152]{1,0:T(8,128)} async-done(((f32[512,1152]{1,0:T(8,128)}), f32[512,1152]{1,0:T(8,128)}) %all-reduce.3.cloned.1.call-update) | async-done | bytes 2359312 | tf_op jit(solution)/shard_map/psum | solution.py:44
  235.6 0.0 copy-start.1
  235.6 2.3 multiply_reduce_fusion.1
  237.9 0.1 copy-done.1
  238.0 0.0 copy-start.2
  238.0 1.8 subtract_multiply_fusion
  239.8 161.3 %reduce-scatter.2.cloned.1.call-done = f32[64,1152]{1,0:T(8,128)} async-done(((f32[2048,1152]{1,0:T(8,128)}), f32[64,1152]{1,0:T(8,128)}) %reduce-scatter.2.cloned.1.call-update) | async-done | bytes 294928 | tf_op jit(solution)/shard_map/reduce_scatter | solution.py:43
  401.1 0.0 copy-done.2
  401.2 1.2 multiply_reduce_fusion.3
  402.3 1.8 subtract_multiply_fusion.1
  (4 shorter events, 0.0 us)
Async XLA Ops:
  7.2 69.9 %all-gather.2.cloned.1.call-start = ((), (), s32[]{:S(2)}) async-start(), calls=%async_computation.1 | async-start | bytes 4866048 | tf_op jit(solution)/shard_map/all_gather | solution.py:26
  10.1 225.6 %all-reduce.3.cloned.1.call-start = ((), (), s32[]{:S(2)}) async-start(), calls=%async_computation.2 | async-start | bytes 4718592 | tf_op jit(solution)/shard_map/psum | solution.py:44
  77.0 12.5 %copy-start.3 = (bf16[2048,1152]{1,0:T(8,128)(2,1)S(1)}, bf16[2048,1152]{1,0:T(8,128)(2,1)}, u32[]{:S(2)}) copy-start(bf16[2048,1152]{1,0:T(8,128)(2,1)} %all-gather.2.cloned.1.call-done) | copy-start | bytes 14155780
  87.5 2.1 copy-start.4
  89.6 5.7 %copy-start = (f32[512,1152]{1,0:T(8,128)S(1)}, f32[512,1152]{1,0:T(8,128)}, u32[]{:S(2)}) copy-start(f32[512,1152]{1,0:T(8,128)} %param.4) | copy-start | bytes 7077892
  95.1 306.1 %reduce-scatter.2.cloned.1.call-start = ((), (), s32[]{:S(2)}) async-start(), calls=%async_computation.3 | async-start | bytes 9732096 | tf_op jit(solution)/shard_map/reduce_scatter | solution.py:43
  235.6 2.4 copy-start.1
  238.0 163.2 %copy-start.2 = (f32[64,1152]{1,0:T(8,128)S(1)}, f32[64,1152]{1,0:T(8,128)}, u32[]{:S(2)}) copy-start(f32[64,1152]{1,0:T(8,128)} %param.5) | copy-start | bytes 884740
Sparse Core Ops, SparseCore 0:
  10.4 66.5 all-gather.1
  95.2 140.3 all-reduce.2
  238.2 162.9 reduce-scatter.1
where the time goes:
time: 411 us
  waiting for transfers between devices  264 us (64%)
  blocking collectives  89 us (22%)
  matrix products  25.7 us (6%)
  between operations  15.8 us (4%)
  other arithmetic  13.5 us (3%)
    reduce_scatter x1, waiting for transfers between devices, per_device(): lax.psum_scatter(complete_contribution, 'blk', scatter_dimension=0, tiled...  161 us
    psum x1, blocking collectives, per_device(): lax.psum((local_sums[0], local_sums[1], local_sums[2]), ('group', 'blk'))  89 us
    all_gather x1, waiting for transfers between devices, per_device(): all_texts = lax.all_gather(text_matrix_rows, 'blk', axis=0, tiled=True)  63.7 us
    psum x1, waiting for transfers between devices, per_device(): image_unit_grad = lax.psum(image_contribution, 'group')  39.2 us
    dot_general x1, matrix products, per_device(): jnp.dot(image_rows, all_texts.T, preferred_element_type=jnp.float32)  10.4 us
    dot_general x1, matrix products, per_device(): lax.dot_general(coefficient_rows, image_rows, (((0,), (0,)), ((), ())), p...  9.75 us
  transfers between devices with their start and end apart: 3, of which 3 were waited for; matrix products, arithmetic and copies ran while one was open for 4% of the time, Pallas kernels for 0%

commit v1 on v0

v1 whole, which is shorter than its diff:
```python
import jax
import jax.numpy as jnp
from jax import lax
from jax.experimental import pallas as pl
from jax.experimental.pallas import tpu as pltpu
from jax.sharding import PartitionSpec as P

AXES = ("group", "blk")
NEAR = (0, -1, 1, 2)
SEND = jnp.float16


def device_index(z, y, x, core):
    return (((z // 4) * 4 + y) * 4 + x) * 8 + (z % 4) * 2 + core


def shifted(dz=0, dy=0, dx=0, swap=0):
    pairs = []
    for z in range(8):
        for y in range(4):
            for x in range(4):
                for core in range(2):
                    there = device_index((z + dz) % 8, (y + dy) % 4, (x + dx) % 4, core ^ swap)
                    pairs.append((device_index(z, y, x, core), there))
    return pairs


def move(value, **shift):
    return lax.ppermute(value, AXES, shifted(**shift))


def normalize_rows(matrix):
    inverse_norm = lax.rsqrt(jnp.sum(matrix * matrix, axis=1, keepdims=True) + 1e-06)
    return (matrix * inverse_norm, inverse_norm)


def fused_kernel(row_chunk, scal_ref, base_ref, ids_ref, other_ref, own_ref, text_ref,
                 gi_ref, gt_ref, stat_ref, coef_ref, image_ref):
    step = pl.program_id(0)
    half = pl.num_programs(0) // 2
    bias = scal_ref[1]
    temperature = scal_ref[0]
    first = jnp.where(step < half, base_ref[0], base_ref[1]) + (step % half) * row_chunk
    rows = pl.ds(pl.multiple_of(step * row_chunk, row_chunk), row_chunk)

    @pl.when(step < half)
    def _():
        image_ref[rows, :] = other_ref[...]

    @pl.when(step >= half)
    def _():
        image_ref[rows, :] = own_ref[...]

    text = text_ref[...]
    products = lax.dot_general(
        image_ref[rows, :], text, (((1,), (1,)), ((), ())), preferred_element_type=jnp.float32
    )
    logits = temperature * products + bias
    row_ids = lax.broadcasted_iota(jnp.int32, products.shape, 0) + first
    paired = row_ids == ids_ref[...]
    negated = jnp.where(paired, -logits, logits)
    decay = jnp.exp(-jnp.abs(negated))
    loss = jnp.maximum(negated, 0.0) + jnp.log1p(decay)
    share = 1.0 / (1.0 + decay)
    sigmoid = jnp.where(negated >= 0.0, share, decay * share)
    coeff = jnp.where(paired, -sigmoid, sigmoid)
    coef_ref[rows, :] = coeff.astype(jnp.bfloat16)
    gi_ref[...] = jnp.dot(coef_ref[rows, :], text, preferred_element_type=jnp.float32)

    @pl.when(step == 0)
    def _():
        stat_ref[...] = jnp.zeros_like(stat_ref)

    width = products.shape[1]
    stat_ref[0] += jnp.sum(loss.reshape(-1, 8, width), axis=0)
    stat_ref[1] += jnp.sum((coeff * products).reshape(-1, 8, width), axis=0)
    stat_ref[2] += jnp.sum(coeff.reshape(-1, 8, width), axis=0)

    @pl.when(step == pl.num_programs(0) - 1)
    def _():
        gt_ref[...] = lax.dot_general(
            coef_ref[...], image_ref[...], (((0,), (0,)), ((), ())), preferred_element_type=jnp.float32
        )


def pair_terms(scalars, bases, ids, other, own, text, row_chunk=256):
    count, width = own.shape
    texts = text.shape[0]
    half = count // row_chunk
    return pl.pallas_call(
        lambda *refs: fused_kernel(row_chunk, *refs),
        grid=(2 * half,),
        in_specs=[
            pl.BlockSpec(memory_space=pltpu.SMEM),
            pl.BlockSpec(memory_space=pltpu.SMEM),
            pl.BlockSpec((1, texts), lambda i: (0, 0)),
            pl.BlockSpec((row_chunk, width), lambda i: (jnp.minimum(i, half - 1), 0)),
            pl.BlockSpec((row_chunk, width), lambda i: (jnp.maximum(i - half, 0), 0)),
            pl.BlockSpec((texts, width), lambda i: (0, 0)),
        ],
        out_specs=[
            pl.BlockSpec((row_chunk, width), lambda i: (i, 0)),
            pl.BlockSpec((texts, width), lambda i: (0, 0)),
            pl.BlockSpec((3, 8, texts), lambda i: (0, 0, 0)),
        ],
        out_shape=[
            jax.ShapeDtypeStruct((2 * count, width), jnp.float32),
            jax.ShapeDtypeStruct((texts, width), jnp.float32),
            jax.ShapeDtypeStruct((3, 8, texts), jnp.float32),
        ],
        scratch_shapes=[
            pltpu.VMEM((2 * count, texts), jnp.bfloat16),
            pltpu.VMEM((2 * count, width), jnp.bfloat16),
        ],
        compiler_params=pltpu.CompilerParams(vmem_limit_bytes=48 * 1024 * 1024),
        cost_estimate=pl.CostEstimate(
            flops=12 * count * texts * width, bytes_accessed=24 * count * width, transcendentals=6 * count * texts
        ),
    )(scalars, bases, ids, other, own, text)


def per_device(picture_embeddings, caption_embeddings, exponent_of_sharpness, offset_shift):
    count, width = picture_embeddings.shape
    group, blk = lax.axis_index("group"), lax.axis_index("blk")
    z, y, x, core = (group // 4) * 4 + (blk // 2) % 4, group % 4, blk // 8, blk % 2

    unit_text, inv_text = normalize_rows(caption_embeddings)
    text_rows = unit_text.astype(jnp.bfloat16)
    unit_image, inv_image = normalize_rows(picture_embeddings)
    image_rows = unit_image.astype(jnp.bfloat16)
    other_rows = move(image_rows, swap=1)

    n = caption_embeddings.shape[0]
    q = n // 4
    low, high = text_rows[: 2 * q], text_rows[2 * q :]
    low_x = [low, move(low, dx=1), move(low, dx=-1), move(low, dx=2)]
    high_z = [
        high,
        move(high, dz=1),
        move(high, dz=-1),
        move(high[:q], dz=2),
        move(high[q:], dz=-2),
    ]
    low_a = jnp.concatenate([v[:q] for v in low_x])
    low_b = jnp.concatenate([v[q:] for v in low_x])
    low_all = jnp.concatenate([low_a, low_b])
    low_z = [low_all, move(low_all, dz=1), move(low_all, dz=-1), move(low_a, dz=2), move(low_b, dz=-2)]
    high_all = jnp.concatenate(high_z)
    high_x = [high_all, move(high_all, dx=1), move(high_all, dx=-1), move(high_all, dx=2)]

    pieces, ids = [], []
    steps = jnp.arange(n, dtype=jnp.int32)
    for k, dx in enumerate(NEAR):
        at = (x + dx) % 4
        for j, dz in enumerate((0, -1, 1, -2, 2)):
            start = device_index((z + dz) % 8, y, at, core) * n
            own = start + steps
            a_low, b_low = slice(k * q, (k + 1) * q), slice(4 * q + k * q, 4 * q + (k + 1) * q)
            if j < 3:
                pieces += [low_z[j][a_low], low_z[j][b_low], high_x[k][2 * q * j : 2 * q * (j + 1)]]
                ids += [own]
            elif j == 3:
                pieces += [low_z[3][a_low], high_x[k][6 * q : 7 * q]]
                ids += [own[:q], own[2 * q : 3 * q]]
            else:
                pieces += [low_z[4][a_low], high_x[k][7 * q : 8 * q]]
                ids += [own[q : 2 * q], own[3 * q :]]
    texts = jnp.concatenate(pieces)
    text_ids = jnp.concatenate(ids)[None]

    temperature = jnp.exp(exponent_of_sharpness[0])
    scalars = jnp.stack([temperature, offset_shift[0]])
    bases = jnp.stack([(blk ^ 1) * count, blk * count]).astype(jnp.int32)
    image_terms, text_terms, sums = pair_terms(scalars, bases, text_ids, other_rows, image_rows, texts)

    quarter = count // 4
    received = move(image_terms[:count].astype(SEND), swap=1)
    chip_sum = (image_terms[count:] + received.astype(jnp.float32)).astype(SEND)
    part = lambda dy: lax.dynamic_slice_in_dim(chip_sum, ((y + dy) % 4) * quarter, quarter)
    y_sum = part(0).astype(jnp.float32)
    for dy in (1, -1, 2):
        y_sum += move(part(dy), dy=dy).astype(jnp.float32)
    y_sum = y_sum.astype(SEND)
    image_grad = y_sum.astype(jnp.float32) + move(y_sum, dz=4).astype(jnp.float32)
    unit_part = lax.dynamic_slice_in_dim(unit_image, y * quarter, quarter)
    tangent = (image_grad - unit_part * jnp.sum(unit_part * image_grad, axis=1, keepdims=True)).astype(SEND)
    slope = jnp.zeros((count, width), SEND)
    for dy in (0, 1, -1, 2):
        got = tangent if dy == 0 else move(tangent, dy=dy)
        slope = lax.dynamic_update_slice_in_dim(slope, got, ((y - dy) % 4) * quarter, 0)
    picture_embedding_slope = slope.astype(jnp.float32) * (temperature * inv_image)

    blocks = text_terms.reshape(4, 4 * n, width)
    x_sum = blocks[0]
    for k, dx in ((1, -1), (2, 1), (3, 2)):
        x_sum += move(blocks[k].astype(SEND), dx=dx).astype(jnp.float32)
    text_sum = x_sum[:n]
    z_send = x_sum[n:].astype(SEND)
    text_sum += move(z_send[:n], dz=-1).astype(jnp.float32)
    text_sum += move(z_send[n : 2 * n], dz=1).astype(jnp.float32)
    from_a = move(z_send[2 * n : 2 * n + 2 * q], dz=-2).astype(jnp.float32)
    from_b = move(z_send[2 * n + 2 * q :], dz=2).astype(jnp.float32)
    text_sum += jnp.concatenate([from_a[:q], from_b[:q], from_a[q:], from_b[q:]])
    text_grad = (
        (text_sum - unit_text * jnp.sum(unit_text * text_sum, axis=1, keepdims=True)) * (temperature * inv_text)
    )

    total = jnp.sum(sums.reshape(3, -1, 128), axis=1)
    total = jnp.concatenate([total, jnp.zeros((5, 128), jnp.float32)])
    for bit in range(8):
        pairs = [(i, i ^ (1 << bit)) for i in range(256)]
        total += lax.ppermute(total, AXES, pairs)
    total = jnp.sum(total, axis=1)
    rows_overall = count * lax.axis_size("blk")
    statistics = jnp.stack([total[0], temperature * total[1], total[2]]) / rows_overall
    return (picture_embedding_slope, text_grad, statistics)


def solution(mesh):
    placed = (P("blk", None), P(("group", "blk"), None), P(), P())
    return jax.shard_map(
        per_device,
        mesh=mesh,
        in_specs=placed,
        out_specs=(P("blk", None), P(("group", "blk"), None), P()),
        check_vma=False,
    )
```

time: 411 us -> 215 us (0.52)
  the two profiles are of different devices: /device:TPU:24 before, /device:TPU:6 now
where the time goes in v1:
time: 215 us; the launch traced here: 212 us
  waiting for transfers between devices  81.6 us (38%)
  starting transfers between devices  53.7 us (25%)
  local copies, waits for them, and re-layouts  29 us (13%)
  other arithmetic  27.9 us (13%)
  Pallas kernels  16.6 us (8%)
  between operations  3 us (1%)
    ppermute x30, waiting for transfers between devices, move(): return lax.ppermute(value, AXES, shifted(**shift))  61.2 us
    ppermute x30, starting transfers between devices, move(): return lax.ppermute(value, AXES, shifted(**shift))  42.7 us
    ppermute x8, waiting for transfers between devices, per_device(): total += lax.ppermute(total, AXES, pairs)  20.4 us
    pallas_call x1, Pallas kernels, pair_terms(): pl.pallas_call(lambda *refs: fused_kernel(row_chunk, *refs), grid=(2 * ha...  16.6 us
    unnamed x82, local copies, waits for them, and re-layouts  16 us
    ppermute x8, starting transfers between devices, per_device(): total += lax.ppermute(total, AXES, pairs)  11 us
    add x14, other arithmetic, per_device(): own = start + steps  7.89 us
    another operation x3, other arithmetic  4.81 us
  transfers between devices with their start and end apart: 38, of which 22 were waited for; matrix products, arithmetic and copies ran while one was open for 22% of the time, Pallas kernels for 0%

profile of v1, /device:TPU:6, one launch (start us, length us, event | category | flops | bytes accessed | tf_op | source)
XLA Modules:
  0.0 211.9 jit_solution(15390682732392569294)
XLA Ops:
  4.2 2.2 %collective-permute-start.1 = (bf16[32,1152]{1,0:T(8,128)(2,1)}, bf16[32,1152]{1,0:T(8,128)(2,1)}, u32[]{:S(2)}, u32[]{:S(2)}) collective-permute-start(bf16[32,1152]{1,0:T(8,128)(2,1)} %get-tuple-element.33), channel_id=1, source_target_pairs={{0,8},{1,9},{8,16},{9,17},{16,24},{17,25},{24,0},{25,1},{32,40},{3... | collective-permute-start | bytes 221192 | tf_op jit(solution)/shard_map/ppermute | solution.py:29
  6.4 1.5 collective-permute-start.3
  7.9 1.7 collective-permute-start.5
  9.6 3.9 %collective-permute-start.7 = (bf16[32,1152]{1,0:T(8,128)(2,1)}, bf16[32,1152]{1,0:T(8,128)(2,1)}, u32[]{:S(2)}, u32[]{:S(2)}) collective-permute-start(bf16[32,1152]{1,0:T(8,128)(2,1)} %get-tuple-element.32), channel_id=1, source_target_pairs={{0,134},{1,135},{8,142},{9,143},{16,150},{17,151},{24,158},{25,159... | collective-permute-start | bytes 221192 | tf_op jit(solution)/shard_map/ppermute | solution.py:29
  18.7 2.0 multiply_reduce_fusion
  21.1 1.7 fusion.3
  30.6 1.4 fusion.10
  32.0 4.1 %collective-permute-start.11 = (bf16[16,1152]{1,0:T(8,128)(2,1)}, bf16[16,1152]{1,0:T(8,128)(2,1)S(1)}, u32[]{:S(2)}, u32[]{:S(2)}) collective-permute-start(bf16[16,1152]{1,0:T(8,128)(2,1)} %get-tuple-element.34), channel_id=1, source_target_pairs={{0,132},{1,133},{8,140},{9,141},{16,148},{17,149},{24,156},{25,157... | collective-permute-start | bytes 110600 | tf_op jit(solution)/shard_map/ppermute | solution.py:29
  46.0 6.9 %collective-permute-done.4 = bf16[128,1152]{1,0:T(8,128)(2,1)S(1)} collective-permute-done((bf16[128,1152]{1,0:T(8,128)(2,1)}, bf16[128,1152]{1,0:T(8,128)(2,1)S(1)}, u32[]{:S(2)}, u32[]{:S(2)}) %collective-permute-start.4) | collective-permute-done | bytes 294944 | tf_op jit(solution)/shard_map/ppermute | solution.py:29
  53.1 1.5 constant_dynamic-update-slice_fusion.11
  54.6 5.3 %collective-permute-done.6 = bf16[128,1152]{1,0:T(8,128)(2,1)S(1)} collective-permute-done((bf16[128,1152]{1,0:T(8,128)(2,1)}, bf16[128,1152]{1,0:T(8,128)(2,1)S(1)}, u32[]{:S(2)}, u32[]{:S(2)}) %collective-permute-start.6) | collective-permute-done | bytes 294944 | tf_op jit(solution)/shard_map/ppermute | solution.py:29
  59.9 4.2 %collective-permute-start.10 = (bf16[64,1152]{1,0:T(8,128)(2,1)S(1)}, bf16[64,1152]{1,0:T(8,128)(2,1)S(1)}, u32[]{:S(2)}, u32[]{:S(2)}) collective-permute-start(bf16[64,1152]{1,0:T(8,128)(2,1)S(1)} %pad_maximum_fusion.1), channel_id=1, source_target_pairs={{0,132},{1,133},{8,140},{9,141},{16,148},{17,149},{24,156},{25,157... | collective-permute-start | bytes 442376 | tf_op jit(solution)/shard_map/ppermute | solution.py:29
  64.1 1.5 constant_dynamic-update-slice_fusion.10
  65.6 2.6 %collective-permute-done.8 = bf16[64,1152]{1,0:T(8,128)(2,1)S(1)} collective-permute-done((bf16[64,1152]{1,0:T(8,128)(2,1)S(1)}, bf16[64,1152]{1,0:T(8,128)(2,1)S(1)}, u32[]{:S(2)}, u32[]{:S(2)}) %collective-permute-start.8) | collective-permute-done | bytes 147488 | tf_op jit(solution)/shard_map/ppermute | solution.py:29
  68.9 1.6 collective-permute-done.10
  71.1 2.1 collective-permute-start.12
  73.3 2.0 collective-permute-start.14
  76.2 1.8 collective-permute-done.12
  79.1 5.5 %collective-permute-done.13 = bf16[128,1152]{1,0:T(8,128)(2,1)S(1)} collective-permute-done((bf16[128,1152]{1,0:T(8,128)(2,1)}, bf16[128,1152]{1,0:T(8,128)(2,1)S(1)}, u32[]{:S(2)}, u32[]{:S(2)}) %collective-permute-start.13) | collective-permute-done | bytes 294944 | tf_op jit(solution)/shard_map/ppermute | solution.py:29
  87.2 1.7 copy-done.1
  88.9 16.6 %shard_map.67 = (f32[1024,1152]{1,0:T(8,128)}, f32[1024,1152]{1,0:T(8,128)}, f32[3,8,1024]{2,1,0:T(8,128)S(1)}) custom-call(f32[2]{0:T(128)S(1)} %pad_maximum_fusion.2.refs_0_, s32[2]{0:T(128)S(1)} %pad_add_fusion.1.refs_1_, s32[1,1024]{1,0:T(1,128)S(1)} %bitcast.6, bf16[512,1152]{1,0:T(8,128)(2,1)S(1)} %collective-permute-done.refs_3_, ...), custom_call_target="tpu_custom_call" | custom-call | flops 7247757312 | bytes 14155776 | tf_op jit(solution)/shard_map/pallas_call | solution.py:90
  106.8 3.6 %collective-permute-done.31 = f32[8,128]{1,0:T(8,128)S(1)} collective-permute-done((f32[8,128]{1,0:T(8,128)S(1)}, f32[8,128]{1,0:T(8,128)S(1)}, u32[]{:S(2)}, u32[]{:S(2)}) %collective-permute-start.31) | collective-permute-done | bytes 4128 | tf_op jit(solution)/shard_map/ppermute | solution.py:212
  110.4 4.1 %collective-permute-start.32 = (f32[8,128]{1,0:T(8,128)S(1)}, f32[8,128]{1,0:T(8,128)S(1)}, u32[]{:S(2)}, u32[]{:S(2)}) collective-permute-start(f32[8,128]{1,0:T(8,128)S(1)} %add.754), channel_id=1, source_target_pairs={{0,4},{1,5},{2,6},{3,7},{4,0},{5,1},{6,2},{7,3},{8,12},{9,13},{10,... | collective-permute-start | bytes 12296 | tf_op jit(solution)/shard_map/ppermute | solution.py:212
  114.5 1.6 collective-permute-done.32
  116.1 3.6 %collective-permute-done.33 = f32[8,128]{1,0:T(8,128)S(1)} collective-permute-done((f32[8,128]{1,0:T(8,128)S(1)}, f32[8,128]{1,0:T(8,128)S(1)}, u32[]{:S(2)}, u32[]{:S(2)}) %collective-permute-start.33) | collective-permute-done | bytes 4128 | tf_op jit(solution)/shard_map/ppermute | solution.py:212
  119.7 5.1 %collective-permute-done.34 = f32[8,128]{1,0:T(8,128)S(1)} collective-permute-done((f32[8,128]{1,0:T(8,128)S(1)}, f32[8,128]{1,0:T(8,128)S(1)}, u32[]{:S(2)}, u32[]{:S(2)}) %collective-permute-start.34) | collective-permute-done | bytes 4128 | tf_op jit(solution)/shard_map/ppermute | solution.py:212
  124.8 1.6 collective-permute-start.35
  126.4 2.8 %convert.12 = f16[1024,1152]{1,0:T(8,128)(2,1)S(1)} convert(f32[1024,1152]{1,0:T(8,128)} %get-tuple-element.7) | non-fusion elementwise | flops 1179648 | bytes 7077888 | tf_op jit(solution)/shard_map/convert.3
  129.2 3.0 %collective-permute-start.36 = (f32[8,128]{1,0:T(8,128)S(1)}, f32[8,128]{1,0:T(8,128)S(1)}, u32[]{:S(2)}, u32[]{:S(2)}) collective-permute-start(f32[8,128]{1,0:T(8,128)S(1)} %add.758), channel_id=1, source_target_pairs={{0,64},{1,65},{2,66},{3,67},{4,68},{5,69},{6,70},{7,71},{8,72},{9,... | collective-permute-start | bytes 12296 | tf_op jit(solution)/shard_map/ppermute | solution.py:212
  133.5 3.2 %collective-permute-start.24 = (f16[256,1152]{1,0:T(8,128)(2,1)}, f16[256,1152]{1,0:T(8,128)(2,1)S(1)}, u32[]{:S(2)}, u32[]{:S(2)}) collective-permute-start(f16[256,1152]{1,0:T(8,128)(2,1)} %get-tuple-element.19), channel_id=1, source_target_pairs={{0,8},{1,9},{8,16},{9,17},{16,24},{17,25},{24,0},{25,1},{32,40},{3... | collective-permute-start | bytes 1769480 | tf_op jit(solution)/shard_map/ppermute | solution.py:29
  136.8 2.2 %collective-permute-start.37 = (f32[8,128]{1,0:T(8,128)S(1)}, f32[8,128]{1,0:T(8,128)S(1)}, u32[]{:S(2)}, u32[]{:S(2)}) collective-permute-start(f32[8,128]{1,0:T(8,128)S(1)} %add.759), channel_id=1, source_target_pairs={{0,128},{1,129},{2,130},{3,131},{4,132},{5,133},{6,134},{7,135},{8... | collective-permute-start | bytes 12296 | tf_op jit(solution)/shard_map/ppermute | solution.py:212
  139.3 5.3 %collective-permute-done.37 = f32[8,128]{1,0:T(8,128)S(1)} collective-permute-done((f32[8,128]{1,0:T(8,128)S(1)}, f32[8,128]{1,0:T(8,128)S(1)}, u32[]{:S(2)}, u32[]{:S(2)}) %collective-permute-start.37) | collective-permute-done | bytes 4128 | tf_op jit(solution)/shard_map/ppermute | solution.py:212
  145.9 1.9 maximum_multiply_fusion
  147.8 10.3 %collective-permute-done.23 = f16[256,1152]{1,0:T(8,128)(2,1)S(1)} collective-permute-done((f16[256,1152]{1,0:T(8,128)(2,1)}, f16[256,1152]{1,0:T(8,128)(2,1)S(1)}, u32[]{:S(2)}, u32[]{:S(2)}) %collective-permute-start.23) | collective-permute-done | bytes 589856 | tf_op jit(solution)/shard_map/ppermute | solution.py:29
  159.0 1.9 fusion.2
  161.9 2.1 collective-permute-start.29
  166.8 2.3 %collective-permute-done.29 = f16[32,1152]{1,0:T(8,128)(2,1)S(1)} collective-permute-done((f16[32,1152]{1,0:T(8,128)(2,1)S(1)}, f16[32,1152]{1,0:T(8,128)(2,1)S(1)}, u32[]{:S(2)}, u32[]{:S(2)}) %collective-permute-start.29) | collective-permute-done | bytes 73760 | tf_op jit(solution)/shard_map/ppermute | solution.py:29
  169.2 2.3 %add_convert_fusion = f16[512,1152]{1,0:T(8,128)(2,1)S(1)} fusion(f16[512,1152]{1,0:T(8,128)(2,1)} %collective-permute-done.15, f32[1024,1152]{1,0:T(8,128)} %get-tuple-element.6), kind=kLoop, calls=%fused_computation.2 | loop fusion | flops 1769472 | bytes 4718592 | tf_op jit(solution)/shard_map/convert_element_type | solution.py:178
  171.9 3.1 %collective-permute-start.17 = (f16[128,1152]{1,0:T(8,128)(2,1)S(1)}, f16[128,1152]{1,0:T(8,128)(2,1)S(1)}, u32[]{:S(2)}, u32[]{:S(2)}) collective-permute-start(f16[128,1152]{1,0:T(8,128)(2,1)S(1)} %get-tuple-element.22), channel_id=1, source_target_pairs={{0,96},{1,97},{8,104},{9,105},{16,112},{17,113},{24,120},{25,121},... | collective-permute-start | bytes 884744 | tf_op jit(solution)/shard_map/ppermute | solution.py:29
  175.0 4.7 %collective-permute-done.16 = f16[128,1152]{1,0:T(8,128)(2,1)S(1)} collective-permute-done((f16[128,1152]{1,0:T(8,128)(2,1)S(1)}, f16[128,1152]{1,0:T(8,128)(2,1)S(1)}, u32[]{:S(2)}, u32[]{:S(2)}) %collective-permute-start.16) | collective-permute-done | bytes 294944 | tf_op jit(solution)/shard_map/ppermute | solution.py:29
  179.7 2.7 %collective-permute-done.17 = f16[128,1152]{1,0:T(8,128)(2,1)S(1)} collective-permute-done((f16[128,1152]{1,0:T(8,128)(2,1)S(1)}, f16[128,1152]{1,0:T(8,128)(2,1)S(1)}, u32[]{:S(2)}, u32[]{:S(2)}) %collective-permute-start.17) | collective-permute-done | bytes 294944 | tf_op jit(solution)/shard_map/ppermute | solution.py:29
  183.4 4.6 %collective-permute-start.19 = (f16[128,1152]{1,0:T(8,128)(2,1)S(1)}, f16[128,1152]{1,0:T(8,128)(2,1)S(1)}, u32[]{:S(2)}, u32[]{:S(2)}) collective-permute-start(f16[128,1152]{1,0:T(8,128)(2,1)S(1)} %add_convert_fusion.1), channel_id=1, source_target_pairs={{0,128},{1,129},{8,136},{9,137},{16,144},{17,145},{24,152},{25,153... | collective-permute-start | bytes 884744 | tf_op jit(solution)/shard_map/ppermute | solution.py:29
  188.3 9.0 %collective-permute-done.19 = f16[128,1152]{1,0:T(8,128)(2,1)S(1)} collective-permute-done((f16[128,1152]{1,0:T(8,128)(2,1)S(1)}, f16[128,1152]{1,0:T(8,128)(2,1)S(1)}, u32[]{:S(2)}, u32[]{:S(2)}) %collective-permute-start.19) | collective-permute-done | bytes 294944 | tf_op jit(solution)/shard_map/ppermute | solution.py:29
  198.3 2.7 %collective-permute-start.21 = (f16[128,1152]{1,0:T(8,128)(2,1)S(1)}, f16[128,1152]{1,0:T(8,128)(2,1)S(1)}, u32[]{:S(2)}, u32[]{:S(2)}) collective-permute-start(f16[128,1152]{1,0:T(8,128)(2,1)S(1)} %get-tuple-element.12), channel_id=1, source_target_pairs={{0,96},{1,97},{8,104},{9,105},{16,112},{17,113},{24,120},{25,121},... | collective-permute-start | bytes 884744 | tf_op jit(solution)/shard_map/ppermute | solution.py:29
  203.0 2.7 %collective-permute-done.20 = f16[128,1152]{1,0:T(8,128)(2,1)S(1)} collective-permute-done((f16[128,1152]{1,0:T(8,128)(2,1)S(1)}, f16[128,1152]{1,0:T(8,128)(2,1)S(1)}, u32[]{:S(2)}, u32[]{:S(2)}) %collective-permute-start.20) | collective-permute-done | bytes 294944 | tf_op jit(solution)/shard_map/ppermute | solution.py:29
  205.8 2.7 %collective-permute-done.21 = f16[128,1152]{1,0:T(8,128)(2,1)S(1)} collective-permute-done((f16[128,1152]{1,0:T(8,128)(2,1)S(1)}, f16[128,1152]{1,0:T(8,128)(2,1)S(1)}, u32[]{:S(2)}, u32[]{:S(2)}) %collective-permute-start.21) | collective-permute-done | bytes 294944 | tf_op jit(solution)/shard_map/ppermute | solution.py:29
  208.6 1.6 collective-permute-done.22
  210.2 1.7 convert_multiply_fusion
  (183 shorter events, 44.6 us)
Async XLA Ops:
  3.5 10.0 %copy-start.5 = (bf16[64,1152]{1,0:T(8,128)(2,1)}, bf16[64,1152]{1,0:T(8,128)(2,1)S(1)}, u32[]{:S(2)}) copy-start(bf16[64,1152]{1,0:T(8,128)(2,1)S(1)} %get-tuple-element.14) | copy-start | bytes 442372
  4.2 26.3 %collective-permute-start.1 = (bf16[32,1152]{1,0:T(8,128)(2,1)}, bf16[32,1152]{1,0:T(8,128)(2,1)}, u32[]{:S(2)}, u32[]{:S(2)}) collective-permute-start(bf16[32,1152]{1,0:T(8,128)(2,1)} %get-tuple-element.33), channel_id=1, source_target_pairs={{0,8},{1,9},{8,16},{9,17},{16,24},{17,25},{24,0},{25,1},{32,40},{3... | collective-permute-start | bytes 221192 | tf_op jit(solution)/shard_map/ppermute | solution.py:29
  6.4 25.6 %collective-permute-start.2 = (bf16[32,1152]{1,0:T(8,128)(2,1)}, bf16[32,1152]{1,0:T(8,128)(2,1)}, u32[]{:S(2)}, u32[]{:S(2)}) collective-permute-start(bf16[32,1152]{1,0:T(8,128)(2,1)} %get-tuple-element.33), channel_id=1, source_target_pairs={{0,24},{1,25},{8,0},{9,1},{16,8},{17,9},{24,16},{25,17},{32,56},{3... | collective-permute-start | bytes 221192 | tf_op jit(solution)/shard_map/ppermute | solution.py:29
  6.4 31.1 %collective-permute-start.3 = (bf16[32,1152]{1,0:T(8,128)(2,1)}, bf16[32,1152]{1,0:T(8,128)(2,1)}, u32[]{:S(2)}, u32[]{:S(2)}) collective-permute-start(bf16[32,1152]{1,0:T(8,128)(2,1)} %get-tuple-element.33), channel_id=1, source_target_pairs={{0,16},{1,17},{8,24},{9,25},{16,0},{17,1},{24,8},{25,9},{32,48},{3... | collective-permute-start | bytes 221192 | tf_op jit(solution)/shard_map/ppermute | solution.py:29
  7.9 45.1 %collective-permute-start.5 = (bf16[32,1152]{1,0:T(8,128)(2,1)}, bf16[32,1152]{1,0:T(8,128)(2,1)}, u32[]{:S(2)}, u32[]{:S(2)}) collective-permute-start(bf16[32,1152]{1,0:T(8,128)(2,1)} %get-tuple-element.32), channel_id=1, source_target_pairs={{0,2},{1,3},{8,10},{9,11},{16,18},{17,19},{24,26},{25,27},{32,34},... | collective-permute-start | bytes 221192 | tf_op jit(solution)/shard_map/ppermute | solution.py:29
  9.6 50.3 %collective-permute-start.7 = (bf16[32,1152]{1,0:T(8,128)(2,1)}, bf16[32,1152]{1,0:T(8,128)(2,1)}, u32[]{:S(2)}, u32[]{:S(2)}) collective-permute-start(bf16[32,1152]{1,0:T(8,128)(2,1)} %get-tuple-element.32), channel_id=1, source_target_pairs={{0,134},{1,135},{8,142},{9,143},{16,150},{17,151},{24,158},{25,159... | collective-permute-start | bytes 221192 | tf_op jit(solution)/shard_map/ppermute | solution.py:29
  21.1 3.7 %copy-start.10 = (s32[64]{0:T(128)S(1)}, s32[64]{0:T(128)}, u32[]{:S(2)}) copy-start(s32[64]{0:T(128)} %iota_add_fusion.5) | copy-start | bytes 772
  21.1 5.4 %copy-start.11 = (s32[64]{0:T(128)S(1)}, s32[64]{0:T(128)}, u32[]{:S(2)}) copy-start(s32[64]{0:T(128)} %iota_add_fusion.11) | copy-start | bytes 772
  21.1 5.4 %copy-start.12 = (s32[64]{0:T(128)S(1)}, s32[64]{0:T(128)}, u32[]{:S(2)}) copy-start(s32[64]{0:T(128)} %iota_add_fusion.10) | copy-start | bytes 772
  21.1 6.7 %copy-start.13 = (s32[64]{0:T(128)S(1)}, s32[64]{0:T(128)}, u32[]{:S(2)}) copy-start(s32[64]{0:T(128)} %iota_add_fusion.16) | copy-start | bytes 772
  21.1 6.7 %copy-start.14 = (s32[64]{0:T(128)S(1)}, s32[64]{0:T(128)}, u32[]{:S(2)}) copy-start(s32[64]{0:T(128)} %iota_add_fusion.15) | copy-start | bytes 772
  30.5 37.7 %collective-permute-start.9 = (bf16[16,1152]{1,0:T(8,128)(2,1)}, bf16[16,1152]{1,0:T(8,128)(2,1)S(1)}, u32[]{:S(2)}, u32[]{:S(2)}) collective-permute-start(bf16[16,1152]{1,0:T(8,128)(2,1)} %get-tuple-element.36), channel_id=1, source_target_pairs={{0,4},{1,5},{8,12},{9,13},{16,20},{17,21},{24,28},{25,29},{32,36},... | collective-permute-start | bytes 110600 | tf_op jit(solution)/shard_map/ppermute | solution.py:29
  32.0 38.5 %collective-permute-start.11 = (bf16[16,1152]{1,0:T(8,128)(2,1)}, bf16[16,1152]{1,0:T(8,128)(2,1)S(1)}, u32[]{:S(2)}, u32[]{:S(2)}) collective-permute-start(bf16[16,1152]{1,0:T(8,128)(2,1)} %get-tuple-element.34), channel_id=1, source_target_pairs={{0,132},{1,133},{8,140},{9,141},{16,148},{17,149},{24,156},{25,157... | collective-permute-start | bytes 110600 | tf_op jit(solution)/shard_map/ppermute | solution.py:29
  44.4 8.5 %collective-permute-start.4 = (bf16[128,1152]{1,0:T(8,128)(2,1)}, bf16[128,1152]{1,0:T(8,128)(2,1)S(1)}, u32[]{:S(2)}, u32[]{:S(2)}) collective-permute-start(bf16[128,1152]{1,0:T(8,128)(2,1)} %constant_dynamic-update-slice_fusion), channel_id=1, source_target_pairs={{0,2},{1,3},{8,10},{9,11},{16,18},{17,19},{24,26},{25,27},{32,34},... | collective-permute-start | bytes 884744 | tf_op jit(solution)/shard_map/ppermute | solution.py:29
  52.9 6.9 %collective-permute-start.6 = (bf16[128,1152]{1,0:T(8,128)(2,1)}, bf16[128,1152]{1,0:T(8,128)(2,1)S(1)}, u32[]{:S(2)}, u32[]{:S(2)}) collective-permute-start(bf16[128,1152]{1,0:T(8,128)(2,1)} %constant_dynamic-update-slice_fusion), channel_id=1, source_target_pairs={{0,134},{1,135},{8,142},{9,143},{16,150},{17,151},{24,158},{25,159... | collective-permute-start | bytes 884744 | tf_op jit(solution)/shard_map/ppermute | solution.py:29
  53.0 34.3 %collective-permute-start = (bf16[512,1152]{1,0:T(8,128)(2,1)S(1)}, bf16[512,1152]{1,0:T(8,128)(2,1)S(1)}, u32[]{:S(2)}, u32[]{:S(2)}) collective-permute-start(bf16[512,1152]{1,0:T(8,128)(2,1)S(1)} %get-tuple-element.15.refs_4_), channel_id=1, source_target_pairs={{0,1},{1,0},{8,9},{9,8},{16,17},{17,16},{24,25},{25,24},{32,33},{3... | collective-permute-start | bytes 3538952 | tf_op jit(solution)/shard_map/ppermute | solution.py:29
  59.8 8.4 %collective-permute-start.8 = (bf16[64,1152]{1,0:T(8,128)(2,1)S(1)}, bf16[64,1152]{1,0:T(8,128)(2,1)S(1)}, u32[]{:S(2)}, u32[]{:S(2)}) collective-permute-start(bf16[64,1152]{1,0:T(8,128)(2,1)S(1)} %pad_maximum_fusion), channel_id=1, source_target_pairs={{0,4},{1,5},{8,12},{9,13},{16,20},{17,21},{24,28},{25,29},{32,36},... | collective-permute-start | bytes 442376 | tf_op jit(solution)/shard_map/ppermute | solution.py:29
  59.9 10.6 %collective-permute-start.10 = (bf16[64,1152]{1,0:T(8,128)(2,1)S(1)}, bf16[64,1152]{1,0:T(8,128)(2,1)S(1)}, u32[]{:S(2)}, u32[]{:S(2)}) collective-permute-start(bf16[64,1152]{1,0:T(8,128)(2,1)S(1)} %pad_maximum_fusion.1), channel_id=1, source_target_pairs={{0,132},{1,133},{8,140},{9,141},{16,148},{17,149},{24,156},{25,157... | collective-permute-start | bytes 442376 | tf_op jit(solution)/shard_map/ppermute | solution.py:29
  71.1 6.9 %collective-permute-start.12 = (bf16[128,1152]{1,0:T(8,128)(2,1)}, bf16[128,1152]{1,0:T(8,128)(2,1)S(1)}, u32[]{:S(2)}, u32[]{:S(2)}) collective-permute-start(bf16[128,1152]{1,0:T(8,128)(2,1)} %get-tuple-element.52), channel_id=1, source_target_pairs={{0,8},{1,9},{8,16},{9,17},{16,24},{17,25},{24,0},{25,1},{32,40},{3... | collective-permute-start | bytes 884744 | tf_op jit(solution)/shard_map/ppermute | solution.py:29
  73.3 11.3 %collective-permute-start.13 = (bf16[128,1152]{1,0:T(8,128)(2,1)}, bf16[128,1152]{1,0:T(8,128)(2,1)S(1)}, u32[]{:S(2)}, u32[]{:S(2)}) collective-permute-start(bf16[128,1152]{1,0:T(8,128)(2,1)} %get-tuple-element.52), channel_id=1, source_target_pairs={{0,24},{1,25},{8,0},{9,1},{16,8},{17,9},{24,16},{25,17},{32,56},{3... | collective-permute-start | bytes 884744 | tf_op jit(solution)/shard_map/ppermute | solution.py:29
  73.3 12.4 %collective-permute-start.14 = (bf16[128,1152]{1,0:T(8,128)(2,1)}, bf16[128,1152]{1,0:T(8,128)(2,1)S(1)}, u32[]{:S(2)}, u32[]{:S(2)}) collective-permute-start(bf16[128,1152]{1,0:T(8,128)(2,1)} %get-tuple-element.52), channel_id=1, source_target_pairs={{0,16},{1,17},{8,24},{9,25},{16,0},{17,1},{24,8},{25,9},{32,48},{3... | collective-permute-start | bytes 884744 | tf_op jit(solution)/shard_map/ppermute | solution.py:29
  105.5 1.3 collective-permute-start.30
  106.8 3.6 %collective-permute-start.31 = (f32[8,128]{1,0:T(8,128)S(1)}, f32[8,128]{1,0:T(8,128)S(1)}, u32[]{:S(2)}, u32[]{:S(2)}) collective-permute-start(f32[8,128]{1,0:T(8,128)S(1)} %pad_add_fusion), channel_id=1, source_target_pairs={{0,2},{1,3},{2,0},{3,1},{4,6},{5,7},{6,4},{7,5},{8,10},{9,11},{10,... | collective-permute-start | bytes 12296 | tf_op jit(solution)/shard_map/ppermute | solution.py:212
  110.4 5.7 %collective-permute-start.32 = (f32[8,128]{1,0:T(8,128)S(1)}, f32[8,128]{1,0:T(8,128)S(1)}, u32[]{:S(2)}, u32[]{:S(2)}) collective-permute-start(f32[8,128]{1,0:T(8,128)S(1)} %add.754), channel_id=1, source_target_pairs={{0,4},{1,5},{2,6},{3,7},{4,0},{5,1},{6,2},{7,3},{8,12},{9,13},{10,... | collective-permute-start | bytes 12296 | tf_op jit(solution)/shard_map/ppermute | solution.py:212
  116.1 3.6 %collective-permute-start.33 = (f32[8,128]{1,0:T(8,128)S(1)}, f32[8,128]{1,0:T(8,128)S(1)}, u32[]{:S(2)}, u32[]{:S(2)}) collective-permute-start(f32[8,128]{1,0:T(8,128)S(1)} %add.755), channel_id=1, source_target_pairs={{0,8},{1,9},{2,10},{3,11},{4,12},{5,13},{6,14},{7,15},{8,0},{9,1},... | collective-permute-start | bytes 12296 | tf_op jit(solution)/shard_map/ppermute | solution.py:212
  119.7 5.1 %collective-permute-start.34 = (f32[8,128]{1,0:T(8,128)S(1)}, f32[8,128]{1,0:T(8,128)S(1)}, u32[]{:S(2)}, u32[]{:S(2)}) collective-permute-start(f32[8,128]{1,0:T(8,128)S(1)} %add.756), channel_id=1, source_target_pairs={{0,16},{1,17},{2,18},{3,19},{4,20},{5,21},{6,22},{7,23},{8,24},{9,... | collective-permute-start | bytes 12296 | tf_op jit(solution)/shard_map/ppermute | solution.py:212
  124.8 4.3 %collective-permute-start.35 = (f32[8,128]{1,0:T(8,128)S(1)}, f32[8,128]{1,0:T(8,128)S(1)}, u32[]{:S(2)}, u32[]{:S(2)}) collective-permute-start(f32[8,128]{1,0:T(8,128)S(1)} %add.757), channel_id=1, source_target_pairs={{0,32},{1,33},{2,34},{3,35},{4,36},{5,37},{6,38},{7,39},{8,40},{9,... | collective-permute-start | bytes 12296 | tf_op jit(solution)/shard_map/ppermute | solution.py:212
  126.4 12.7 %slice-start = ((s8[4718592]{0:T(1024)(128)(4,1)}), s8[4194304]{0:T(1024)(128)(4,1)S(1)}, s32[]{:S(2)}) async-start(s8[4718592]{0:T(1024)(128)(4,1)} %bitcast.7), calls=%async_computation | async-start | bytes 8388608
  126.4 12.7 %slice-start.1 = ((s8[4718592]{0:T(1024)(128)(4,1)}), s8[524288]{0:T(1024)(128)(4,1)S(1)}, s32[]{:S(2)}) async-start(s8[4718592]{0:T(1024)(128)(4,1)} %bitcast.7), calls=%async_computation.1 | async-start | bytes 1048576
  129.2 7.6 %collective-permute-start.36 = (f32[8,128]{1,0:T(8,128)S(1)}, f32[8,128]{1,0:T(8,128)S(1)}, u32[]{:S(2)}, u32[]{:S(2)}) collective-permute-start(f32[8,128]{1,0:T(8,128)S(1)} %add.758), channel_id=1, source_target_pairs={{0,64},{1,65},{2,66},{3,67},{4,68},{5,69},{6,70},{7,71},{8,72},{9,... | collective-permute-start | bytes 12296 | tf_op jit(solution)/shard_map/ppermute | solution.py:212
  133.5 24.6 %collective-permute-start.23 = (f16[256,1152]{1,0:T(8,128)(2,1)}, f16[256,1152]{1,0:T(8,128)(2,1)S(1)}, u32[]{:S(2)}, u32[]{:S(2)}) collective-permute-start(f16[256,1152]{1,0:T(8,128)(2,1)} %get-tuple-element.17), channel_id=1, source_target_pairs={{0,24},{1,25},{8,0},{9,1},{16,8},{17,9},{24,16},{25,17},{32,56},{3... | collective-permute-start | bytes 1769480 | tf_op jit(solution)/shard_map/ppermute | solution.py:29
  133.5 24.6 %collective-permute-start.24 = (f16[256,1152]{1,0:T(8,128)(2,1)}, f16[256,1152]{1,0:T(8,128)(2,1)S(1)}, u32[]{:S(2)}, u32[]{:S(2)}) collective-permute-start(f16[256,1152]{1,0:T(8,128)(2,1)} %get-tuple-element.19), channel_id=1, source_target_pairs={{0,8},{1,9},{8,16},{9,17},{16,24},{17,25},{24,0},{25,1},{32,40},{3... | collective-permute-start | bytes 1769480 | tf_op jit(solution)/shard_map/ppermute | solution.py:29
  136.8 22.2 %collective-permute-start.25 = (f16[256,1152]{1,0:T(8,128)(2,1)}, f16[256,1152]{1,0:T(8,128)(2,1)}, u32[]{:S(2)}, u32[]{:S(2)}) collective-permute-start(f16[256,1152]{1,0:T(8,128)(2,1)} %get-tuple-element.18), channel_id=1, source_target_pairs={{0,16},{1,17},{8,24},{9,25},{16,0},{17,1},{24,8},{25,9},{32,48},{3... | collective-permute-start | bytes 1769480 | tf_op jit(solution)/shard_map/ppermute | solution.py:29
  136.8 7.8 %collective-permute-start.37 = (f32[8,128]{1,0:T(8,128)S(1)}, f32[8,128]{1,0:T(8,128)S(1)}, u32[]{:S(2)}, u32[]{:S(2)}) collective-permute-start(f32[8,128]{1,0:T(8,128)S(1)} %add.759), channel_id=1, source_target_pairs={{0,128},{1,129},{2,130},{3,131},{4,132},{5,133},{6,134},{7,135},{8... | collective-permute-start | bytes 12296 | tf_op jit(solution)/shard_map/ppermute | solution.py:212
  139.2 30.0 %collective-permute-start.15 = (f16[512,1152]{1,0:T(8,128)(2,1)S(1)}, f16[512,1152]{1,0:T(8,128)(2,1)}, u32[]{:S(2)}, u32[]{:S(2)}) collective-permute-start(f16[512,1152]{1,0:T(8,128)(2,1)S(1)} %slice_convert_fusion), channel_id=1, source_target_pairs={{0,1},{1,0},{8,9},{9,8},{16,17},{17,16},{24,25},{25,24},{32,33},{3... | collective-permute-start | bytes 3538952 | tf_op jit(solution)/shard_map/ppermute | solution.py:29
  161.0 5.8 %collective-permute-start.28 = (f16[32,1152]{1,0:T(8,128)(2,1)S(1)}, f16[32,1152]{1,0:T(8,128)(2,1)S(1)}, u32[]{:S(2)}, u32[]{:S(2)}) collective-permute-start(f16[32,1152]{1,0:T(8,128)(2,1)S(1)} %get-tuple-element.25), channel_id=1, source_target_pairs={{0,132},{1,133},{8,140},{9,141},{16,148},{17,149},{24,156},{25,157... | collective-permute-start | bytes 221192 | tf_op jit(solution)/shard_map/ppermute | solution.py:29
  161.9 7.3 %collective-permute-start.29 = (f16[32,1152]{1,0:T(8,128)(2,1)S(1)}, f16[32,1152]{1,0:T(8,128)(2,1)S(1)}, u32[]{:S(2)}, u32[]{:S(2)}) collective-permute-start(f16[32,1152]{1,0:T(8,128)(2,1)S(1)} %get-tuple-element.26), channel_id=1, source_target_pairs={{0,4},{1,5},{8,12},{9,13},{16,20},{17,21},{24,28},{25,29},{32,36},... | collective-permute-start | bytes 221192 | tf_op jit(solution)/shard_map/ppermute | solution.py:29
  164.0 24.0 %collective-permute-start.26 = (f16[64,1152]{1,0:T(8,128)(2,1)S(1)}, f16[64,1152]{1,0:T(8,128)(2,1)S(1)}, u32[]{:S(2)}, u32[]{:S(2)}) collective-permute-start(f16[64,1152]{1,0:T(8,128)(2,1)S(1)} %get-tuple-element.23), channel_id=1, source_target_pairs={{0,134},{1,135},{8,142},{9,143},{16,150},{17,151},{24,158},{25,159... | collective-permute-start | bytes 442376 | tf_op jit(solution)/shard_map/ppermute | solution.py:29
  165.0 23.1 %collective-permute-start.27 = (f16[64,1152]{1,0:T(8,128)(2,1)S(1)}, f16[64,1152]{1,0:T(8,128)(2,1)S(1)}, u32[]{:S(2)}, u32[]{:S(2)}) collective-permute-start(f16[64,1152]{1,0:T(8,128)(2,1)S(1)} %get-tuple-element.24), channel_id=1, source_target_pairs={{0,2},{1,3},{8,10},{9,11},{16,18},{17,19},{24,26},{25,27},{32,34},... | collective-permute-start | bytes 442376 | tf_op jit(solution)/shard_map/ppermute | solution.py:29
  171.5 16.6 %copy-start.4 = (f32[64,1152]{1,0:T(8,128)S(1)}, f32[64,1152]{1,0:T(8,128)}, u32[]{:S(2)}) copy-start(f32[64,1152]{1,0:T(8,128)} %param.5) | copy-start | bytes 884740
  171.5 25.8 %copy-start.3 = (f32[512,1152]{1,0:T(8,128)S(1)}, f32[512,1152]{1,0:T(8,128)}, u32[]{:S(2)}) copy-start(f32[512,1152]{1,0:T(8,128)} %get-tuple-element.16) | copy-start | bytes 7077892
  171.7 8.0 %collective-permute-start.16 = (f16[128,1152]{1,0:T(8,128)(2,1)S(1)}, f16[128,1152]{1,0:T(8,128)(2,1)S(1)}, u32[]{:S(2)}, u32[]{:S(2)}) collective-permute-start(f16[128,1152]{1,0:T(8,128)(2,1)S(1)} %get-tuple-element.20), channel_id=1, source_target_pairs={{0,32},{1,33},{8,40},{9,41},{16,48},{17,49},{24,56},{25,57},{32,64... | collective-permute-start | bytes 884744 | tf_op jit(solution)/shard_map/ppermute | solution.py:29
  171.9 10.5 %collective-permute-start.17 = (f16[128,1152]{1,0:T(8,128)(2,1)S(1)}, f16[128,1152]{1,0:T(8,128)(2,1)S(1)}, u32[]{:S(2)}, u32[]{:S(2)}) collective-permute-start(f16[128,1152]{1,0:T(8,128)(2,1)S(1)} %get-tuple-element.22), channel_id=1, source_target_pairs={{0,96},{1,97},{8,104},{9,105},{16,112},{17,113},{24,120},{25,121},... | collective-permute-start | bytes 884744 | tf_op jit(solution)/shard_map/ppermute | solution.py:29
  175.0 8.2 %collective-permute-start.18 = (f16[128,1152]{1,0:T(8,128)(2,1)S(1)}, f16[128,1152]{1,0:T(8,128)(2,1)S(1)}, u32[]{:S(2)}, u32[]{:S(2)}) collective-permute-start(f16[128,1152]{1,0:T(8,128)(2,1)S(1)} %get-tuple-element.21), channel_id=1, source_target_pairs={{0,64},{1,65},{8,72},{9,73},{16,80},{17,81},{24,88},{25,89},{32,96... | collective-permute-start | bytes 884744 | tf_op jit(solution)/shard_map/ppermute | solution.py:29
  183.4 13.9 %collective-permute-start.19 = (f16[128,1152]{1,0:T(8,128)(2,1)S(1)}, f16[128,1152]{1,0:T(8,128)(2,1)S(1)}, u32[]{:S(2)}, u32[]{:S(2)}) collective-permute-start(f16[128,1152]{1,0:T(8,128)(2,1)S(1)} %add_convert_fusion.1), channel_id=1, source_target_pairs={{0,128},{1,129},{8,136},{9,137},{16,144},{17,145},{24,152},{25,153... | collective-permute-start | bytes 884744 | tf_op jit(solution)/shard_map/ppermute | solution.py:29
  197.8 8.0 %collective-permute-start.20 = (f16[128,1152]{1,0:T(8,128)(2,1)S(1)}, f16[128,1152]{1,0:T(8,128)(2,1)S(1)}, u32[]{:S(2)}, u32[]{:S(2)}) collective-permute-start(f16[128,1152]{1,0:T(8,128)(2,1)S(1)} %get-tuple-element.12), channel_id=1, source_target_pairs={{0,32},{1,33},{8,40},{9,41},{16,48},{17,49},{24,56},{25,57},{32,64... | collective-permute-start | bytes 884744 | tf_op jit(solution)/shard_map/ppermute | solution.py:29
  198.3 10.2 %collective-permute-start.21 = (f16[128,1152]{1,0:T(8,128)(2,1)S(1)}, f16[128,1152]{1,0:T(8,128)(2,1)S(1)}, u32[]{:S(2)}, u32[]{:S(2)}) collective-permute-start(f16[128,1152]{1,0:T(8,128)(2,1)S(1)} %get-tuple-element.12), channel_id=1, source_target_pairs={{0,96},{1,97},{8,104},{9,105},{16,112},{17,113},{24,120},{25,121},... | collective-permute-start | bytes 884744 | tf_op jit(solution)/shard_map/ppermute | solution.py:29
  201.9 8.2 %collective-permute-start.22 = (f16[128,1152]{1,0:T(8,128)(2,1)S(1)}, f16[128,1152]{1,0:T(8,128)(2,1)S(1)}, u32[]{:S(2)}, u32[]{:S(2)}) collective-permute-start(f16[128,1152]{1,0:T(8,128)(2,1)S(1)} %get-tuple-element.12), channel_id=1, source_target_pairs={{0,64},{1,65},{8,72},{9,73},{16,80},{17,81},{24,88},{25,89},{32,96... | collective-permute-start | bytes 884744 | tf_op jit(solution)/shard_map/ppermute | solution.py:29
  (7 other events, 14.8 us)

commit v2 on v0

v2 whole, which is shorter than its diff:
```python
import jax
import jax.numpy as jnp
from jax import lax
from jax.experimental import pallas as pl
from jax.experimental.pallas import tpu as pltpu
from jax.sharding import PartitionSpec as P

AXES = ("group", "blk")
SEND = jnp.float16
VMEM_BYTES = 58 * 1024 * 1024
PAIR_VMEM_BYTES = 44 * 1024 * 1024
SMEM = pl.BlockSpec(memory_space=pltpu.SMEM)
HBM = pl.BlockSpec(memory_space=pltpu.HBM)


def device_index(z, y, x, core):
    return (((z // 4) * 4 + y) * 4 + x) * 8 + (z % 4) * 2 + core


def shifted(dz=0, dy=0, dx=0, swap=0):
    pairs = []
    for z in range(8):
        for y in range(4):
            for x in range(4):
                for core in range(2):
                    there = device_index((z + dz) % 8, (y + dy) % 4, (x + dx) % 4, core ^ swap)
                    pairs.append((device_index(z, y, x, core), there))
    return pairs


def move(value, **shift):
    return lax.ppermute(value, AXES, shifted(**shift))


def normalize_rows(matrix):
    inverse_norm = lax.rsqrt(jnp.sum(matrix * matrix, axis=1, keepdims=True) + 1e-06)
    return (matrix * inverse_norm, inverse_norm)


def text_kernel(text_ref, rows_ref, a_ref, b_ref):
    text = text_ref[...]
    rows = (text * lax.rsqrt(jnp.sum(text * text, axis=1, keepdims=True) + 1e-06)).astype(jnp.bfloat16)
    half = a_ref.shape[0]
    rows_ref[...] = rows
    a_ref[...] = rows[:half]
    b_ref[...] = rows[half:]


def text_messages(texts):
    n, width = texts.shape
    shape = lambda rows: jax.ShapeDtypeStruct((rows, width), jnp.bfloat16)
    return pl.pallas_call(
        text_kernel,
        grid=(1,),
        in_specs=[pl.BlockSpec((n, width), lambda i: (0, 0))],
        out_specs=[pl.BlockSpec((rows, width), lambda i: (0, 0)) for rows in (n, n // 2, n // 2)],
        out_shape=[shape(n), shape(n // 2), shape(n // 2)],
        compiler_params=pltpu.CompilerParams(vmem_limit_bytes=VMEM_BYTES),
        name="text_rows",
    )(texts)


def run_copies(pairs, sems):
    copies = [pltpu.make_async_copy(source, target, sems.at[i]) for i, (source, target) in enumerate(pairs)]
    for copy in copies:
        copy.start()
    for copy in copies:
        copy.wait()


def join_kernel(*refs):
    parts, (column_ref, ends_ref, sems) = refs[:-3], refs[-3:]
    pairs = []
    for out_ref, sources in ((column_ref, parts[:4]), (ends_ref, parts[4:])):
        start = 0
        for ref in sources:
            pairs.append((ref, out_ref.at[start : start + ref.shape[0], :]))
            start += ref.shape[0]
    run_copies(pairs, sems)


def join(column, ends):
    width = column[0].shape[1]
    heights = [sum(part.shape[0] for part in parts) for parts in (column, ends)]
    return pl.pallas_call(
        join_kernel,
        grid=(1,),
        in_specs=[HBM] * 6,
        out_specs=[pl.BlockSpec((rows, width), lambda i: (0, 0)) for rows in heights],
        out_shape=[jax.ShapeDtypeStruct((rows, width), column[0].dtype) for rows in heights],
        scratch_shapes=[pltpu.SemaphoreType.DMA((6,))],
        compiler_params=pltpu.CompilerParams(vmem_limit_bytes=PAIR_VMEM_BYTES),
        name="join",
    )(*column, *ends)


def text_index(place_ref, texts):
    lane = lax.broadcasted_iota(jnp.int32, (1, texts), 1)
    column, part, row = lane >> 8, (lane >> 6) & 3, lane & 63
    dx = jnp.where(column == 1, -1, column - (column >> 1))
    far = jnp.where(row < 32, -2, 2)
    dz = jnp.where(part == 3, far, jnp.where(part == 2, 1, -part))
    z = (place_ref[0] + dz) & 7
    x = (place_ref[2] + dx) & 3
    device = (z >> 2) * 128 + place_ref[1] * 32 + x * 8 + (z & 3) * 2 + place_ref[3]
    return device * 64 + row


def pair_block(scal_ref, image, text, row_ids, text_ids, stat_ref):
    products = lax.dot_general(image, text, (((1,), (1,)), ((), ())), preferred_element_type=jnp.float32)
    logits = scal_ref[0] * products + scal_ref[1]
    paired = row_ids == text_ids
    grown = jnp.exp(logits)
    above = 1.0 + grown
    coeff = jnp.where(paired, -1.0, grown) * pl.reciprocal(above)
    loss = jnp.where(grown < 1e-3, grown * (1.0 - 0.5 * grown), jnp.log(above))
    loss = loss - jnp.where(paired, logits, 0.0)
    width = products.shape[1]
    stat_ref[0] += jnp.sum(loss.reshape(-1, 8, width), axis=0)
    stat_ref[1] += jnp.sum((coeff * products).reshape(-1, 8, width), axis=0)
    stat_ref[2] += jnp.sum(coeff.reshape(-1, 8, width), axis=0)
    return coeff.astype(jnp.bfloat16)


def pair_kernel(side, scal_ref, place_ref, image_ref, *rest):
    if side == 0:
        pieces, rest = rest[:7], rest[7:]
        grad_ref, coef_ref, copy_ref, text_ref, stat_ref, sems = rest
    else:
        text_ref, sums_ref, _, _, grad_ref, coef_ref, copy_ref, total_ref, stat_ref, sems = rest
    count = image_ref.shape[0]
    quarter = count // 4
    columns = coef_ref.shape[2]
    block = columns // 4
    starts = [pl.multiple_of(((place_ref[1] + dy) & 3) * quarter, quarter) for dy in (0, 1, 3, 2)]
    pairs = [
        (image_ref.at[pl.ds(start, quarter), :], copy_ref.at[i * quarter : (i + 1) * quarter, :])
        for i, start in enumerate(starts)
    ]
    if side == 0:
        for k in range(4):
            for j in range(4):
                piece = pieces[j].at[block * k : block * (k + 1), :] if j < 3 else pieces[3 + k]
                at = columns * k + block * j
                pairs.append((piece, text_ref.at[at : at + block, :]))
    run_copies(pairs, sems)
    stat_ref[...] = jnp.zeros_like(stat_ref) if side == 0 else sums_ref[...]
    text = text_ref[...]
    ids = text_index(place_ref, text.shape[0])
    row_iota = lax.broadcasted_iota(jnp.int32, (quarter, 1), 0) + place_ref[4 + side]
    for half in range(2):
        rows = slice(2 * half * quarter, 2 * (half + 1) * quarter)
        row_ids = jnp.concatenate([row_iota + start for start in starts[2 * half : 2 * half + 2]])
        coeff = pair_block(scal_ref, copy_ref[rows, :], text, row_ids, ids, stat_ref)
        grad_ref[rows, :] = jnp.dot(coeff, text, preferred_element_type=jnp.float32)
        for k in range(4):
            coef_ref[k, rows, :] = coeff[:, k * columns : (k + 1) * columns]
    if side == 1:
        total_ref[...] = jnp.zeros_like(total_ref)
        for k in range(3):
            stat = stat_ref[k]
            lanes = sum(stat[:, 128 * i : 128 * (i + 1)] for i in range(stat.shape[1] // 128))
            total_ref[k : k + 1, :] = jnp.sum(lanes, axis=0, keepdims=True)


def pair_terms(scalars, place, other, own, col, below, above, far):
    count, width = own.shape
    texts = 4 * col.shape[0]
    f32, bf16 = jnp.float32, jnp.bfloat16
    shape = jax.ShapeDtypeStruct
    cost = pl.CostEstimate(
        flops=4 * count * texts * width, bytes_accessed=12 * count * width, transcendentals=3 * count * texts
    )
    params = pltpu.CompilerParams(vmem_limit_bytes=PAIR_VMEM_BYTES)
    whole = lambda *dims: pl.BlockSpec(dims, lambda i: (0,) * len(dims))
    coef_shape, copy_shape = shape((4, 2 * count, texts // 4), bf16), shape((2 * count, width), bf16)
    stat = (3, 8, texts)
    grad_other, coef, copies, text, sums = pl.pallas_call(
        lambda *refs: pair_kernel(0, *refs),
        grid=(1,),
        in_specs=[SMEM, SMEM] + [HBM] * 8,
        out_specs=[
            whole(count, width),
            whole(4, count, texts // 4),
            whole(count, width),
            whole(texts, width),
            whole(*stat),
        ],
        out_shape=[shape((count, width), f32), coef_shape, copy_shape, shape((texts, width), bf16), shape(stat, f32)],
        scratch_shapes=[pltpu.SemaphoreType.DMA((20,))],
        compiler_params=params,
        cost_estimate=cost,
        name="other_rows",
    )(scalars, place, other, col, below, above, *far)
    grad_own, coef, copies, total = pl.pallas_call(
        lambda *refs: pair_kernel(1, *refs),
        grid=(1,),
        in_specs=[SMEM, SMEM, HBM, whole(texts, width), whole(*stat), HBM, HBM],
        out_specs=[
            whole(count, width),
            pl.BlockSpec((4, count, texts // 4), lambda i: (0, 1, 0)),
            pl.BlockSpec((count, width), lambda i: (1, 0)),
            whole(8, 128),
        ],
        out_shape=[shape((count, width), f32), coef_shape, copy_shape, shape((8, 128), f32)],
        scratch_shapes=[pltpu.VMEM(stat, f32), pltpu.SemaphoreType.DMA((4,))],
        input_output_aliases={5: 1, 6: 2},
        compiler_params=params,
        cost_estimate=cost,
        name="own_rows",
    )(scalars, place, own, text, sums, coef, copies)
    return grad_other, grad_own, coef, copies, total


def per_device(picture_embeddings, caption_embeddings, exponent_of_sharpness, offset_shift):
    count, width = picture_embeddings.shape
    group, blk = lax.axis_index("group"), lax.axis_index("blk")
    z, y, x, core = (group // 4) * 4 + (blk // 2) % 4, group % 4, blk // 8, blk % 2
    temperature = jnp.exp(exponent_of_sharpness[0])
    scalars = jnp.stack([temperature, offset_shift[0]])
    place = jnp.stack([z, y, x, core, (blk ^ 1) * count, blk * count]).astype(jnp.int32)

    text_rows, text_a, text_b = text_messages(caption_embeddings)
    pictures, text_rows = lax.optimization_barrier((picture_embeddings, text_rows))
    column, ends = join(
        (text_rows, move(text_rows, dx=1), move(text_rows, dx=-1), move(text_rows, dx=2)),
        (move(text_a, dz=2), move(text_b, dz=-2)),
    )
    unit_image, inv_image = normalize_rows(pictures)
    image_rows = unit_image.astype(jnp.bfloat16)
    other_rows = move(image_rows, swap=1)
    below, above = move(column, dz=1), move(column, dz=-1)
    far = [ends, move(ends, dx=1), move(ends, dx=-1), move(ends, dx=2)]

    grad_other, grad_own, coef, copies, total = pair_terms(
        scalars, place, other_rows, image_rows, column, below, above, far
    )

    quarter = count // 4
    received = move(grad_other, swap=1)
    parts = [
        (grad_own[k * quarter : (k + 1) * quarter] + received[k * quarter : (k + 1) * quarter]).astype(SEND)
        for k in range(4)
    ]
    arrived = [move(parts[1], dy=1), move(parts[2], dy=-1), move(parts[3], dy=2)]

    coef, copies, parts[0] = lax.optimization_barrier((coef, copies, parts[0]))
    blocks = [
        lax.dot_general(coef[k], copies, (((0,), (0,)), ((), ())), preferred_element_type=jnp.float32).astype(SEND)
        for k in range(4)
    ]
    x_terms = [blocks[0], move(blocks[1], dx=-1), move(blocks[2], dx=1), move(blocks[3], dx=2)]

    y_sum = sum(part.astype(jnp.float32) for part in [parts[0]] + arrived).astype(SEND)
    image_grad = y_sum.astype(jnp.float32) + move(y_sum, dz=4).astype(jnp.float32)
    unit_part = lax.dynamic_slice_in_dim(unit_image, y * quarter, quarter)
    tangent = (image_grad - unit_part * jnp.sum(unit_part * image_grad, axis=1, keepdims=True)).astype(SEND)
    tangents = [tangent] + [move(tangent, dy=dy) for dy in (1, -1, 2)]

    n = caption_embeddings.shape[0]
    h = n // 2
    *x_terms, tangent = lax.optimization_barrier((*x_terms, tangent))
    x_sum = sum(term.astype(jnp.float32) for term in x_terms).astype(SEND)
    near = [move(x_sum[n : 2 * n], dz=-1), move(x_sum[2 * n : 3 * n], dz=1)]
    ends_sum = [move(x_sum[3 * n : 3 * n + h], dz=-2), move(x_sum[3 * n + h :], dz=2)]
    *tangents, near[0], near[1], ends_sum[0], ends_sum[1] = lax.optimization_barrier((*tangents, *near, *ends_sum))

    slope = jnp.zeros((count, width), SEND)
    for dy, got in zip((0, 1, -1, 2), tangents):
        slope = lax.dynamic_update_slice_in_dim(slope, got, ((y - dy) % 4) * quarter, 0)
    picture_embedding_slope = slope.astype(jnp.float32) * (temperature * inv_image)

    text_sum = x_sum[:n].astype(jnp.float32) + jnp.concatenate(ends_sum).astype(jnp.float32)
    text_sum += near[0].astype(jnp.float32) + near[1].astype(jnp.float32)
    unit_text, inv_text = normalize_rows(caption_embeddings)
    text_grad = (text_sum - unit_text * jnp.sum(unit_text * text_sum, axis=1, keepdims=True)) * (
        temperature * inv_text
    )

    for done, bits in ((parts[0], (0, 3, 4)), (y_sum, (5, 6)), (tangent, (1, 2, 7))):
        total, _ = lax.optimization_barrier((total, done))
        for bit in bits:
            total += lax.ppermute(total, AXES, [(i, i ^ (1 << bit)) for i in range(256)])
    total = jnp.sum(total, axis=1)
    rows_overall = count * lax.axis_size("blk")
    statistics = jnp.stack([total[0], temperature * total[1], total[2]]) / rows_overall
    return (picture_embedding_slope, text_grad, statistics)


def solution(mesh):
    placed = (P("blk", None), P(("group", "blk"), None), P(), P())
    return jax.shard_map(
        per_device,
        mesh=mesh,
        in_specs=placed,
        out_specs=(P("blk", None), P(("group", "blk"), None), P()),
        check_vma=False,
    )
```

time: 411 us -> 147 us (0.36)
  the two profiles are of different devices: /device:TPU:24 before, /device:TPU:6 now
where the time goes in v2:
time: 147 us
  starting transfers between devices  54.3 us (37%)
  waiting for transfers between devices  50.8 us (35%)
  Pallas kernels  16.8 us (11%)
  other arithmetic  9.68 us (7%)
  matrix products  6.37 us (4%)
  local copies, waits for them, and re-layouts  6.18 us (4%)
  between operations  2.9 us (2%)
    ppermute x26, starting transfers between devices, move(): return lax.ppermute(value, AXES, shifted(**shift))  43.4 us
    ppermute x26, waiting for transfers between devices, move(): return lax.ppermute(value, AXES, shifted(**shift))  34.1 us
    ppermute x8, waiting for transfers between devices, per_device(): total += lax.ppermute(total, AXES, [(i, i ^ 1 << bit) for i in range(256)])  16.8 us
    ppermute x8, starting transfers between devices, per_device(): total += lax.ppermute(total, AXES, [(i, i ^ 1 << bit) for i in range(256)])  10.9 us
    pallas_call x1, Pallas kernels, pair_terms(): pl.pallas_call(lambda *refs: pair_kernel(0, *refs), grid=(1,), in_specs=[...  7.34 us
    dot_general x4, matrix products, per_device(): lax.dot_general(coef[k], copies, (((0,), (0,)), ((), ())), preferred_elem...  6.37 us
    pallas_call x1, Pallas kernels, pair_terms(): pl.pallas_call(lambda *refs: pair_kernel(1, *refs), grid=(1,), in_specs=[...  5.82 us
    unnamed x26, local copies, waits for them, and re-layouts  5.03 us
  transfers between devices with their start and end apart: 34, of which 17 were waited for; matrix products, arithmetic and copies ran while one was open for 7% of the time, Pallas kernels for 5%

profile of v2, /device:TPU:6, one launch (start us, length us, event | category | flops | bytes accessed | tf_op | source)
XLA Modules:
  0.0 147.0 jit_solution(7917417120606849789)
XLA Ops:
  0.6 1.9 %text_rows.1 = (bf16[64,1152]{1,0:T(8,128)(2,1)}, bf16[32,1152]{1,0:T(8,128)(2,1)}, bf16[32,1152]{1,0:T(8,128)(2,1)}) custom-call(f32[64,1152]{1,0:T(8,128)} %text_ref.1), custom_call_target="tpu_custom_call" | custom-call | tf_op jit(solution)/shard_map/text_rows/pallas_call | solution.py:52
  2.6 1.9 %multiply_reduce_fusion = f32[512]{0:T(512)S(1)} fusion(f32[512,1152]{1,0:T(8,128)} %param.4), kind=kLoop, calls=%fused_computation.5 | loop fusion | flops 1179136 | bytes 2361344 | tf_op jit(solution)/shard_map/reduce_sum | solution.py:36
  5.2 1.7 %fusion.12 = (bf16[512,1152]{1,0:T(8,128)(2,1)S(1)}, f32[512,1152]{1,0:T(8,128)}) fusion(f32[512,1152]{1,0:T(8,128)S(1)} %copy-done.8, f32[512]{0:T(512)S(1)} %get-tuple-element.80), kind=kLoop, calls=%fused_computation.43 | loop fusion | flops 1179648 | bytes 5900288 | tf_op jit(solution)/shard_map/convert_element_type | solution.py:230
  6.9 3.3 %collective-permute-start.4 = (bf16[32,1152]{1,0:T(8,128)(2,1)S(1)}, bf16[32,1152]{1,0:T(8,128)(2,1)S(1)}, u32[]{:S(2)}, u32[]{:S(2)}) collective-permute-start(bf16[32,1152]{1,0:T(8,128)(2,1)S(1)} %copy-done.12), channel_id=1, source_target_pairs={{0,4},{1,5},{8,12},{9,13},{16,20},{17,21},{24,28},{25,29},{32,36},... | collective-permute-start | bytes 221192 | tf_op jit(solution)/shard_map/ppermute | solution.py:32
  10.7 1.5 %collective-permute-start.2 = (bf16[64,1152]{1,0:T(8,128)(2,1)S(1)}, bf16[64,1152]{1,0:T(8,128)(2,1)S(1)}, u32[]{:S(2)}, u32[]{:S(2)}) collective-permute-start(bf16[64,1152]{1,0:T(8,128)(2,1)S(1)} %copy-done.5), channel_id=1, source_target_pairs={{0,24},{1,25},{8,0},{9,1},{16,8},{17,9},{24,16},{25,17},{32,56},{3... | collective-permute-start | bytes 442376 | tf_op jit(solution)/shard_map/ppermute | solution.py:32
  12.2 1.4 collective-permute-start.3
  13.6 2.6 %collective-permute-done.4.refs_4_ = bf16[32,1152]{1,0:T(8,128)(2,1)S(1)} collective-permute-done((bf16[32,1152]{1,0:T(8,128)(2,1)S(1)}, bf16[32,1152]{1,0:T(8,128)(2,1)S(1)}, u32[]{:S(2)}, u32[]{:S(2)}) %collective-permute-start.4) | collective-permute-done | bytes 73760 | tf_op jit(solution)/shard_map/ppermute | solution.py:32
  16.3 2.6 %collective-permute-start.5 = (bf16[32,1152]{1,0:T(8,128)(2,1)S(1)}, bf16[32,1152]{1,0:T(8,128)(2,1)S(1)}, u32[]{:S(2)}, u32[]{:S(2)}) collective-permute-start(bf16[32,1152]{1,0:T(8,128)(2,1)S(1)} %copy-done.11), channel_id=1, source_target_pairs={{0,132},{1,133},{8,140},{9,141},{16,148},{17,149},{24,156},{25,157... | collective-permute-start | bytes 221192 | tf_op jit(solution)/shard_map/ppermute | solution.py:32
  18.9 2.6 %collective-permute-done.5.refs_5_ = bf16[32,1152]{1,0:T(8,128)(2,1)S(1)} collective-permute-done((bf16[32,1152]{1,0:T(8,128)(2,1)S(1)}, bf16[32,1152]{1,0:T(8,128)(2,1)S(1)}, u32[]{:S(2)}, u32[]{:S(2)}) %collective-permute-start.5) | collective-permute-done | bytes 73760 | tf_op jit(solution)/shard_map/ppermute | solution.py:32
  21.5 1.7 %join.1 = (bf16[256,1152]{1,0:T(8,128)(2,1)S(1)}, bf16[64,1152]{1,0:T(8,128)(2,1)}) custom-call(bf16[64,1152]{1,0:T(8,128)(2,1)S(1)} %copy-done.5, bf16[64,1152]{1,0:T(8,128)(2,1)S(1)} %collective-permute-done.1.refs_1_, bf16[64,1152]{1,0:T(8,128)(2,1)S(1)} %collective-permute-done.2.refs_2_, bf16[64,1152]{1,0:T(8,128)(2,1)S(1)} %collective-permute-done.3.refs_3_, ...), custom_call_target="tpu_custom_call" | custom-call | tf_op jit(solution)/shard_map/join/pallas_call | solution.py:85
  23.2 3.0 %collective-permute-start.6 = (bf16[256,1152]{1,0:T(8,128)(2,1)S(1)}, bf16[256,1152]{1,0:T(8,128)(2,1)S(1)}, u32[]{:S(2)}, u32[]{:S(2)}) collective-permute-start(bf16[256,1152]{1,0:T(8,128)(2,1)S(1)} %get-tuple-element.41.refs_3_), channel_id=1, source_target_pairs={{0,2},{1,3},{8,10},{9,11},{16,18},{17,19},{24,26},{25,27},{32,34},... | collective-permute-start | bytes 1769480 | tf_op jit(solution)/shard_map/ppermute | solution.py:32
  26.2 2.0 %collective-permute-start.7 = (bf16[256,1152]{1,0:T(8,128)(2,1)S(1)}, bf16[256,1152]{1,0:T(8,128)(2,1)}, u32[]{:S(2)}, u32[]{:S(2)}) collective-permute-start(bf16[256,1152]{1,0:T(8,128)(2,1)S(1)} %get-tuple-element.41.refs_3_), channel_id=1, source_target_pairs={{0,134},{1,135},{8,142},{9,143},{16,150},{17,151},{24,158},{25,159... | collective-permute-start | bytes 1769480 | tf_op jit(solution)/shard_map/ppermute | solution.py:32
  28.3 1.4 collective-permute-start.10
  29.7 2.1 %collective-permute-start.8 = (bf16[64,1152]{1,0:T(8,128)(2,1)}, bf16[64,1152]{1,0:T(8,128)(2,1)}, u32[]{:S(2)}, u32[]{:S(2)}) collective-permute-start(bf16[64,1152]{1,0:T(8,128)(2,1)} %get-tuple-element.42.refs_6_), channel_id=1, source_target_pairs={{0,8},{1,9},{8,16},{9,17},{16,24},{17,25},{24,0},{25,1},{32,40},{3... | collective-permute-start | bytes 442376 | tf_op jit(solution)/shard_map/ppermute | solution.py:32
  31.8 3.4 %collective-permute-done.10.refs_9_ = bf16[64,1152]{1,0:T(8,128)(2,1)S(1)} collective-permute-done((bf16[64,1152]{1,0:T(8,128)(2,1)}, bf16[64,1152]{1,0:T(8,128)(2,1)S(1)}, u32[]{:S(2)}, u32[]{:S(2)}) %collective-permute-start.10) | collective-permute-done | bytes 147488 | tf_op jit(solution)/shard_map/ppermute | solution.py:32
  35.8 1.6 %collective-permute-start.9 = (bf16[64,1152]{1,0:T(8,128)(2,1)}, bf16[64,1152]{1,0:T(8,128)(2,1)}, u32[]{:S(2)}, u32[]{:S(2)}) collective-permute-start(bf16[64,1152]{1,0:T(8,128)(2,1)} %get-tuple-element.42.refs_6_), channel_id=1, source_target_pairs={{0,24},{1,25},{8,0},{9,1},{16,8},{17,9},{24,16},{25,17},{32,56},{3... | collective-permute-start | bytes 442376 | tf_op jit(solution)/shard_map/ppermute | solution.py:32
  38.2 4.3 %collective-permute-done.9.refs_8_ = bf16[64,1152]{1,0:T(8,128)(2,1)} collective-permute-done((bf16[64,1152]{1,0:T(8,128)(2,1)}, bf16[64,1152]{1,0:T(8,128)(2,1)}, u32[]{:S(2)}, u32[]{:S(2)}) %collective-permute-start.9) | collective-permute-done | bytes 147488 | tf_op jit(solution)/shard_map/ppermute | solution.py:32
  43.4 7.3 %other_rows.1 = (f32[512,1152]{1,0:T(8,128)S(1)}, bf16[4,1024,256]{2,1,0:T(8,128)(2,1)S(1)}, bf16[1024,1152]{1,0:T(8,128)(2,1)}, bf16[1024,1152]{1,0:T(8,128)(2,1)}, f32[3,8,1024]{2,1,0:T(8,128)S(1)}) custom-call(f32[2]{0:T(128)S(1)} %pad_maximum_fusion.refs_0_, s32[6]{0:T(128)S(1)} %stack.38.refs_1_, bf16[512,1152]{1,0:T(8,128)(2,1)S(1)} %collective-permute-done.refs_2_, ...), custom_call_target="tpu_custom_call" | custom-call | flops 2415919104 | bytes 7077888 | tf_op jit(solution)/shard_map/other_rows/pallas_call | solution.py:178
  50.8 1.7 %copy-done = bf16[1024,1152]{1,0:T(8,128)(2,1)S(1)} copy-done((bf16[1024,1152]{1,0:T(8,128)(2,1)S(1)}, bf16[1024,1152]{1,0:T(8,128)(2,1)}, u32[]{:S(2)}) %copy-start) | copy-done | bytes 2359320
  52.5 5.8 %own_rows.1 = (f32[512,1152]{1,0:T(8,128)S(1)}, bf16[4,1024,256]{2,1,0:T(8,128)(2,1)S(1)}, bf16[1024,1152]{1,0:T(8,128)(2,1)S(1)}, f32[8,128]{1,0:T(8,128)S(1)}) custom-call(f32[2]{0:T(128)S(1)} %pad_maximum_fusion.refs_0_, s32[6]{0:T(128)S(1)} %stack.38.refs_1_, ...), custom_call_target="tpu_custom_call", output_to_operand_aliasing={{1}: (5, {}), {2}: (6, {})} | custom-call | flops 2415919104 | bytes 7077888 | tf_op jit(solution)/shard_map/own_rows/pallas_call | solution.py:195
  60.4 1.6 %collective-permute-start.12 = (f16[128,1152]{1,0:T(8,128)(2,1)S(1)}, f16[128,1152]{1,0:T(8,128)(2,1)S(1)}, u32[]{:S(2)}, u32[]{:S(2)}) collective-permute-start(f16[128,1152]{1,0:T(8,128)(2,1)S(1)} %get-tuple-element.74), channel_id=1, source_target_pairs={{0,32},{1,33},{8,40},{9,41},{16,48},{17,49},{24,56},{25,57},{32,64... | collective-permute-start | bytes 884744 | tf_op jit(solution)/shard_map/ppermute | solution.py:32
  62.0 1.7 %collective-permute-start.13 = (f16[128,1152]{1,0:T(8,128)(2,1)S(1)}, f16[128,1152]{1,0:T(8,128)(2,1)S(1)}, u32[]{:S(2)}, u32[]{:S(2)}) collective-permute-start(f16[128,1152]{1,0:T(8,128)(2,1)S(1)} %get-tuple-element.73), channel_id=1, source_target_pairs={{0,96},{1,97},{8,104},{9,105},{16,112},{17,113},{24,120},{25,121},... | collective-permute-start | bytes 884744 | tf_op jit(solution)/shard_map/ppermute | solution.py:32
  63.6 2.0 %collective-permute-start.14 = (f16[128,1152]{1,0:T(8,128)(2,1)S(1)}, f16[128,1152]{1,0:T(8,128)(2,1)S(1)}, u32[]{:S(2)}, u32[]{:S(2)}) collective-permute-start(f16[128,1152]{1,0:T(8,128)(2,1)S(1)} %get-tuple-element.72), channel_id=1, source_target_pairs={{0,64},{1,65},{8,72},{9,73},{16,80},{17,81},{24,88},{25,89},{32,96... | collective-permute-start | bytes 884744 | tf_op jit(solution)/shard_map/ppermute | solution.py:32
  67.1 3.2 %collective-permute-done.27 = f32[8,128]{1,0:T(8,128)S(1)} collective-permute-done((f32[8,128]{1,0:T(8,128)S(1)}, f32[8,128]{1,0:T(8,128)S(1)}, u32[]{:S(2)}, u32[]{:S(2)}) %collective-permute-start.27) | collective-permute-done | bytes 4128 | tf_op jit(solution)/shard_map/ppermute | solution.py:283
  71.3 4.2 %collective-permute-done.28 = f32[8,128]{1,0:T(8,128)S(1)} collective-permute-done((f32[8,128]{1,0:T(8,128)S(1)}, f32[8,128]{1,0:T(8,128)S(1)}, u32[]{:S(2)}, u32[]{:S(2)}) %collective-permute-start.28) | collective-permute-done | bytes 4128 | tf_op jit(solution)/shard_map/ppermute | solution.py:283
  75.5 3.0 %collective-permute-done.14 = f16[128,1152]{1,0:T(8,128)(2,1)S(1)} collective-permute-done((f16[128,1152]{1,0:T(8,128)(2,1)S(1)}, f16[128,1152]{1,0:T(8,128)(2,1)S(1)}, u32[]{:S(2)}, u32[]{:S(2)}) %collective-permute-start.14) | collective-permute-done | bytes 294944 | tf_op jit(solution)/shard_map/ppermute | solution.py:32
  78.8 1.4 collective-permute-start.29
  80.2 2.5 %collective-permute-done.29 = f32[8,128]{1,0:T(8,128)S(1)} collective-permute-done((f32[8,128]{1,0:T(8,128)S(1)}, f32[8,128]{1,0:T(8,128)S(1)}, u32[]{:S(2)}, u32[]{:S(2)}) %collective-permute-start.29) | collective-permute-done | bytes 4128 | tf_op jit(solution)/shard_map/ppermute | solution.py:283
  82.7 1.2 collective-permute-start.30
  83.9 2.7 %convolution_convert_fusion = f16[256,1152]{1,0:T(8,128)(2,1)S(1)} fusion(bf16[1024,1152]{1,0:T(8,128)(2,1)} %copy-done.1, bf16[4,1024,256]{2,1,0:T(8,128)(2,1)} %copy-done.3), kind=kOutput, calls=%fused_computation | convolution fusion | flops 604274688 | bytes 3473408 | tf_op jit(solution)/shard_map/dot_general | solution.py:249
  88.7 1.9 %convolution_convert_fusion.1 = f16[256,1152]{1,0:T(8,128)(2,1)S(1)} fusion(bf16[1024,1152]{1,0:T(8,128)(2,1)S(1)} %copy-done.2, bf16[4,1024,256]{2,1,0:T(8,128)(2,1)} %copy-done.3), kind=kOutput, calls=%fused_computation.1 | convolution fusion | flops 604274688 | bytes 3473408 | tf_op jit(solution)/shard_map/dot_general | solution.py:249
  91.4 2.3 %collective-permute-start.32 = (f32[8,128]{1,0:T(8,128)S(1)}, f32[8,128]{1,0:T(8,128)S(1)}, u32[]{:S(2)}, u32[]{:S(2)}) collective-permute-start(f32[8,128]{1,0:T(8,128)S(1)} %add.176), channel_id=1, source_target_pairs={{0,4},{1,5},{2,6},{3,7},{4,0},{5,1},{6,2},{7,3},{8,12},{9,13},{10,... | collective-permute-start | bytes 12296 | tf_op jit(solution)/shard_map/ppermute | solution.py:283
  94.5 2.8 %collective-permute-start.15 = (f16[128,1152]{1,0:T(8,128)(2,1)S(1)}, f16[128,1152]{1,0:T(8,128)(2,1)S(1)}, u32[]{:S(2)}, u32[]{:S(2)}) collective-permute-start(f16[128,1152]{1,0:T(8,128)(2,1)S(1)} %add_convert_fusion.1), channel_id=1, source_target_pairs={{0,128},{1,129},{8,136},{9,137},{16,144},{17,145},{24,152},{25,153... | collective-permute-start | bytes 884744 | tf_op jit(solution)/shard_map/ppermute | solution.py:32
  97.3 3.9 %collective-permute-start.33 = (f32[8,128]{1,0:T(8,128)S(1)}, f32[8,128]{1,0:T(8,128)S(1)}, u32[]{:S(2)}, u32[]{:S(2)}) collective-permute-start(f32[8,128]{1,0:T(8,128)S(1)} %add.177), channel_id=1, source_target_pairs={{0,128},{1,129},{2,130},{3,131},{4,132},{5,133},{6,134},{7,135},{8... | collective-permute-start | bytes 12296 | tf_op jit(solution)/shard_map/ppermute | solution.py:283
  102.9 2.3 %collective-permute-start.20 = (f16[256,1152]{1,0:T(8,128)(2,1)S(1)}, f16[256,1152]{1,0:T(8,128)(2,1)S(1)}, u32[]{:S(2)}, u32[]{:S(2)}) collective-permute-start(f16[256,1152]{1,0:T(8,128)(2,1)S(1)} %convolution_convert_fusion.1), channel_id=1, source_target_pairs={{0,8},{1,9},{8,16},{9,17},{16,24},{17,25},{24,0},{25,1},{32,40},{3... | collective-permute-start | bytes 1769480 | tf_op jit(solution)/shard_map/ppermute | solution.py:32
  105.2 3.8 %collective-permute-done.33 = f32[8,128]{1,0:T(8,128)S(1)} collective-permute-done((f32[8,128]{1,0:T(8,128)S(1)}, f32[8,128]{1,0:T(8,128)S(1)}, u32[]{:S(2)}, u32[]{:S(2)}) %collective-permute-start.33) | collective-permute-done | bytes 4128 | tf_op jit(solution)/shard_map/ppermute | solution.py:283
  110.2 2.6 %collective-permute-start.17 = (f16[128,1152]{1,0:T(8,128)(2,1)S(1)}, f16[128,1152]{1,0:T(8,128)(2,1)S(1)}, u32[]{:S(2)}, u32[]{:S(2)}) collective-permute-start(f16[128,1152]{1,0:T(8,128)(2,1)S(1)} %subtract_convert_fusion), channel_id=1, source_target_pairs={{0,96},{1,97},{8,104},{9,105},{16,112},{17,113},{24,120},{25,121},... | collective-permute-start | bytes 884744 | tf_op jit(solution)/shard_map/ppermute | solution.py:32
  112.8 7.2 %collective-permute-done.21 = f16[256,1152]{1,0:T(8,128)(2,1)S(1)} collective-permute-done((f16[256,1152]{1,0:T(8,128)(2,1)S(1)}, f16[256,1152]{1,0:T(8,128)(2,1)S(1)}, u32[]{:S(2)}, u32[]{:S(2)}) %collective-permute-start.21) | collective-permute-done | bytes 589856 | tf_op jit(solution)/shard_map/ppermute | solution.py:32
  120.0 1.3 collective-permute-start.18
  121.3 3.8 %collective-permute-done.20 = f16[256,1152]{1,0:T(8,128)(2,1)S(1)} collective-permute-done((f16[256,1152]{1,0:T(8,128)(2,1)S(1)}, f16[256,1152]{1,0:T(8,128)(2,1)S(1)}, u32[]{:S(2)}, u32[]{:S(2)}) %collective-permute-start.20) | collective-permute-done | bytes 589856 | tf_op jit(solution)/shard_map/ppermute | solution.py:32
  125.0 2.2 %collective-permute-done.19 = f16[256,1152]{1,0:T(8,128)(2,1)S(1)} collective-permute-done((f16[256,1152]{1,0:T(8,128)(2,1)S(1)}, f16[256,1152]{1,0:T(8,128)(2,1)S(1)}, u32[]{:S(2)}, u32[]{:S(2)}) %collective-permute-start.19) | collective-permute-done | bytes 589856 | tf_op jit(solution)/shard_map/ppermute | solution.py:32
  127.6 2.7 %collective-permute-start.24 = (f16[32,1152]{1,0:T(8,128)(2,1)S(1)}, f16[32,1152]{1,0:T(8,128)(2,1)S(1)}, u32[]{:S(2)}, u32[]{:S(2)}) collective-permute-start(f16[32,1152]{1,0:T(8,128)(2,1)S(1)} %get-tuple-element.76), channel_id=1, source_target_pairs={{0,132},{1,133},{8,140},{9,141},{16,148},{17,149},{24,156},{25,157... | collective-permute-start | bytes 221192 | tf_op jit(solution)/shard_map/ppermute | solution.py:32
  130.6 3.3 %collective-permute-done.24 = f16[32,1152]{1,0:T(8,128)(2,1)S(1)} collective-permute-done((f16[32,1152]{1,0:T(8,128)(2,1)S(1)}, f16[32,1152]{1,0:T(8,128)(2,1)S(1)}, u32[]{:S(2)}, u32[]{:S(2)}) %collective-permute-start.24) | collective-permute-done | bytes 73760 | tf_op jit(solution)/shard_map/ppermute | solution.py:32
  134.0 3.4 %collective-permute-start.22 = (f16[64,1152]{1,0:T(8,128)(2,1)S(1)}, f16[64,1152]{1,0:T(8,128)(2,1)S(1)}, u32[]{:S(2)}, u32[]{:S(2)}) collective-permute-start(f16[64,1152]{1,0:T(8,128)(2,1)S(1)} %get-tuple-element.78), channel_id=1, source_target_pairs={{0,134},{1,135},{8,142},{9,143},{16,150},{17,151},{24,158},{25,159... | collective-permute-start | bytes 442376 | tf_op jit(solution)/shard_map/ppermute | solution.py:32
  137.4 1.7 %collective-permute-start.23 = (f16[64,1152]{1,0:T(8,128)(2,1)S(1)}, f16[64,1152]{1,0:T(8,128)(2,1)S(1)}, u32[]{:S(2)}, u32[]{:S(2)}) collective-permute-start(f16[64,1152]{1,0:T(8,128)(2,1)S(1)} %get-tuple-element.77), channel_id=1, source_target_pairs={{0,2},{1,3},{8,10},{9,11},{16,18},{17,19},{24,26},{25,27},{32,34},... | collective-permute-start | bytes 442376 | tf_op jit(solution)/shard_map/ppermute | solution.py:32
  140.3 1.9 %maximum_multiply_fusion = f32[3]{0:T(128)} fusion(f32[1]{0:T(128)} %get-tuple-element.82, f32[1]{0:T(128)} %bitcast.12, f32[1]{0:T(128)} %get-tuple-element.81), kind=kLoop, calls=%fused_computation.40 | loop fusion | flops 9 | bytes 24 | tf_op jit(solution)/shard_map/div | solution.py:286
  142.2 1.7 %collective-permute-done.23 = f16[64,1152]{1,0:T(8,128)(2,1)S(1)} collective-permute-done((f16[64,1152]{1,0:T(8,128)(2,1)S(1)}, f16[64,1152]{1,0:T(8,128)(2,1)S(1)}, u32[]{:S(2)}, u32[]{:S(2)}) %collective-permute-start.23) | collective-permute-done | bytes 147488 | tf_op jit(solution)/shard_map/ppermute | solution.py:32
  145.4 1.7 %convert_multiply_fusion = f32[512,1152]{1,0:T(8,128)} fusion(f16[512,1152]{1,0:T(8,128)(2,1)S(1)} %constant_dynamic-update-slice_fusion, f32[512]{0:T(512)S(1)} %get-tuple-element.79), kind=kLoop, calls=%fused_computation.4 | loop fusion | flops 1179648 | bytes 3540992 | tf_op jit(solution)/shard_map/mul | solution.py:271
  (86 shorter events, 16.4 us)
Async XLA Ops:
  0.6 4.5 %copy-start.8 = (f32[512,1152]{1,0:T(8,128)S(1)}, f32[512,1152]{1,0:T(8,128)}, u32[]{:S(2)}) copy-start(f32[512,1152]{1,0:T(8,128)} %param.4) | copy-start | bytes 7077892
  5.2 1.7 %copy-start.12 = (bf16[32,1152]{1,0:T(8,128)(2,1)S(1)}, bf16[32,1152]{1,0:T(8,128)(2,1)}, u32[]{:S(2)}) copy-start(bf16[32,1152]{1,0:T(8,128)(2,1)} %get-tuple-element.39) | copy-start | bytes 221188
  5.2 5.0 %copy-start.5 = (bf16[64,1152]{1,0:T(8,128)(2,1)S(1)}, bf16[64,1152]{1,0:T(8,128)(2,1)}, u32[]{:S(2)}) copy-start(bf16[64,1152]{1,0:T(8,128)(2,1)} %get-tuple-element.38.refs_0_) | copy-start | bytes 442372
  5.2 11.1 %copy-start.11 = (bf16[32,1152]{1,0:T(8,128)(2,1)S(1)}, bf16[32,1152]{1,0:T(8,128)(2,1)}, u32[]{:S(2)}) copy-start(bf16[32,1152]{1,0:T(8,128)(2,1)} %get-tuple-element.40) | copy-start | bytes 221188
  6.9 35.5 %collective-permute-start = (bf16[512,1152]{1,0:T(8,128)(2,1)S(1)}, bf16[512,1152]{1,0:T(8,128)(2,1)S(1)}, u32[]{:S(2)}, u32[]{:S(2)}) collective-permute-start(bf16[512,1152]{1,0:T(8,128)(2,1)S(1)} %get-tuple-element.69.refs_2_), channel_id=1, source_target_pairs={{0,1},{1,0},{8,9},{9,8},{16,17},{17,16},{24,25},{25,24},{32,33},{3... | collective-permute-start | bytes 3538952 | tf_op jit(solution)/shard_map/ppermute | solution.py:32
  6.9 9.3 %collective-permute-start.4 = (bf16[32,1152]{1,0:T(8,128)(2,1)S(1)}, bf16[32,1152]{1,0:T(8,128)(2,1)S(1)}, u32[]{:S(2)}, u32[]{:S(2)}) collective-permute-start(bf16[32,1152]{1,0:T(8,128)(2,1)S(1)} %copy-done.12), channel_id=1, source_target_pairs={{0,4},{1,5},{8,12},{9,13},{16,20},{17,21},{24,28},{25,29},{32,36},... | collective-permute-start | bytes 221192 | tf_op jit(solution)/shard_map/ppermute | solution.py:32
  10.2 11.3 %collective-permute-start.1 = (bf16[64,1152]{1,0:T(8,128)(2,1)S(1)}, bf16[64,1152]{1,0:T(8,128)(2,1)S(1)}, u32[]{:S(2)}, u32[]{:S(2)}) collective-permute-start(bf16[64,1152]{1,0:T(8,128)(2,1)S(1)} %copy-done.5), channel_id=1, source_target_pairs={{0,8},{1,9},{8,16},{9,17},{16,24},{17,25},{24,0},{25,1},{32,40},{3... | collective-permute-start | bytes 442376 | tf_op jit(solution)/shard_map/ppermute | solution.py:32
  10.7 10.8 %collective-permute-start.2 = (bf16[64,1152]{1,0:T(8,128)(2,1)S(1)}, bf16[64,1152]{1,0:T(8,128)(2,1)S(1)}, u32[]{:S(2)}, u32[]{:S(2)}) collective-permute-start(bf16[64,1152]{1,0:T(8,128)(2,1)S(1)} %copy-done.5), channel_id=1, source_target_pairs={{0,24},{1,25},{8,0},{9,1},{16,8},{17,9},{24,16},{25,17},{32,56},{3... | collective-permute-start | bytes 442376 | tf_op jit(solution)/shard_map/ppermute | solution.py:32
  12.2 9.3 %collective-permute-start.3 = (bf16[64,1152]{1,0:T(8,128)(2,1)S(1)}, bf16[64,1152]{1,0:T(8,128)(2,1)S(1)}, u32[]{:S(2)}, u32[]{:S(2)}) collective-permute-start(bf16[64,1152]{1,0:T(8,128)(2,1)S(1)} %copy-done.5), channel_id=1, source_target_pairs={{0,16},{1,17},{8,24},{9,25},{16,0},{17,1},{24,8},{25,9},{32,48},{3... | collective-permute-start | bytes 442376 | tf_op jit(solution)/shard_map/ppermute | solution.py:32
  16.3 5.3 %collective-permute-start.5 = (bf16[32,1152]{1,0:T(8,128)(2,1)S(1)}, bf16[32,1152]{1,0:T(8,128)(2,1)S(1)}, u32[]{:S(2)}, u32[]{:S(2)}) collective-permute-start(bf16[32,1152]{1,0:T(8,128)(2,1)S(1)} %copy-done.11), channel_id=1, source_target_pairs={{0,132},{1,133},{8,140},{9,141},{16,148},{17,149},{24,156},{25,157... | collective-permute-start | bytes 221192 | tf_op jit(solution)/shard_map/ppermute | solution.py:32
  23.2 19.2 %collective-permute-start.6 = (bf16[256,1152]{1,0:T(8,128)(2,1)S(1)}, bf16[256,1152]{1,0:T(8,128)(2,1)S(1)}, u32[]{:S(2)}, u32[]{:S(2)}) collective-permute-start(bf16[256,1152]{1,0:T(8,128)(2,1)S(1)} %get-tuple-element.41.refs_3_), channel_id=1, source_target_pairs={{0,2},{1,3},{8,10},{9,11},{16,18},{17,19},{24,26},{25,27},{32,34},... | collective-permute-start | bytes 1769480 | tf_op jit(solution)/shard_map/ppermute | solution.py:32
  26.2 16.2 %collective-permute-start.7 = (bf16[256,1152]{1,0:T(8,128)(2,1)S(1)}, bf16[256,1152]{1,0:T(8,128)(2,1)}, u32[]{:S(2)}, u32[]{:S(2)}) collective-permute-start(bf16[256,1152]{1,0:T(8,128)(2,1)S(1)} %get-tuple-element.41.refs_3_), channel_id=1, source_target_pairs={{0,134},{1,135},{8,142},{9,143},{16,150},{17,151},{24,158},{25,159... | collective-permute-start | bytes 1769480 | tf_op jit(solution)/shard_map/ppermute | solution.py:32
  28.3 6.9 %collective-permute-start.10 = (bf16[64,1152]{1,0:T(8,128)(2,1)}, bf16[64,1152]{1,0:T(8,128)(2,1)S(1)}, u32[]{:S(2)}, u32[]{:S(2)}) collective-permute-start(bf16[64,1152]{1,0:T(8,128)(2,1)} %get-tuple-element.42.refs_6_), channel_id=1, source_target_pairs={{0,16},{1,17},{8,24},{9,25},{16,0},{17,1},{24,8},{25,9},{32,48},{3... | collective-permute-start | bytes 442376 | tf_op jit(solution)/shard_map/ppermute | solution.py:32
  29.7 8.5 %collective-permute-start.8 = (bf16[64,1152]{1,0:T(8,128)(2,1)}, bf16[64,1152]{1,0:T(8,128)(2,1)}, u32[]{:S(2)}, u32[]{:S(2)}) collective-permute-start(bf16[64,1152]{1,0:T(8,128)(2,1)} %get-tuple-element.42.refs_6_), channel_id=1, source_target_pairs={{0,8},{1,9},{8,16},{9,17},{16,24},{17,25},{24,0},{25,1},{32,40},{3... | collective-permute-start | bytes 442376 | tf_op jit(solution)/shard_map/ppermute | solution.py:32
  35.1 0.7 copy-start.6
  35.8 6.7 %collective-permute-start.9 = (bf16[64,1152]{1,0:T(8,128)(2,1)}, bf16[64,1152]{1,0:T(8,128)(2,1)}, u32[]{:S(2)}, u32[]{:S(2)}) collective-permute-start(bf16[64,1152]{1,0:T(8,128)(2,1)} %get-tuple-element.42.refs_6_), channel_id=1, source_target_pairs={{0,24},{1,25},{8,0},{9,1},{16,8},{17,9},{24,16},{25,17},{32,56},{3... | collective-permute-start | bytes 442376 | tf_op jit(solution)/shard_map/ppermute | solution.py:32
  42.5 0.9 copy-start.7
  50.7 7.6 %collective-permute-start.11 = (f32[512,1152]{1,0:T(8,128)S(1)}, f32[512,1152]{1,0:T(8,128)S(1)}, u32[]{:S(2)}, u32[]{:S(2)}) collective-permute-start(f32[512,1152]{1,0:T(8,128)S(1)} %get-tuple-element.50), channel_id=1, source_target_pairs={{0,1},{1,0},{8,9},{9,8},{16,17},{17,16},{24,25},{25,24},{32,33},{3... | collective-permute-start | bytes 7077896 | tf_op jit(solution)/shard_map/ppermute | solution.py:32
  50.8 1.7 %copy-start = (bf16[1024,1152]{1,0:T(8,128)(2,1)S(1)}, bf16[1024,1152]{1,0:T(8,128)(2,1)}, u32[]{:S(2)}) copy-start(bf16[1024,1152]{1,0:T(8,128)(2,1)} %get-tuple-element.46.refs_6_) | copy-start | bytes 7077892
  58.3 1.4 copy-start.1
  58.3 2.1 %copy-start.3 = (bf16[4,1024,256]{2,1,0:T(8,128)(2,1)}, bf16[4,1024,256]{2,1,0:T(8,128)(2,1)S(1)}, u32[]{:S(2)}) copy-start(bf16[4,1024,256]{2,1,0:T(8,128)(2,1)S(1)} %get-tuple-element.52) | copy-start | bytes 6291460
  58.4 12.8 %copy-start.10 = (f32[64,1152]{1,0:T(8,128)S(1)}, f32[64,1152]{1,0:T(8,128)}, u32[]{:S(2)}) copy-start(f32[64,1152]{1,0:T(8,128)} %text_ref.1) | copy-start | bytes 884740
  60.4 15.1 %collective-permute-start.12 = (f16[128,1152]{1,0:T(8,128)(2,1)S(1)}, f16[128,1152]{1,0:T(8,128)(2,1)S(1)}, u32[]{:S(2)}, u32[]{:S(2)}) collective-permute-start(f16[128,1152]{1,0:T(8,128)(2,1)S(1)} %get-tuple-element.74), channel_id=1, source_target_pairs={{0,32},{1,33},{8,40},{9,41},{16,48},{17,49},{24,56},{25,57},{32,64... | collective-permute-start | bytes 884744 | tf_op jit(solution)/shard_map/ppermute | solution.py:32
  62.0 13.5 %collective-permute-start.13 = (f16[128,1152]{1,0:T(8,128)(2,1)S(1)}, f16[128,1152]{1,0:T(8,128)(2,1)S(1)}, u32[]{:S(2)}, u32[]{:S(2)}) collective-permute-start(f16[128,1152]{1,0:T(8,128)(2,1)S(1)} %get-tuple-element.73), channel_id=1, source_target_pairs={{0,96},{1,97},{8,104},{9,105},{16,112},{17,113},{24,120},{25,121},... | collective-permute-start | bytes 884744 | tf_op jit(solution)/shard_map/ppermute | solution.py:32
  63.6 14.9 %collective-permute-start.14 = (f16[128,1152]{1,0:T(8,128)(2,1)S(1)}, f16[128,1152]{1,0:T(8,128)(2,1)S(1)}, u32[]{:S(2)}, u32[]{:S(2)}) collective-permute-start(f16[128,1152]{1,0:T(8,128)(2,1)S(1)} %get-tuple-element.72), channel_id=1, source_target_pairs={{0,64},{1,65},{8,72},{9,73},{16,80},{17,81},{24,88},{25,89},{32,96... | collective-permute-start | bytes 884744 | tf_op jit(solution)/shard_map/ppermute | solution.py:32
  65.6 1.2 collective-permute-start.26
  66.8 3.6 %collective-permute-start.27 = (f32[8,128]{1,0:T(8,128)S(1)}, f32[8,128]{1,0:T(8,128)S(1)}, u32[]{:S(2)}, u32[]{:S(2)}) collective-permute-start(f32[8,128]{1,0:T(8,128)S(1)} %add.171), channel_id=1, source_target_pairs={{0,8},{1,9},{2,10},{3,11},{4,12},{5,13},{6,14},{7,15},{8,0},{9,1},... | collective-permute-start | bytes 12296 | tf_op jit(solution)/shard_map/ppermute | solution.py:283
  70.4 5.1 %collective-permute-start.28 = (f32[8,128]{1,0:T(8,128)S(1)}, f32[8,128]{1,0:T(8,128)S(1)}, u32[]{:S(2)}, u32[]{:S(2)}) collective-permute-start(f32[8,128]{1,0:T(8,128)S(1)} %add.172), channel_id=1, source_target_pairs={{0,16},{1,17},{2,18},{3,19},{4,20},{5,21},{6,22},{7,23},{8,24},{9,... | collective-permute-start | bytes 12296 | tf_op jit(solution)/shard_map/ppermute | solution.py:283
  78.8 10.0 %copy-start.2 = (bf16[1024,1152]{1,0:T(8,128)(2,1)S(1)}, bf16[1024,1152]{1,0:T(8,128)(2,1)}, u32[]{:S(2)}) copy-start(bf16[1024,1152]{1,0:T(8,128)(2,1)} %copy-done.1) | copy-start | bytes 7077892
  78.8 3.9 %collective-permute-start.29 = (f32[8,128]{1,0:T(8,128)S(1)}, f32[8,128]{1,0:T(8,128)S(1)}, u32[]{:S(2)}, u32[]{:S(2)}) collective-permute-start(f32[8,128]{1,0:T(8,128)S(1)} %add.173), channel_id=1, source_target_pairs={{0,32},{1,33},{2,34},{3,35},{4,36},{5,37},{6,38},{7,39},{8,40},{9,... | collective-permute-start | bytes 12296 | tf_op jit(solution)/shard_map/ppermute | solution.py:283
  82.7 5.1 %collective-permute-start.30 = (f32[8,128]{1,0:T(8,128)S(1)}, f32[8,128]{1,0:T(8,128)S(1)}, u32[]{:S(2)}, u32[]{:S(2)}) collective-permute-start(f32[8,128]{1,0:T(8,128)S(1)} %add.174), channel_id=1, source_target_pairs={{0,64},{1,65},{2,66},{3,67},{4,68},{5,69},{6,70},{7,71},{8,72},{9,... | collective-permute-start | bytes 12296 | tf_op jit(solution)/shard_map/ppermute | solution.py:283
  86.6 7.0 %copy-start.4 = (bf16[4,1024,256]{2,1,0:T(8,128)(2,1)S(1)}, bf16[4,1024,256]{2,1,0:T(8,128)(2,1)}, u32[]{:S(2)}) copy-start(bf16[4,1024,256]{2,1,0:T(8,128)(2,1)} %copy-done.3) | copy-start | bytes 6291460
  87.8 3.6 %collective-permute-start.31 = (f32[8,128]{1,0:T(8,128)S(1)}, f32[8,128]{1,0:T(8,128)S(1)}, u32[]{:S(2)}, u32[]{:S(2)}) collective-permute-start(f32[8,128]{1,0:T(8,128)S(1)} %add.175), channel_id=1, source_target_pairs={{0,2},{1,3},{2,0},{3,1},{4,6},{5,7},{6,4},{7,5},{8,10},{9,11},{10,... | collective-permute-start | bytes 12296 | tf_op jit(solution)/shard_map/ppermute | solution.py:283
  91.4 5.9 %collective-permute-start.32 = (f32[8,128]{1,0:T(8,128)S(1)}, f32[8,128]{1,0:T(8,128)S(1)}, u32[]{:S(2)}, u32[]{:S(2)}) collective-permute-start(f32[8,128]{1,0:T(8,128)S(1)} %add.176), channel_id=1, source_target_pairs={{0,4},{1,5},{2,6},{3,7},{4,0},{5,1},{6,2},{7,3},{8,12},{9,13},{10,... | collective-permute-start | bytes 12296 | tf_op jit(solution)/shard_map/ppermute | solution.py:283
  94.5 14.6 %copy-start.9 = (f32[512,1152]{1,0:T(8,128)S(1)}, f32[512,1152]{1,0:T(8,128)}, u32[]{:S(2)}) copy-start(f32[512,1152]{1,0:T(8,128)} %get-tuple-element.70) | copy-start | bytes 7077892
  94.5 14.6 %collective-permute-start.15 = (f16[128,1152]{1,0:T(8,128)(2,1)S(1)}, f16[128,1152]{1,0:T(8,128)(2,1)S(1)}, u32[]{:S(2)}, u32[]{:S(2)}) collective-permute-start(f16[128,1152]{1,0:T(8,128)(2,1)S(1)} %add_convert_fusion.1), channel_id=1, source_target_pairs={{0,128},{1,129},{8,136},{9,137},{16,144},{17,145},{24,152},{25,153... | collective-permute-start | bytes 884744 | tf_op jit(solution)/shard_map/ppermute | solution.py:32
  97.3 11.7 %collective-permute-start.33 = (f32[8,128]{1,0:T(8,128)S(1)}, f32[8,128]{1,0:T(8,128)S(1)}, u32[]{:S(2)}, u32[]{:S(2)}) collective-permute-start(f32[8,128]{1,0:T(8,128)S(1)} %add.177), channel_id=1, source_target_pairs={{0,128},{1,129},{2,130},{3,131},{4,132},{5,133},{6,134},{7,135},{8... | collective-permute-start | bytes 12296 | tf_op jit(solution)/shard_map/ppermute | solution.py:283
  102.1 17.9 %collective-permute-start.21 = (f16[256,1152]{1,0:T(8,128)(2,1)S(1)}, f16[256,1152]{1,0:T(8,128)(2,1)S(1)}, u32[]{:S(2)}, u32[]{:S(2)}) collective-permute-start(f16[256,1152]{1,0:T(8,128)(2,1)S(1)} %convolution_convert_fusion), channel_id=1, source_target_pairs={{0,16},{1,17},{8,24},{9,25},{16,0},{17,1},{24,8},{25,9},{32,48},{3... | collective-permute-start | bytes 1769480 | tf_op jit(solution)/shard_map/ppermute | solution.py:32
  102.9 22.1 %collective-permute-start.20 = (f16[256,1152]{1,0:T(8,128)(2,1)S(1)}, f16[256,1152]{1,0:T(8,128)(2,1)S(1)}, u32[]{:S(2)}, u32[]{:S(2)}) collective-permute-start(f16[256,1152]{1,0:T(8,128)(2,1)S(1)} %convolution_convert_fusion.1), channel_id=1, source_target_pairs={{0,8},{1,9},{8,16},{9,17},{16,24},{17,25},{24,0},{25,1},{32,40},{3... | collective-permute-start | bytes 1769480 | tf_op jit(solution)/shard_map/ppermute | solution.py:32
  105.2 22.0 %collective-permute-start.19 = (f16[256,1152]{1,0:T(8,128)(2,1)S(1)}, f16[256,1152]{1,0:T(8,128)(2,1)S(1)}, u32[]{:S(2)}, u32[]{:S(2)}) collective-permute-start(f16[256,1152]{1,0:T(8,128)(2,1)S(1)} %convolution_convert_fusion.2), channel_id=1, source_target_pairs={{0,24},{1,25},{8,0},{9,1},{16,8},{17,9},{24,16},{25,17},{32,56},{3... | collective-permute-start | bytes 1769480 | tf_op jit(solution)/shard_map/ppermute | solution.py:32
  109.5 34.4 %collective-permute-start.16 = (f16[128,1152]{1,0:T(8,128)(2,1)S(1)}, f16[128,1152]{1,0:T(8,128)(2,1)S(1)}, u32[]{:S(2)}, u32[]{:S(2)}) collective-permute-start(f16[128,1152]{1,0:T(8,128)(2,1)S(1)} %subtract_convert_fusion), channel_id=1, source_target_pairs={{0,32},{1,33},{8,40},{9,41},{16,48},{17,49},{24,56},{25,57},{32,64... | collective-permute-start | bytes 884744 | tf_op jit(solution)/shard_map/ppermute | solution.py:32
  110.2 33.7 %collective-permute-start.17 = (f16[128,1152]{1,0:T(8,128)(2,1)S(1)}, f16[128,1152]{1,0:T(8,128)(2,1)S(1)}, u32[]{:S(2)}, u32[]{:S(2)}) collective-permute-start(f16[128,1152]{1,0:T(8,128)(2,1)S(1)} %subtract_convert_fusion), channel_id=1, source_target_pairs={{0,96},{1,97},{8,104},{9,105},{16,112},{17,113},{24,120},{25,121},... | collective-permute-start | bytes 884744 | tf_op jit(solution)/shard_map/ppermute | solution.py:32
  120.0 23.9 %collective-permute-start.18 = (f16[128,1152]{1,0:T(8,128)(2,1)S(1)}, f16[128,1152]{1,0:T(8,128)(2,1)S(1)}, u32[]{:S(2)}, u32[]{:S(2)}) collective-permute-start(f16[128,1152]{1,0:T(8,128)(2,1)S(1)} %subtract_convert_fusion), channel_id=1, source_target_pairs={{0,64},{1,65},{8,72},{9,73},{16,80},{17,81},{24,88},{25,89},{32,96... | collective-permute-start | bytes 884744 | tf_op jit(solution)/shard_map/ppermute | solution.py:32
  127.6 6.4 %collective-permute-start.24 = (f16[32,1152]{1,0:T(8,128)(2,1)S(1)}, f16[32,1152]{1,0:T(8,128)(2,1)S(1)}, u32[]{:S(2)}, u32[]{:S(2)}) collective-permute-start(f16[32,1152]{1,0:T(8,128)(2,1)S(1)} %get-tuple-element.76), channel_id=1, source_target_pairs={{0,132},{1,133},{8,140},{9,141},{16,148},{17,149},{24,156},{25,157... | collective-permute-start | bytes 221192 | tf_op jit(solution)/shard_map/ppermute | solution.py:32
  130.3 7.1 %collective-permute-start.25 = (f16[32,1152]{1,0:T(8,128)(2,1)S(1)}, f16[32,1152]{1,0:T(8,128)(2,1)S(1)}, u32[]{:S(2)}, u32[]{:S(2)}) collective-permute-start(f16[32,1152]{1,0:T(8,128)(2,1)S(1)} %get-tuple-element.75), channel_id=1, source_target_pairs={{0,4},{1,5},{8,12},{9,13},{16,20},{17,21},{24,28},{25,29},{32,36},... | collective-permute-start | bytes 221192 | tf_op jit(solution)/shard_map/ppermute | solution.py:32
  134.0 8.3 %collective-permute-start.22 = (f16[64,1152]{1,0:T(8,128)(2,1)S(1)}, f16[64,1152]{1,0:T(8,128)(2,1)S(1)}, u32[]{:S(2)}, u32[]{:S(2)}) collective-permute-start(f16[64,1152]{1,0:T(8,128)(2,1)S(1)} %get-tuple-element.78), channel_id=1, source_target_pairs={{0,134},{1,135},{8,142},{9,143},{16,150},{17,151},{24,158},{25,159... | collective-permute-start | bytes 442376 | tf_op jit(solution)/shard_map/ppermute | solution.py:32
  137.4 6.5 %collective-permute-start.23 = (f16[64,1152]{1,0:T(8,128)(2,1)S(1)}, f16[64,1152]{1,0:T(8,128)(2,1)S(1)}, u32[]{:S(2)}, u32[]{:S(2)}) collective-permute-start(f16[64,1152]{1,0:T(8,128)(2,1)S(1)} %get-tuple-element.77), channel_id=1, source_target_pairs={{0,2},{1,3},{8,10},{9,11},{16,18},{17,19},{24,26},{25,27},{32,34},... | collective-permute-start | bytes 442376 | tf_op jit(solution)/shard_map/ppermute | solution.py:32

commit v3 on v2

--- a/solution.py
+++ b/solution.py
@@ -7,6 +7,7 @@
 
 AXES = ("group", "blk")
 SEND = jnp.float16
+STAT_SCALE = 2.0**-14
 VMEM_BYTES = 58 * 1024 * 1024
 PAIR_VMEM_BYTES = 44 * 1024 * 1024
 SMEM = pl.BlockSpec(memory_space=pltpu.SMEM)
@@ -30,6 +31,22 @@
 
 def move(value, **shift):
     return lax.ppermute(value, AXES, shifted(**shift))
+
+
+def sums_rows(total, width):
+    high = lax.optimization_barrier(total.astype(SEND))
+    low = (total - high.astype(jnp.float32)).astype(SEND)
+    sums = jnp.pad(jnp.concatenate([high, low]), ((0, 0), (0, width - total.shape[1])))
+    return lax.optimization_barrier(sums)
+
+
+def ring_sum(own, ahead, behind, far):
+    return (own + far) + (ahead + behind)
+
+
+def sums_of(message):
+    high, low = message[-8:-4, :128], message[-4:, :128]
+    return high.astype(jnp.float32) + low.astype(jnp.float32)
 
 
 def normalize_rows(matrix):
@@ -160,7 +177,8 @@
         for k in range(3):
             stat = stat_ref[k]
             lanes = sum(stat[:, 128 * i : 128 * (i + 1)] for i in range(stat.shape[1] // 128))
-            total_ref[k : k + 1, :] = jnp.sum(lanes, axis=0, keepdims=True)
+            each = jnp.sum(jnp.sum(lanes, axis=0, keepdims=True), axis=1, keepdims=True)
+            total_ref[k : k + 1, :] = jnp.broadcast_to(each * STAT_SCALE, (1, 128))
 
 
 def pair_terms(scalars, place, other, own, col, below, above, far):
@@ -242,7 +260,11 @@
         (grad_own[k * quarter : (k + 1) * quarter] + received[k * quarter : (k + 1) * quarter]).astype(SEND)
         for k in range(4)
     ]
-    arrived = [move(parts[1], dy=1), move(parts[2], dy=-1), move(parts[3], dy=2)]
+    total = total[:4]
+    for bit in (0, 3, 4):
+        total += lax.ppermute(total, AXES, [(i, i ^ (1 << bit)) for i in range(256)])
+    own_sums = sums_rows(total, width)
+    arrived = [move(jnp.concatenate([part, own_sums]), dy=dy) for part, dy in zip(parts[1:], (1, -1, 2))]
 
     coef, copies, parts[0] = lax.optimization_barrier((coef, copies, parts[0]))
     blocks = [
@@ -251,39 +273,45 @@
     ]
     x_terms = [blocks[0], move(blocks[1], dx=-1), move(blocks[2], dx=1), move(blocks[3], dx=2)]
 
-    y_sum = sum(part.astype(jnp.float32) for part in [parts[0]] + arrived).astype(SEND)
-    image_grad = y_sum.astype(jnp.float32) + move(y_sum, dz=4).astype(jnp.float32)
+    y_sum = sum(part[:quarter].astype(jnp.float32) for part in [parts[0]] + arrived).astype(SEND)
+    total = ring_sum(sums_of(own_sums), *[sums_of(message) for message in arrived])
+    y_sum = lax.optimization_barrier(jnp.concatenate([y_sum, sums_rows(total, width)]))
+    z_sum = move(y_sum, dz=4)
+    total = sums_of(y_sum) + sums_of(z_sum)
+    image_grad = y_sum[:quarter].astype(jnp.float32) + z_sum[:quarter].astype(jnp.float32)
     unit_part = lax.dynamic_slice_in_dim(unit_image, y * quarter, quarter)
     tangent = (image_grad - unit_part * jnp.sum(unit_part * image_grad, axis=1, keepdims=True)).astype(SEND)
+    tangent = lax.optimization_barrier(tangent)
     tangents = [tangent] + [move(tangent, dy=dy) for dy in (1, -1, 2)]
 
     n = caption_embeddings.shape[0]
     h = n // 2
-    *x_terms, tangent = lax.optimization_barrier((*x_terms, tangent))
+    *x_terms, tangents[1] = lax.optimization_barrier((*x_terms, tangents[1]))
     x_sum = sum(term.astype(jnp.float32) for term in x_terms).astype(SEND)
-    near = [move(x_sum[n : 2 * n], dz=-1), move(x_sum[2 * n : 3 * n], dz=1)]
-    ends_sum = [move(x_sum[3 * n : 3 * n + h], dz=-2), move(x_sum[3 * n + h :], dz=2)]
-    *tangents, near[0], near[1], ends_sum[0], ends_sum[1] = lax.optimization_barrier((*tangents, *near, *ends_sum))
+    own_sums = sums_rows(total, width)
+    ride = lambda rows: jnp.concatenate([rows, own_sums])
+    near = [move(ride(x_sum[n : 2 * n]), dz=-1), move(ride(x_sum[2 * n : 3 * n]), dz=1)]
+    ends_sum = [move(ride(x_sum[3 * n : 3 * n + h]), dz=-2), move(x_sum[3 * n + h :], dz=2)]
 
     slope = jnp.zeros((count, width), SEND)
     for dy, got in zip((0, 1, -1, 2), tangents):
         slope = lax.dynamic_update_slice_in_dim(slope, got, ((y - dy) % 4) * quarter, 0)
     picture_embedding_slope = slope.astype(jnp.float32) * (temperature * inv_image)
-
-    text_sum = x_sum[:n].astype(jnp.float32) + jnp.concatenate(ends_sum).astype(jnp.float32)
-    text_sum += near[0].astype(jnp.float32) + near[1].astype(jnp.float32)
+    picture_embedding_slope, near[0], near[1], ends_sum[0], ends_sum[1] = lax.optimization_barrier(
+        (picture_embedding_slope, *near, *ends_sum)
+    )
+
+    total = ring_sum(*[sums_of(message) for message in (own_sums, near[0], near[1], ends_sum[0])])
+    text_sum = x_sum[:n].astype(jnp.float32) + jnp.concatenate([ends_sum[0][:h], ends_sum[1]]).astype(jnp.float32)
+    text_sum += near[0][:n].astype(jnp.float32) + near[1][:n].astype(jnp.float32)
     unit_text, inv_text = normalize_rows(caption_embeddings)
     text_grad = (text_sum - unit_text * jnp.sum(unit_text * text_sum, axis=1, keepdims=True)) * (
         temperature * inv_text
     )
 
-    for done, bits in ((parts[0], (0, 3, 4)), (y_sum, (5, 6)), (tangent, (1, 2, 7))):
-        total, _ = lax.optimization_barrier((total, done))
-        for bit in bits:
-            total += lax.ppermute(total, AXES, [(i, i ^ (1 << bit)) for i in range(256)])
-    total = jnp.sum(total, axis=1)
     rows_overall = count * lax.axis_size("blk")
-    statistics = jnp.stack([total[0], temperature * total[1], total[2]]) / rows_overall
+    scale = jnp.where(jnp.arange(3) == 1, temperature, 1.0) / (STAT_SCALE * rows_overall)
+    statistics = total[:3, 0] * scale
     return (picture_embedding_slope, text_grad, statistics)
 
 

time: 147 us -> 140 us (0.952)
  starting transfers between devices: 54.3 us -> 43.9 us
  waiting for transfers between devices: 50.8 us -> 54.3 us
  matrix products: 6.37 us -> 3.47 us
  Pallas kernels: 16.8 us -> 18.7 us
    ppermute x26, waiting for transfers between devices: 34.1 us -> 46.1 us  [move(): return lax.ppermute(value, AXES, shifted(**shift))]
    ppermute x8 -> x3, starting transfers between devices: 10.9 us -> 1.66 us  [per_device(): total += lax.ppermute(total, AXES, [(i, i ^ 1 << bit) for i in range(256)])]
    ppermute x8 -> x3, waiting for transfers between devices: 16.8 us -> 8.2 us  [per_device(): total += lax.ppermute(total, AXES, [(i, i ^ 1 << bit) for i in range(256)])]
    dot_general x4, matrix products: 6.37 us -> 3.47 us  [per_device(): lax.dot_general(coef[k], copies, (((0,), (0,)), ((), ())), preferred_elem...]
    div x1 -> x0, other arithmetic: 1.88 us -> none  [per_device(): jnp.stack([total[0], temperature * total[1], total[2]]) / rows_overall]
    pallas_call x1, Pallas kernels: 7.34 us -> 9.18 us  [pair_terms(): pl.pallas_call(lambda *refs: pair_kernel(0, *refs), grid=(1,), in_specs=[...]
    convert_element_type x1, other arithmetic: 0.24 us -> 1.99 us  [per_device(): (grad_own[k * quarter:(k + 1) * quarter] + received[k * quarter:(k + 1) *...]
    unnamed x26 -> x28, local copies, waits for them, and re-layouts: 5.03 us -> 6.02 us
  transfers between devices with their start and end apart: 34 -> 29, of which waited for: 17 -> 16; matrix products, arithmetic and copies ran while one was open for 7% -> 5% of each run, Pallas kernels for 5% -> 5%
where the time goes in v3:
time: 140 us
  waiting for transfers between devices  54.3 us (39%)
  starting transfers between devices  43.9 us (31%)
  Pallas kernels  18.7 us (13%)
  other arithmetic  10.5 us (8%)
  local copies, waits for them, and re-layouts  6.68 us (5%)
  matrix products  3.47 us (2%)
  between operations  2.32 us (2%)
    ppermute x26, waiting for transfers between devices, move(): return lax.ppermute(value, AXES, shifted(**shift))  46.1 us
    ppermute x26, starting transfers between devices, move(): return lax.ppermute(value, AXES, shifted(**shift))  42.2 us
    pallas_call x1, Pallas kernels, pair_terms(): pl.pallas_call(lambda *refs: pair_kernel(0, *refs), grid=(1,), in_specs=[...  9.18 us
    ppermute x3, waiting for transfers between devices, per_device(): total += lax.ppermute(total, AXES, [(i, i ^ 1 << bit) for i in range(256)])  8.2 us
    unnamed x28, local copies, waits for them, and re-layouts  6.02 us
    pallas_call x1, Pallas kernels, pair_terms(): pl.pallas_call(lambda *refs: pair_kernel(1, *refs), grid=(1,), in_specs=[...  5.92 us
    dot_general x4, matrix products, per_device(): lax.dot_general(coef[k], copies, (((0,), (0,)), ((), ())), preferred_elem...  3.47 us
  transfers between devices with their start and end apart: 29, of which 16 were waited for; matrix products, arithmetic and copies ran while one was open for 5% of the time, Pallas kernels for 5%

profile of v3, /device:TPU:6, one launch (start us, length us, event | category | flops | bytes accessed | tf_op | source)
XLA Modules:
  0.0 139.8 jit_solution(4774679748878090852)
XLA Ops:
  0.6 1.9 %text_rows.1 = (bf16[64,1152]{1,0:T(8,128)(2,1)}, bf16[32,1152]{1,0:T(8,128)(2,1)}, bf16[32,1152]{1,0:T(8,128)(2,1)}) custom-call(f32[64,1152]{1,0:T(8,128)} %text_ref.1), custom_call_target="tpu_custom_call" | custom-call | tf_op jit(solution)/shard_map/text_rows/pallas_call | solution.py:69
  2.6 1.9 %multiply_reduce_fusion = f32[512]{0:T(512)S(1)} fusion(f32[512,1152]{1,0:T(8,128)} %param.4), kind=kLoop, calls=%fused_computation.5 | loop fusion | flops 1179136 | bytes 2361344 | tf_op jit(solution)/shard_map/reduce_sum | solution.py:53
  5.2 1.7 %fusion.25 = (bf16[512,1152]{1,0:T(8,128)(2,1)S(1)}, f32[512,1152]{1,0:T(8,128)}) fusion(f32[512,1152]{1,0:T(8,128)S(1)} %copy-done.8, f32[512]{0:T(512)S(1)} %get-tuple-element.81), kind=kLoop, calls=%fused_computation.71 | loop fusion | flops 1179648 | bytes 5900288 | tf_op jit(solution)/shard_map/convert_element_type | solution.py:248
  6.9 3.3 %collective-permute-start.4 = (bf16[32,1152]{1,0:T(8,128)(2,1)S(1)}, bf16[32,1152]{1,0:T(8,128)(2,1)S(1)}, u32[]{:S(2)}, u32[]{:S(2)}) collective-permute-start(bf16[32,1152]{1,0:T(8,128)(2,1)S(1)} %copy-done.13), channel_id=1, source_target_pairs={{0,4},{1,5},{8,12},{9,13},{16,20},{17,21},{24,28},{25,29},{32,36},... | collective-permute-start | bytes 221192 | tf_op jit(solution)/shard_map/ppermute | solution.py:33
  10.7 1.5 %collective-permute-start.2 = (bf16[64,1152]{1,0:T(8,128)(2,1)S(1)}, bf16[64,1152]{1,0:T(8,128)(2,1)S(1)}, u32[]{:S(2)}, u32[]{:S(2)}) collective-permute-start(bf16[64,1152]{1,0:T(8,128)(2,1)S(1)} %copy-done.5), channel_id=1, source_target_pairs={{0,24},{1,25},{8,0},{9,1},{16,8},{17,9},{24,16},{25,17},{32,56},{3... | collective-permute-start | bytes 442376 | tf_op jit(solution)/shard_map/ppermute | solution.py:33
  12.2 1.4 %collective-permute-start.3 = (bf16[64,1152]{1,0:T(8,128)(2,1)S(1)}, bf16[64,1152]{1,0:T(8,128)(2,1)S(1)}, u32[]{:S(2)}, u32[]{:S(2)}) collective-permute-start(bf16[64,1152]{1,0:T(8,128)(2,1)S(1)} %copy-done.5), channel_id=1, source_target_pairs={{0,16},{1,17},{8,24},{9,25},{16,0},{17,1},{24,8},{25,9},{32,48},{3... | collective-permute-start | bytes 442376 | tf_op jit(solution)/shard_map/ppermute | solution.py:33
  13.6 2.6 %collective-permute-done.4.refs_4_ = bf16[32,1152]{1,0:T(8,128)(2,1)S(1)} collective-permute-done((bf16[32,1152]{1,0:T(8,128)(2,1)S(1)}, bf16[32,1152]{1,0:T(8,128)(2,1)S(1)}, u32[]{:S(2)}, u32[]{:S(2)}) %collective-permute-start.4) | collective-permute-done | bytes 73760 | tf_op jit(solution)/shard_map/ppermute | solution.py:33
  16.3 2.6 %collective-permute-start.5 = (bf16[32,1152]{1,0:T(8,128)(2,1)S(1)}, bf16[32,1152]{1,0:T(8,128)(2,1)S(1)}, u32[]{:S(2)}, u32[]{:S(2)}) collective-permute-start(bf16[32,1152]{1,0:T(8,128)(2,1)S(1)} %copy-done.12), channel_id=1, source_target_pairs={{0,132},{1,133},{8,140},{9,141},{16,148},{17,149},{24,156},{25,157... | collective-permute-start | bytes 221192 | tf_op jit(solution)/shard_map/ppermute | solution.py:33
  18.9 2.6 %collective-permute-done.5.refs_5_ = bf16[32,1152]{1,0:T(8,128)(2,1)S(1)} collective-permute-done((bf16[32,1152]{1,0:T(8,128)(2,1)S(1)}, bf16[32,1152]{1,0:T(8,128)(2,1)S(1)}, u32[]{:S(2)}, u32[]{:S(2)}) %collective-permute-start.5) | collective-permute-done | bytes 73760 | tf_op jit(solution)/shard_map/ppermute | solution.py:33
  21.5 1.7 %join.1 = (bf16[256,1152]{1,0:T(8,128)(2,1)S(1)}, bf16[64,1152]{1,0:T(8,128)(2,1)}) custom-call(bf16[64,1152]{1,0:T(8,128)(2,1)S(1)} %copy-done.5, bf16[64,1152]{1,0:T(8,128)(2,1)S(1)} %collective-permute-done.1.refs_1_, bf16[64,1152]{1,0:T(8,128)(2,1)S(1)} %collective-permute-done.2.refs_2_, bf16[64,1152]{1,0:T(8,128)(2,1)S(1)} %collective-permute-done.3.refs_3_, ...), custom_call_target="tpu_custom_call" | custom-call | tf_op jit(solution)/shard_map/join/pallas_call | solution.py:102
  23.2 3.0 %collective-permute-start.6 = (bf16[256,1152]{1,0:T(8,128)(2,1)S(1)}, bf16[256,1152]{1,0:T(8,128)(2,1)S(1)}, u32[]{:S(2)}, u32[]{:S(2)}) collective-permute-start(bf16[256,1152]{1,0:T(8,128)(2,1)S(1)} %get-tuple-element.37.refs_3_), channel_id=1, source_target_pairs={{0,2},{1,3},{8,10},{9,11},{16,18},{17,19},{24,26},{25,27},{32,34},... | collective-permute-start | bytes 1769480 | tf_op jit(solution)/shard_map/ppermute | solution.py:33
  26.2 2.0 %collective-permute-start.7 = (bf16[256,1152]{1,0:T(8,128)(2,1)S(1)}, bf16[256,1152]{1,0:T(8,128)(2,1)}, u32[]{:S(2)}, u32[]{:S(2)}) collective-permute-start(bf16[256,1152]{1,0:T(8,128)(2,1)S(1)} %get-tuple-element.37.refs_3_), channel_id=1, source_target_pairs={{0,134},{1,135},{8,142},{9,143},{16,150},{17,151},{24,158},{25,159... | collective-permute-start | bytes 1769480 | tf_op jit(solution)/shard_map/ppermute | solution.py:33
  28.3 1.4 %collective-permute-start.10 = (bf16[64,1152]{1,0:T(8,128)(2,1)}, bf16[64,1152]{1,0:T(8,128)(2,1)S(1)}, u32[]{:S(2)}, u32[]{:S(2)}) collective-permute-start(bf16[64,1152]{1,0:T(8,128)(2,1)} %get-tuple-element.38.refs_6_), channel_id=1, source_target_pairs={{0,16},{1,17},{8,24},{9,25},{16,0},{17,1},{24,8},{25,9},{32,48},{3... | collective-permute-start | bytes 442376 | tf_op jit(solution)/shard_map/ppermute | solution.py:33
  29.7 2.1 %collective-permute-start.8 = (bf16[64,1152]{1,0:T(8,128)(2,1)}, bf16[64,1152]{1,0:T(8,128)(2,1)}, u32[]{:S(2)}, u32[]{:S(2)}) collective-permute-start(bf16[64,1152]{1,0:T(8,128)(2,1)} %get-tuple-element.38.refs_6_), channel_id=1, source_target_pairs={{0,8},{1,9},{8,16},{9,17},{16,24},{17,25},{24,0},{25,1},{32,40},{3... | collective-permute-start | bytes 442376 | tf_op jit(solution)/shard_map/ppermute | solution.py:33
  31.8 3.4 %collective-permute-done.10.refs_9_ = bf16[64,1152]{1,0:T(8,128)(2,1)S(1)} collective-permute-done((bf16[64,1152]{1,0:T(8,128)(2,1)}, bf16[64,1152]{1,0:T(8,128)(2,1)S(1)}, u32[]{:S(2)}, u32[]{:S(2)}) %collective-permute-start.10) | collective-permute-done | bytes 147488 | tf_op jit(solution)/shard_map/ppermute | solution.py:33
  35.8 1.6 %collective-permute-start.9 = (bf16[64,1152]{1,0:T(8,128)(2,1)}, bf16[64,1152]{1,0:T(8,128)(2,1)}, u32[]{:S(2)}, u32[]{:S(2)}) collective-permute-start(bf16[64,1152]{1,0:T(8,128)(2,1)} %get-tuple-element.38.refs_6_), channel_id=1, source_target_pairs={{0,24},{1,25},{8,0},{9,1},{16,8},{17,9},{24,16},{25,17},{32,56},{3... | collective-permute-start | bytes 442376 | tf_op jit(solution)/shard_map/ppermute | solution.py:33
  38.2 4.3 %collective-permute-done.9.refs_8_ = bf16[64,1152]{1,0:T(8,128)(2,1)} collective-permute-done((bf16[64,1152]{1,0:T(8,128)(2,1)}, bf16[64,1152]{1,0:T(8,128)(2,1)}, u32[]{:S(2)}, u32[]{:S(2)}) %collective-permute-start.9) | collective-permute-done | bytes 147488 | tf_op jit(solution)/shard_map/ppermute | solution.py:33
  42.5 0.9 copy-done.7
  43.4 9.2 %other_rows.1 = (f32[512,1152]{1,0:T(8,128)}, bf16[4,1024,256]{2,1,0:T(8,128)(2,1)S(1)}, bf16[1024,1152]{1,0:T(8,128)(2,1)}, bf16[1024,1152]{1,0:T(8,128)(2,1)}, f32[3,8,1024]{2,1,0:T(8,128)S(1)}) custom-call(f32[2]{0:T(128)S(1)} %pad_maximum_fusion.7.refs_0_, s32[6]{0:T(128)S(1)} %stack.32.refs_1_, bf16[512,1152]{1,0:T(8,128)(2,1)S(1)} %collective-permute-done.refs_2_, ...), custom_call_target="tpu_custom_call" | custom-call | flops 2415919104 | bytes 7077888 | tf_op jit(solution)/shard_map/other_rows/pallas_call | solution.py:196
  52.7 1.7 %copy-done = bf16[1024,1152]{1,0:T(8,128)(2,1)S(1)} copy-done((bf16[1024,1152]{1,0:T(8,128)(2,1)S(1)}, bf16[1024,1152]{1,0:T(8,128)(2,1)}, u32[]{:S(2)}) %copy-start) | copy-done | bytes 2359320
  54.3 5.9 %own_rows.1 = (f32[512,1152]{1,0:T(8,128)S(1)}, bf16[4,1024,256]{2,1,0:T(8,128)(2,1)S(1)}, bf16[1024,1152]{1,0:T(8,128)(2,1)S(1)}, f32[8,128]{1,0:T(8,128)S(1)}) custom-call(f32[2]{0:T(128)S(1)} %pad_maximum_fusion.7.refs_0_, s32[6]{0:T(128)S(1)} %stack.32.refs_1_, ...), custom_call_target="tpu_custom_call", output_to_operand_aliasing={{1}: (5, {}), {2}: (6, {})} | custom-call | flops 2415919104 | bytes 7077888 | tf_op jit(solution)/shard_map/own_rows/pallas_call | solution.py:213
  60.3 1.4 %copy-done.1 = bf16[1024,1152]{1,0:T(8,128)(2,1)} copy-done((bf16[1024,1152]{1,0:T(8,128)(2,1)}, bf16[1024,1152]{1,0:T(8,128)(2,1)S(1)}, u32[]{:S(2)}) %copy-start.1) | copy-done | bytes 2359320
  61.7 1.3 copy-done.3
  64.7 3.2 %collective-permute-done.13 = f32[4,128]{1,0:T(4,128)S(1)} collective-permute-done((f32[4,128]{1,0:T(4,128)S(1)}, f32[4,128]{1,0:T(4,128)S(1)}, u32[]{:S(2)}, u32[]{:S(2)}) %collective-permute-start.13) | collective-permute-done | bytes 2080 | tf_op jit(solution)/shard_map/ppermute | solution.py:265
  68.7 4.3 %collective-permute-done.14 = f32[4,128]{1,0:T(4,128)S(1)} collective-permute-done((f32[4,128]{1,0:T(4,128)S(1)}, f32[4,128]{1,0:T(4,128)S(1)}, u32[]{:S(2)}, u32[]{:S(2)}) %collective-permute-start.14) | collective-permute-done | bytes 2080 | tf_op jit(solution)/shard_map/ppermute | solution.py:265
  73.1 2.0 %fusion.3 = (f16[128,1152]{1,0:T(8,128)(2,1)S(1)}, f16[128,1152]{1,0:T(8,128)(2,1)S(1)}, f16[128,1152]{1,0:T(8,128)(2,1)S(1)}, f16[128,1152]{1,0:T(8,128)(2,1)S(1)}) fusion(f32[512,1152]{1,0:T(8,128)} %collective-permute-done.11, f32[512,1152]{1,0:T(8,128)S(1)} %get-tuple-element.45), kind=kLoop, calls=%fused_computation.15 | loop fusion | flops 1179648 | bytes 5898240 | tf_op jit(solution)/shard_map/convert_element_type | solution.py:260
  75.3 1.6 %collective-permute-start.15 = (f16[136,1152]{1,0:T(8,128)(2,1)S(1)}, f16[136,1152]{1,0:T(8,128)(2,1)S(1)}, u32[]{:S(2)}, u32[]{:S(2)}) collective-permute-start(f16[136,1152]{1,0:T(8,128)(2,1)S(1)} %get-tuple-element.79), channel_id=1, source_target_pairs={{0,32},{1,33},{8,40},{9,41},{16,48},{17,49},{24,56},{25,57},{32,64... | collective-permute-start | bytes 940040 | tf_op jit(solution)/shard_map/ppermute | solution.py:33
  77.0 1.7 %collective-permute-start.16 = (f16[136,1152]{1,0:T(8,128)(2,1)S(1)}, f16[136,1152]{1,0:T(8,128)(2,1)S(1)}, u32[]{:S(2)}, u32[]{:S(2)}) collective-permute-start(f16[136,1152]{1,0:T(8,128)(2,1)S(1)} %get-tuple-element.78), channel_id=1, source_target_pairs={{0,96},{1,97},{8,104},{9,105},{16,112},{17,113},{24,120},{25,121},... | collective-permute-start | bytes 940040 | tf_op jit(solution)/shard_map/ppermute | solution.py:33
  78.6 2.0 %collective-permute-start.17 = (f16[136,1152]{1,0:T(8,128)(2,1)S(1)}, f16[136,1152]{1,0:T(8,128)(2,1)S(1)}, u32[]{:S(2)}, u32[]{:S(2)}) collective-permute-start(f16[136,1152]{1,0:T(8,128)(2,1)S(1)} %get-tuple-element.77), channel_id=1, source_target_pairs={{0,64},{1,65},{8,72},{9,73},{16,80},{17,81},{24,88},{25,89},{32,96... | collective-permute-start | bytes 940040 | tf_op jit(solution)/shard_map/ppermute | solution.py:33
  81.5 0.9 convolution_convert_fusion.1
  82.3 3.5 %collective-permute-done.15 = f16[136,1152]{1,0:T(8,128)(2,1)S(1)} collective-permute-done((f16[136,1152]{1,0:T(8,128)(2,1)S(1)}, f16[136,1152]{1,0:T(8,128)(2,1)S(1)}, u32[]{:S(2)}, u32[]{:S(2)}) %collective-permute-start.15) | collective-permute-done | bytes 313376 | tf_op jit(solution)/shard_map/ppermute | solution.py:33
  85.8 4.3 %collective-permute-done.16 = f16[136,1152]{1,0:T(8,128)(2,1)S(1)} collective-permute-done((f16[136,1152]{1,0:T(8,128)(2,1)S(1)}, f16[136,1152]{1,0:T(8,128)(2,1)S(1)}, u32[]{:S(2)}, u32[]{:S(2)}) %collective-permute-start.16) | collective-permute-done | bytes 313376 | tf_op jit(solution)/shard_map/ppermute | solution.py:33
  90.1 1.8 %collective-permute-done.17 = f16[136,1152]{1,0:T(8,128)(2,1)S(1)} collective-permute-done((f16[136,1152]{1,0:T(8,128)(2,1)S(1)}, f16[136,1152]{1,0:T(8,128)(2,1)S(1)}, u32[]{:S(2)}, u32[]{:S(2)}) %collective-permute-start.17) | collective-permute-done | bytes 313376 | tf_op jit(solution)/shard_map/ppermute | solution.py:33
  92.2 5.0 %collective-permute-start.18 = (f16[136,1152]{1,0:T(8,128)(2,1)S(1)}, f16[136,1152]{1,0:T(8,128)(2,1)S(1)}, u32[]{:S(2)}, u32[]{:S(2)}) collective-permute-start(f16[136,1152]{1,0:T(8,128)(2,1)S(1)} %pad_maximum_fusion.3), channel_id=1, source_target_pairs={{0,128},{1,129},{8,136},{9,137},{16,144},{17,145},{24,152},{25,153... | collective-permute-start | bytes 940040 | tf_op jit(solution)/shard_map/ppermute | solution.py:33
  98.6 2.6 %collective-permute-start.20 = (f16[256,1152]{1,0:T(8,128)(2,1)S(1)}, f16[256,1152]{1,0:T(8,128)(2,1)S(1)}, u32[]{:S(2)}, u32[]{:S(2)}) collective-permute-start(f16[256,1152]{1,0:T(8,128)(2,1)S(1)} %convolution_convert_fusion.1), channel_id=1, source_target_pairs={{0,8},{1,9},{8,16},{9,17},{16,24},{17,25},{24,0},{25,1},{32,40},{3... | collective-permute-start | bytes 1769480 | tf_op jit(solution)/shard_map/ppermute | solution.py:33
  102.1 7.3 %collective-permute-done.18 = f16[136,1152]{1,0:T(8,128)(2,1)S(1)} collective-permute-done((f16[136,1152]{1,0:T(8,128)(2,1)S(1)}, f16[136,1152]{1,0:T(8,128)(2,1)S(1)}, u32[]{:S(2)}, u32[]{:S(2)}) %collective-permute-start.18) | collective-permute-done | bytes 313376 | tf_op jit(solution)/shard_map/ppermute | solution.py:33
  109.7 0.9 collective-permute-start.22
  110.6 2.4 %collective-permute-start.23 = (f16[128,1152]{1,0:T(8,128)(2,1)S(1)}, f16[128,1152]{1,0:T(8,128)(2,1)S(1)}, u32[]{:S(2)}, u32[]{:S(2)}) collective-permute-start(f16[128,1152]{1,0:T(8,128)(2,1)S(1)} %subtract_convert_fusion), channel_id=1, source_target_pairs={{0,96},{1,97},{8,104},{9,105},{16,112},{17,113},{24,120},{25,121},... | collective-permute-start | bytes 884744 | tf_op jit(solution)/shard_map/ppermute | solution.py:33
  113.2 2.7 %collective-permute-done.21 = f16[256,1152]{1,0:T(8,128)(2,1)S(1)} collective-permute-done((f16[256,1152]{1,0:T(8,128)(2,1)S(1)}, f16[256,1152]{1,0:T(8,128)(2,1)S(1)}, u32[]{:S(2)}, u32[]{:S(2)}) %collective-permute-start.21) | collective-permute-done | bytes 589856 | tf_op jit(solution)/shard_map/ppermute | solution.py:33
  116.7 5.2 %collective-permute-done.20 = f16[256,1152]{1,0:T(8,128)(2,1)S(1)} collective-permute-done((f16[256,1152]{1,0:T(8,128)(2,1)S(1)}, f16[256,1152]{1,0:T(8,128)(2,1)S(1)}, u32[]{:S(2)}, u32[]{:S(2)}) %collective-permute-start.20) | collective-permute-done | bytes 589856 | tf_op jit(solution)/shard_map/ppermute | solution.py:33
  121.9 2.5 %collective-permute-done.19 = f16[256,1152]{1,0:T(8,128)(2,1)S(1)} collective-permute-done((f16[256,1152]{1,0:T(8,128)(2,1)S(1)}, f16[256,1152]{1,0:T(8,128)(2,1)S(1)}, u32[]{:S(2)}, u32[]{:S(2)}) %collective-permute-start.19) | collective-permute-done | bytes 589856 | tf_op jit(solution)/shard_map/ppermute | solution.py:33
  124.4 0.9 collective-permute-done.22
  126.0 1.6 %collective-permute-start.25 = (f16[72,1152]{1,0:T(8,128)(2,1)S(1)}, f16[72,1152]{1,0:T(8,128)(2,1)S(1)}, u32[]{:S(2)}, u32[]{:S(2)}) collective-permute-start(f16[72,1152]{1,0:T(8,128)(2,1)S(1)} %get-tuple-element.76), channel_id=1, source_target_pairs={{0,134},{1,135},{8,142},{9,143},{16,150},{17,151},{24,158},{25,159... | collective-permute-start | bytes 497672 | tf_op jit(solution)/shard_map/ppermute | solution.py:33
  127.6 1.5 %collective-permute-start.26 = (f16[72,1152]{1,0:T(8,128)(2,1)S(1)}, f16[72,1152]{1,0:T(8,128)(2,1)S(1)}, u32[]{:S(2)}, u32[]{:S(2)}) collective-permute-start(f16[72,1152]{1,0:T(8,128)(2,1)S(1)} %get-tuple-element.75), channel_id=1, source_target_pairs={{0,2},{1,3},{8,10},{9,11},{16,18},{17,19},{24,26},{25,27},{32,34},... | collective-permute-start | bytes 497672 | tf_op jit(solution)/shard_map/ppermute | solution.py:33
  129.2 2.0 %collective-permute-start.28 = (f16[32,1152]{1,0:T(8,128)(2,1)S(1)}, f16[32,1152]{1,0:T(8,128)(2,1)S(1)}, u32[]{:S(2)}, u32[]{:S(2)}) collective-permute-start(f16[32,1152]{1,0:T(8,128)(2,1)S(1)} %get-tuple-element.71), channel_id=1, source_target_pairs={{0,4},{1,5},{8,12},{9,13},{16,20},{17,21},{24,28},{25,29},{32,36},... | collective-permute-start | bytes 221192 | tf_op jit(solution)/shard_map/ppermute | solution.py:33
  131.3 1.7 %convert_multiply_fusion = f32[512,1152]{1,0:T(8,128)} fusion(f16[512,1152]{1,0:T(8,128)(2,1)S(1)} %constant_dynamic-update-slice_fusion, f32[512]{0:T(512)S(1)} %get-tuple-element.80), kind=kLoop, calls=%fused_computation.4 | loop fusion | flops 1179648 | bytes 3540992 | tf_op jit(solution)/shard_map/mul | solution.py:299
  133.0 5.0 %collective-permute-done.28 = f16[32,1152]{1,0:T(8,128)(2,1)S(1)} collective-permute-done((f16[32,1152]{1,0:T(8,128)(2,1)S(1)}, f16[32,1152]{1,0:T(8,128)(2,1)S(1)}, u32[]{:S(2)}, u32[]{:S(2)}) %collective-permute-start.28) | collective-permute-done | bytes 73760 | tf_op jit(solution)/shard_map/ppermute | solution.py:33
  138.9 0.9 subtract_multiply_fusion
  (88 shorter events, 10.6 us)
Async XLA Ops:
  0.6 4.5 %copy-start.8 = (f32[512,1152]{1,0:T(8,128)S(1)}, f32[512,1152]{1,0:T(8,128)}, u32[]{:S(2)}) copy-start(f32[512,1152]{1,0:T(8,128)} %param.4) | copy-start | bytes 7077892
  5.2 1.7 %copy-start.13 = (bf16[32,1152]{1,0:T(8,128)(2,1)S(1)}, bf16[32,1152]{1,0:T(8,128)(2,1)}, u32[]{:S(2)}) copy-start(bf16[32,1152]{1,0:T(8,128)(2,1)} %get-tuple-element.35) | copy-start | bytes 221188
  5.2 5.0 %copy-start.5 = (bf16[64,1152]{1,0:T(8,128)(2,1)S(1)}, bf16[64,1152]{1,0:T(8,128)(2,1)}, u32[]{:S(2)}) copy-start(bf16[64,1152]{1,0:T(8,128)(2,1)} %get-tuple-element.34.refs_0_) | copy-start | bytes 442372
  5.2 11.1 %copy-start.12 = (bf16[32,1152]{1,0:T(8,128)(2,1)S(1)}, bf16[32,1152]{1,0:T(8,128)(2,1)}, u32[]{:S(2)}) copy-start(bf16[32,1152]{1,0:T(8,128)(2,1)} %get-tuple-element.36) | copy-start | bytes 221188
  6.9 35.5 %collective-permute-start = (bf16[512,1152]{1,0:T(8,128)(2,1)S(1)}, bf16[512,1152]{1,0:T(8,128)(2,1)S(1)}, u32[]{:S(2)}, u32[]{:S(2)}) collective-permute-start(bf16[512,1152]{1,0:T(8,128)(2,1)S(1)} %get-tuple-element.65.refs_2_), channel_id=1, source_target_pairs={{0,1},{1,0},{8,9},{9,8},{16,17},{17,16},{24,25},{25,24},{32,33},{3... | collective-permute-start | bytes 3538952 | tf_op jit(solution)/shard_map/ppermute | solution.py:33
  6.9 9.3 %collective-permute-start.4 = (bf16[32,1152]{1,0:T(8,128)(2,1)S(1)}, bf16[32,1152]{1,0:T(8,128)(2,1)S(1)}, u32[]{:S(2)}, u32[]{:S(2)}) collective-permute-start(bf16[32,1152]{1,0:T(8,128)(2,1)S(1)} %copy-done.13), channel_id=1, source_target_pairs={{0,4},{1,5},{8,12},{9,13},{16,20},{17,21},{24,28},{25,29},{32,36},... | collective-permute-start | bytes 221192 | tf_op jit(solution)/shard_map/ppermute | solution.py:33
  10.2 11.3 %collective-permute-start.1 = (bf16[64,1152]{1,0:T(8,128)(2,1)S(1)}, bf16[64,1152]{1,0:T(8,128)(2,1)S(1)}, u32[]{:S(2)}, u32[]{:S(2)}) collective-permute-start(bf16[64,1152]{1,0:T(8,128)(2,1)S(1)} %copy-done.5), channel_id=1, source_target_pairs={{0,8},{1,9},{8,16},{9,17},{16,24},{17,25},{24,0},{25,1},{32,40},{3... | collective-permute-start | bytes 442376 | tf_op jit(solution)/shard_map/ppermute | solution.py:33
  10.7 10.8 %collective-permute-start.2 = (bf16[64,1152]{1,0:T(8,128)(2,1)S(1)}, bf16[64,1152]{1,0:T(8,128)(2,1)S(1)}, u32[]{:S(2)}, u32[]{:S(2)}) collective-permute-start(bf16[64,1152]{1,0:T(8,128)(2,1)S(1)} %copy-done.5), channel_id=1, source_target_pairs={{0,24},{1,25},{8,0},{9,1},{16,8},{17,9},{24,16},{25,17},{32,56},{3... | collective-permute-start | bytes 442376 | tf_op jit(solution)/shard_map/ppermute | solution.py:33
  12.2 9.3 %collective-permute-start.3 = (bf16[64,1152]{1,0:T(8,128)(2,1)S(1)}, bf16[64,1152]{1,0:T(8,128)(2,1)S(1)}, u32[]{:S(2)}, u32[]{:S(2)}) collective-permute-start(bf16[64,1152]{1,0:T(8,128)(2,1)S(1)} %copy-done.5), channel_id=1, source_target_pairs={{0,16},{1,17},{8,24},{9,25},{16,0},{17,1},{24,8},{25,9},{32,48},{3... | collective-permute-start | bytes 442376 | tf_op jit(solution)/shard_map/ppermute | solution.py:33
  16.3 5.3 %collective-permute-start.5 = (bf16[32,1152]{1,0:T(8,128)(2,1)S(1)}, bf16[32,1152]{1,0:T(8,128)(2,1)S(1)}, u32[]{:S(2)}, u32[]{:S(2)}) collective-permute-start(bf16[32,1152]{1,0:T(8,128)(2,1)S(1)} %copy-done.12), channel_id=1, source_target_pairs={{0,132},{1,133},{8,140},{9,141},{16,148},{17,149},{24,156},{25,157... | collective-permute-start | bytes 221192 | tf_op jit(solution)/shard_map/ppermute | solution.py:33
  23.2 19.2 %collective-permute-start.6 = (bf16[256,1152]{1,0:T(8,128)(2,1)S(1)}, bf16[256,1152]{1,0:T(8,128)(2,1)S(1)}, u32[]{:S(2)}, u32[]{:S(2)}) collective-permute-start(bf16[256,1152]{1,0:T(8,128)(2,1)S(1)} %get-tuple-element.37.refs_3_), channel_id=1, source_target_pairs={{0,2},{1,3},{8,10},{9,11},{16,18},{17,19},{24,26},{25,27},{32,34},... | collective-permute-start | bytes 1769480 | tf_op jit(solution)/shard_map/ppermute | solution.py:33
  26.2 16.2 %collective-permute-start.7 = (bf16[256,1152]{1,0:T(8,128)(2,1)S(1)}, bf16[256,1152]{1,0:T(8,128)(2,1)}, u32[]{:S(2)}, u32[]{:S(2)}) collective-permute-start(bf16[256,1152]{1,0:T(8,128)(2,1)S(1)} %get-tuple-element.37.refs_3_), channel_id=1, source_target_pairs={{0,134},{1,135},{8,142},{9,143},{16,150},{17,151},{24,158},{25,159... | collective-permute-start | bytes 1769480 | tf_op jit(solution)/shard_map/ppermute | solution.py:33
  28.3 6.9 %collective-permute-start.10 = (bf16[64,1152]{1,0:T(8,128)(2,1)}, bf16[64,1152]{1,0:T(8,128)(2,1)S(1)}, u32[]{:S(2)}, u32[]{:S(2)}) collective-permute-start(bf16[64,1152]{1,0:T(8,128)(2,1)} %get-tuple-element.38.refs_6_), channel_id=1, source_target_pairs={{0,16},{1,17},{8,24},{9,25},{16,0},{17,1},{24,8},{25,9},{32,48},{3... | collective-permute-start | bytes 442376 | tf_op jit(solution)/shard_map/ppermute | solution.py:33
  29.7 8.5 %collective-permute-start.8 = (bf16[64,1152]{1,0:T(8,128)(2,1)}, bf16[64,1152]{1,0:T(8,128)(2,1)}, u32[]{:S(2)}, u32[]{:S(2)}) collective-permute-start(bf16[64,1152]{1,0:T(8,128)(2,1)} %get-tuple-element.38.refs_6_), channel_id=1, source_target_pairs={{0,8},{1,9},{8,16},{9,17},{16,24},{17,25},{24,0},{25,1},{32,40},{3... | collective-permute-start | bytes 442376 | tf_op jit(solution)/shard_map/ppermute | solution.py:33
  35.1 0.6 copy-start.6
  35.8 6.7 %collective-permute-start.9 = (bf16[64,1152]{1,0:T(8,128)(2,1)}, bf16[64,1152]{1,0:T(8,128)(2,1)}, u32[]{:S(2)}, u32[]{:S(2)}) collective-permute-start(bf16[64,1152]{1,0:T(8,128)(2,1)} %get-tuple-element.38.refs_6_), channel_id=1, source_target_pairs={{0,24},{1,25},{8,0},{9,1},{16,8},{17,9},{24,16},{25,17},{32,56},{3... | collective-permute-start | bytes 442376 | tf_op jit(solution)/shard_map/ppermute | solution.py:33
  42.5 0.9 copy-start.7
  52.6 20.5 %collective-permute-start.11 = (f32[512,1152]{1,0:T(8,128)}, f32[512,1152]{1,0:T(8,128)}, u32[]{:S(2)}, u32[]{:S(2)}) collective-permute-start(f32[512,1152]{1,0:T(8,128)} %get-tuple-element.46), channel_id=1, source_target_pairs={{0,1},{1,0},{8,9},{9,8},{16,17},{17,16},{24,25},{25,24},{32,33},{3... | collective-permute-start | bytes 7077896 | tf_op jit(solution)/shard_map/ppermute | solution.py:33
  52.7 1.7 %copy-start = (bf16[1024,1152]{1,0:T(8,128)(2,1)S(1)}, bf16[1024,1152]{1,0:T(8,128)(2,1)}, u32[]{:S(2)}) copy-start(bf16[1024,1152]{1,0:T(8,128)(2,1)} %get-tuple-element.42.refs_6_) | copy-start | bytes 7077892
  54.3 9.2 %copy-start.10 = (f32[64,1152]{1,0:T(8,128)S(1)}, f32[64,1152]{1,0:T(8,128)}, u32[]{:S(2)}) copy-start(f32[64,1152]{1,0:T(8,128)} %text_ref.1) | copy-start | bytes 884740
  60.3 1.4 %copy-start.1 = (bf16[1024,1152]{1,0:T(8,128)(2,1)}, bf16[1024,1152]{1,0:T(8,128)(2,1)S(1)}, u32[]{:S(2)}) copy-start(bf16[1024,1152]{1,0:T(8,128)(2,1)S(1)} %get-tuple-element.50) | copy-start | bytes 7077892
  61.7 1.3 copy-start.3
  63.0 1.3 collective-permute-start.12
  64.3 3.6 %collective-permute-start.13 = (f32[4,128]{1,0:T(4,128)S(1)}, f32[4,128]{1,0:T(4,128)S(1)}, u32[]{:S(2)}, u32[]{:S(2)}) collective-permute-start(f32[4,128]{1,0:T(4,128)S(1)} %slice_add_fusion.4), channel_id=1, source_target_pairs={{0,8},{1,9},{2,10},{3,11},{4,12},{5,13},{6,14},{7,15},{8,0},{9,1},... | collective-permute-start | bytes 6152 | tf_op jit(solution)/shard_map/ppermute | solution.py:265
  67.9 5.1 %collective-permute-start.14 = (f32[4,128]{1,0:T(4,128)S(1)}, f32[4,128]{1,0:T(4,128)S(1)}, u32[]{:S(2)}, u32[]{:S(2)}) collective-permute-start(f32[4,128]{1,0:T(4,128)S(1)} %add.191), channel_id=1, source_target_pairs={{0,16},{1,17},{2,18},{3,19},{4,20},{5,21},{6,22},{7,23},{8,24},{9,... | collective-permute-start | bytes 6152 | tf_op jit(solution)/shard_map/ppermute | solution.py:265
  73.1 7.5 %copy-start.2 = (bf16[1024,1152]{1,0:T(8,128)(2,1)S(1)}, bf16[1024,1152]{1,0:T(8,128)(2,1)}, u32[]{:S(2)}) copy-start(bf16[1024,1152]{1,0:T(8,128)(2,1)} %copy-done.1) | copy-start | bytes 7077892
  73.1 7.5 %copy-start.4 = (bf16[4,1024,256]{2,1,0:T(8,128)(2,1)S(1)}, bf16[4,1024,256]{2,1,0:T(8,128)(2,1)}, u32[]{:S(2)}) copy-start(bf16[4,1024,256]{2,1,0:T(8,128)(2,1)} %copy-done.3) | copy-start | bytes 6291460
  75.3 10.5 %collective-permute-start.15 = (f16[136,1152]{1,0:T(8,128)(2,1)S(1)}, f16[136,1152]{1,0:T(8,128)(2,1)S(1)}, u32[]{:S(2)}, u32[]{:S(2)}) collective-permute-start(f16[136,1152]{1,0:T(8,128)(2,1)S(1)} %get-tuple-element.79), channel_id=1, source_target_pairs={{0,32},{1,33},{8,40},{9,41},{16,48},{17,49},{24,56},{25,57},{32,64... | collective-permute-start | bytes 940040 | tf_op jit(solution)/shard_map/ppermute | solution.py:33
  77.0 13.1 %collective-permute-start.16 = (f16[136,1152]{1,0:T(8,128)(2,1)S(1)}, f16[136,1152]{1,0:T(8,128)(2,1)S(1)}, u32[]{:S(2)}, u32[]{:S(2)}) collective-permute-start(f16[136,1152]{1,0:T(8,128)(2,1)S(1)} %get-tuple-element.78), channel_id=1, source_target_pairs={{0,96},{1,97},{8,104},{9,105},{16,112},{17,113},{24,120},{25,121},... | collective-permute-start | bytes 940040 | tf_op jit(solution)/shard_map/ppermute | solution.py:33
  78.6 13.3 %collective-permute-start.17 = (f16[136,1152]{1,0:T(8,128)(2,1)S(1)}, f16[136,1152]{1,0:T(8,128)(2,1)S(1)}, u32[]{:S(2)}, u32[]{:S(2)}) collective-permute-start(f16[136,1152]{1,0:T(8,128)(2,1)S(1)} %get-tuple-element.77), channel_id=1, source_target_pairs={{0,64},{1,65},{8,72},{9,73},{16,80},{17,81},{24,88},{25,89},{32,96... | collective-permute-start | bytes 940040 | tf_op jit(solution)/shard_map/ppermute | solution.py:33
  92.2 17.1 %collective-permute-start.18 = (f16[136,1152]{1,0:T(8,128)(2,1)S(1)}, f16[136,1152]{1,0:T(8,128)(2,1)S(1)}, u32[]{:S(2)}, u32[]{:S(2)}) collective-permute-start(f16[136,1152]{1,0:T(8,128)(2,1)S(1)} %pad_maximum_fusion.3), channel_id=1, source_target_pairs={{0,128},{1,129},{8,136},{9,137},{16,144},{17,145},{24,152},{25,153... | collective-permute-start | bytes 940040 | tf_op jit(solution)/shard_map/ppermute | solution.py:33
  98.1 11.2 %copy-start.9 = (f32[512,1152]{1,0:T(8,128)S(1)}, f32[512,1152]{1,0:T(8,128)}, u32[]{:S(2)}) copy-start(f32[512,1152]{1,0:T(8,128)} %get-tuple-element.66) | copy-start | bytes 7077892
  98.1 17.9 %collective-permute-start.21 = (f16[256,1152]{1,0:T(8,128)(2,1)S(1)}, f16[256,1152]{1,0:T(8,128)(2,1)S(1)}, u32[]{:S(2)}, u32[]{:S(2)}) collective-permute-start(f16[256,1152]{1,0:T(8,128)(2,1)S(1)} %convolution_convert_fusion), channel_id=1, source_target_pairs={{0,16},{1,17},{8,24},{9,25},{16,0},{17,1},{24,8},{25,9},{32,48},{3... | collective-permute-start | bytes 1769480 | tf_op jit(solution)/shard_map/ppermute | solution.py:33
  98.6 23.3 %collective-permute-start.20 = (f16[256,1152]{1,0:T(8,128)(2,1)S(1)}, f16[256,1152]{1,0:T(8,128)(2,1)S(1)}, u32[]{:S(2)}, u32[]{:S(2)}) collective-permute-start(f16[256,1152]{1,0:T(8,128)(2,1)S(1)} %convolution_convert_fusion.1), channel_id=1, source_target_pairs={{0,8},{1,9},{8,16},{9,17},{16,24},{17,25},{24,0},{25,1},{32,40},{3... | collective-permute-start | bytes 1769480 | tf_op jit(solution)/shard_map/ppermute | solution.py:33
  101.2 23.2 %collective-permute-start.19 = (f16[256,1152]{1,0:T(8,128)(2,1)S(1)}, f16[256,1152]{1,0:T(8,128)(2,1)S(1)}, u32[]{:S(2)}, u32[]{:S(2)}) collective-permute-start(f16[256,1152]{1,0:T(8,128)(2,1)S(1)} %convolution_convert_fusion.2), channel_id=1, source_target_pairs={{0,24},{1,25},{8,0},{9,1},{16,8},{17,9},{24,16},{25,17},{32,56},{3... | collective-permute-start | bytes 1769480 | tf_op jit(solution)/shard_map/ppermute | solution.py:33
  109.7 15.7 %collective-permute-start.22 = (f16[128,1152]{1,0:T(8,128)(2,1)S(1)}, f16[128,1152]{1,0:T(8,128)(2,1)S(1)}, u32[]{:S(2)}, u32[]{:S(2)}) collective-permute-start(f16[128,1152]{1,0:T(8,128)(2,1)S(1)} %subtract_convert_fusion), channel_id=1, source_target_pairs={{0,32},{1,33},{8,40},{9,41},{16,48},{17,49},{24,56},{25,57},{32,64... | collective-permute-start | bytes 884744 | tf_op jit(solution)/shard_map/ppermute | solution.py:33
  110.6 18.5 %collective-permute-start.23 = (f16[128,1152]{1,0:T(8,128)(2,1)S(1)}, f16[128,1152]{1,0:T(8,128)(2,1)S(1)}, u32[]{:S(2)}, u32[]{:S(2)}) collective-permute-start(f16[128,1152]{1,0:T(8,128)(2,1)S(1)} %subtract_convert_fusion), channel_id=1, source_target_pairs={{0,96},{1,97},{8,104},{9,105},{16,112},{17,113},{24,120},{25,121},... | collective-permute-start | bytes 884744 | tf_op jit(solution)/shard_map/ppermute | solution.py:33
  116.0 15.3 %collective-permute-start.24 = (f16[128,1152]{1,0:T(8,128)(2,1)S(1)}, f16[128,1152]{1,0:T(8,128)(2,1)S(1)}, u32[]{:S(2)}, u32[]{:S(2)}) collective-permute-start(f16[128,1152]{1,0:T(8,128)(2,1)S(1)} %subtract_convert_fusion), channel_id=1, source_target_pairs={{0,64},{1,65},{8,72},{9,73},{16,80},{17,81},{24,88},{25,89},{32,96... | collective-permute-start | bytes 884744 | tf_op jit(solution)/shard_map/ppermute | solution.py:33
  125.8 12.1 %collective-permute-start.27 = (f16[40,1152]{1,0:T(8,128)(2,1)S(1)}, f16[40,1152]{1,0:T(8,128)(2,1)S(1)}, u32[]{:S(2)}, u32[]{:S(2)}) collective-permute-start(f16[40,1152]{1,0:T(8,128)(2,1)S(1)} %pad_maximum_fusion.6), channel_id=1, source_target_pairs={{0,132},{1,133},{8,140},{9,141},{16,148},{17,149},{24,156},{25,157... | collective-permute-start | bytes 276488 | tf_op jit(solution)/shard_map/ppermute | solution.py:33
  126.0 12.0 %collective-permute-start.25 = (f16[72,1152]{1,0:T(8,128)(2,1)S(1)}, f16[72,1152]{1,0:T(8,128)(2,1)S(1)}, u32[]{:S(2)}, u32[]{:S(2)}) collective-permute-start(f16[72,1152]{1,0:T(8,128)(2,1)S(1)} %get-tuple-element.76), channel_id=1, source_target_pairs={{0,134},{1,135},{8,142},{9,143},{16,150},{17,151},{24,158},{25,159... | collective-permute-start | bytes 497672 | tf_op jit(solution)/shard_map/ppermute | solution.py:33
  127.6 10.4 %collective-permute-start.26 = (f16[72,1152]{1,0:T(8,128)(2,1)S(1)}, f16[72,1152]{1,0:T(8,128)(2,1)S(1)}, u32[]{:S(2)}, u32[]{:S(2)}) collective-permute-start(f16[72,1152]{1,0:T(8,128)(2,1)S(1)} %get-tuple-element.75), channel_id=1, source_target_pairs={{0,2},{1,3},{8,10},{9,11},{16,18},{17,19},{24,26},{25,27},{32,34},... | collective-permute-start | bytes 497672 | tf_op jit(solution)/shard_map/ppermute | solution.py:33
  129.2 8.8 %collective-permute-start.28 = (f16[32,1152]{1,0:T(8,128)(2,1)S(1)}, f16[32,1152]{1,0:T(8,128)(2,1)S(1)}, u32[]{:S(2)}, u32[]{:S(2)}) collective-permute-start(f16[32,1152]{1,0:T(8,128)(2,1)S(1)} %get-tuple-element.71), channel_id=1, source_target_pairs={{0,4},{1,5},{8,12},{9,13},{16,20},{17,21},{24,28},{25,29},{32,36},... | collective-permute-start | bytes 221192 | tf_op jit(solution)/shard_map/ppermute | solution.py:33
  131.2 7.4 %copy-start.11 = (f32[64,1152]{1,0:T(8,128)S(1)}, f32[64,1152]{1,0:T(8,128)}, u32[]{:S(2)}) copy-start(f32[64,1152]{1,0:T(8,128)} %text_ref.1) | copy-start | bytes 884740

commit v4 on v3

--- a/solution.py
+++ b/solution.py
@@ -8,8 +8,8 @@
 AXES = ("group", "blk")
 SEND = jnp.float16
 STAT_SCALE = 2.0**-14
-VMEM_BYTES = 58 * 1024 * 1024
-PAIR_VMEM_BYTES = 44 * 1024 * 1024
+VMEM_BYTES = 28 * 1024 * 1024
+PAIR_VMEM_BYTES = 28 * 1024 * 1024
 SMEM = pl.BlockSpec(memory_space=pltpu.SMEM)
 HBM = pl.BlockSpec(memory_space=pltpu.HBM)
 

time: 140 us -> 138 us (0.986)
  Pallas kernels: 18.7 us -> 14.7 us
    pallas_call x1, Pallas kernels: 1.93 us -> 0.12 us  [text_messages(): pl.pallas_call(text_kernel, grid=(1,), in_specs=[pl.BlockSpec((n, width),...]
    unnamed x28 -> x22, local copies, waits for them, and re-layouts: 6.02 us -> 7.19 us
  transfers between devices with their start and end apart: 29 -> 29, of which waited for: 16 -> 17; matrix products, arithmetic and copies ran while one was open for 5% -> 5% of each run, Pallas kernels for 5% -> 4%
where the time goes in v4:
time: 138 us; the launch traced here: 137 us
  waiting for transfers between devices  52.9 us (38%)
  starting transfers between devices  44.8 us (32%)
  Pallas kernels  14.7 us (11%)
  other arithmetic  11.3 us (8%)
  local copies, waits for them, and re-layouts  7.85 us (6%)
  matrix products  3.51 us (3%)
  between operations  2.29 us (2%)
    ppermute x26, waiting for transfers between devices, move(): return lax.ppermute(value, AXES, shifted(**shift))  46 us
    ppermute x26, starting transfers between devices, move(): return lax.ppermute(value, AXES, shifted(**shift))  41.8 us
    pallas_call x1, Pallas kernels, pair_terms(): pl.pallas_call(lambda *refs: pair_kernel(0, *refs), grid=(1,), in_specs=[...  8.73 us
    unnamed x22, local copies, waits for them, and re-layouts  7.19 us
    ppermute x3, waiting for transfers between devices, per_device(): total += lax.ppermute(total, AXES, [(i, i ^ 1 << bit) for i in range(256)])  6.89 us
    pallas_call x1, Pallas kernels, pair_terms(): pl.pallas_call(lambda *refs: pair_kernel(1, *refs), grid=(1,), in_specs=[...  4.83 us
    dot_general x4, matrix products, per_device(): lax.dot_general(coef[k], copies, (((0,), (0,)), ((), ())), preferred_elem...  3.51 us
    ppermute x3, starting transfers between devices, per_device(): total += lax.ppermute(total, AXES, [(i, i ^ 1 << bit) for i in range(256)])  2.94 us
  transfers between devices with their start and end apart: 29, of which 17 were waited for; matrix products, arithmetic and copies ran while one was open for 5% of the time, Pallas kernels for 4%

profile of v4, /device:TPU:6, one launch (start us, length us, event | category | flops | bytes accessed | tf_op | source)
XLA Modules:
  0.0 137.3 jit_solution(10454682857917403139)
XLA Ops:
  0.6 1.0 copy-done
  1.7 2.0 %multiply_reduce_fusion = f32[512]{0:T(512)S(1)} fusion(f32[512,1152]{1,0:T(8,128)} %param.4), kind=kLoop, calls=%fused_computation.5 | loop fusion | flops 1179136 | bytes 2361344 | tf_op jit(solution)/shard_map/reduce_sum | solution.py:53
  4.5 1.7 %fusion.25 = (bf16[512,1152]{1,0:T(8,128)(2,1)S(1)}, f32[512,1152]{1,0:T(8,128)}) fusion(f32[512,1152]{1,0:T(8,128)S(1)} %copy-done.9, f32[512]{0:T(512)S(1)} %get-tuple-element.81), kind=kLoop, calls=%fused_computation.71 | loop fusion | flops 1179648 | bytes 5900288 | tf_op jit(solution)/shard_map/convert_element_type | solution.py:248
  6.2 1.1 copy-done.5
  7.2 3.3 %collective-permute-start.4 = (bf16[32,1152]{1,0:T(8,128)(2,1)S(1)}, bf16[32,1152]{1,0:T(8,128)(2,1)S(1)}, u32[]{:S(2)}, u32[]{:S(2)}) collective-permute-start(bf16[32,1152]{1,0:T(8,128)(2,1)S(1)} %get-tuple-element.35), channel_id=1, source_target_pairs={{0,4},{1,5},{8,12},{9,13},{16,20},{17,21},{24,28},{25,29},{32,36},... | collective-permute-start | bytes 221192 | tf_op jit(solution)/shard_map/ppermute | solution.py:33
  11.0 1.5 %collective-permute-start.2 = (bf16[64,1152]{1,0:T(8,128)(2,1)S(1)}, bf16[64,1152]{1,0:T(8,128)(2,1)S(1)}, u32[]{:S(2)}, u32[]{:S(2)}) collective-permute-start(bf16[64,1152]{1,0:T(8,128)(2,1)S(1)} %get-tuple-element.34.refs_0_), channel_id=1, source_target_pairs={{0,24},{1,25},{8,0},{9,1},{16,8},{17,9},{24,16},{25,17},{32,56},{3... | collective-permute-start | bytes 442376 | tf_op jit(solution)/shard_map/ppermute | solution.py:33
  12.5 1.4 %collective-permute-start.3 = (bf16[64,1152]{1,0:T(8,128)(2,1)S(1)}, bf16[64,1152]{1,0:T(8,128)(2,1)S(1)}, u32[]{:S(2)}, u32[]{:S(2)}) collective-permute-start(bf16[64,1152]{1,0:T(8,128)(2,1)S(1)} %get-tuple-element.34.refs_0_), channel_id=1, source_target_pairs={{0,16},{1,17},{8,24},{9,25},{16,0},{17,1},{24,8},{25,9},{32,48},{3... | collective-permute-start | bytes 442376 | tf_op jit(solution)/shard_map/ppermute | solution.py:33
  13.9 2.6 %collective-permute-done.4.refs_4_ = bf16[32,1152]{1,0:T(8,128)(2,1)S(1)} collective-permute-done((bf16[32,1152]{1,0:T(8,128)(2,1)S(1)}, bf16[32,1152]{1,0:T(8,128)(2,1)S(1)}, u32[]{:S(2)}, u32[]{:S(2)}) %collective-permute-start.4) | collective-permute-done | bytes 73760 | tf_op jit(solution)/shard_map/ppermute | solution.py:33
  16.6 2.6 %collective-permute-start.5 = (bf16[32,1152]{1,0:T(8,128)(2,1)S(1)}, bf16[32,1152]{1,0:T(8,128)(2,1)S(1)}, u32[]{:S(2)}, u32[]{:S(2)}) collective-permute-start(bf16[32,1152]{1,0:T(8,128)(2,1)S(1)} %get-tuple-element.36), channel_id=1, source_target_pairs={{0,132},{1,133},{8,140},{9,141},{16,148},{17,149},{24,156},{25,157... | collective-permute-start | bytes 221192 | tf_op jit(solution)/shard_map/ppermute | solution.py:33
  19.2 2.6 %collective-permute-done.5.refs_5_ = bf16[32,1152]{1,0:T(8,128)(2,1)S(1)} collective-permute-done((bf16[32,1152]{1,0:T(8,128)(2,1)S(1)}, bf16[32,1152]{1,0:T(8,128)(2,1)S(1)}, u32[]{:S(2)}, u32[]{:S(2)}) %collective-permute-start.5) | collective-permute-done | bytes 73760 | tf_op jit(solution)/shard_map/ppermute | solution.py:33
  21.8 1.0 join.1
  22.9 3.0 %collective-permute-start.6 = (bf16[256,1152]{1,0:T(8,128)(2,1)S(1)}, bf16[256,1152]{1,0:T(8,128)(2,1)}, u32[]{:S(2)}, u32[]{:S(2)}) collective-permute-start(bf16[256,1152]{1,0:T(8,128)(2,1)S(1)} %get-tuple-element.37.refs_3_), channel_id=1, source_target_pairs={{0,2},{1,3},{8,10},{9,11},{16,18},{17,19},{24,26},{25,27},{32,34},... | collective-permute-start | bytes 1769480 | tf_op jit(solution)/shard_map/ppermute | solution.py:33
  25.9 2.1 %collective-permute-start.7 = (bf16[256,1152]{1,0:T(8,128)(2,1)S(1)}, bf16[256,1152]{1,0:T(8,128)(2,1)}, u32[]{:S(2)}, u32[]{:S(2)}) collective-permute-start(bf16[256,1152]{1,0:T(8,128)(2,1)S(1)} %get-tuple-element.37.refs_3_), channel_id=1, source_target_pairs={{0,134},{1,135},{8,142},{9,143},{16,150},{17,151},{24,158},{25,159... | collective-permute-start | bytes 1769480 | tf_op jit(solution)/shard_map/ppermute | solution.py:33
  27.9 1.4 %collective-permute-start.10 = (bf16[64,1152]{1,0:T(8,128)(2,1)S(1)}, bf16[64,1152]{1,0:T(8,128)(2,1)S(1)}, u32[]{:S(2)}, u32[]{:S(2)}) collective-permute-start(bf16[64,1152]{1,0:T(8,128)(2,1)S(1)} %get-tuple-element.38.refs_6_), channel_id=1, source_target_pairs={{0,16},{1,17},{8,24},{9,25},{16,0},{17,1},{24,8},{25,9},{32,48},{3... | collective-permute-start | bytes 442376 | tf_op jit(solution)/shard_map/ppermute | solution.py:33
  29.3 2.1 %collective-permute-start.8 = (bf16[64,1152]{1,0:T(8,128)(2,1)S(1)}, bf16[64,1152]{1,0:T(8,128)(2,1)S(1)}, u32[]{:S(2)}, u32[]{:S(2)}) collective-permute-start(bf16[64,1152]{1,0:T(8,128)(2,1)S(1)} %get-tuple-element.38.refs_6_), channel_id=1, source_target_pairs={{0,8},{1,9},{8,16},{9,17},{16,24},{17,25},{24,0},{25,1},{32,40},{3... | collective-permute-start | bytes 442376 | tf_op jit(solution)/shard_map/ppermute | solution.py:33
  31.4 3.2 %collective-permute-done.10.refs_9_ = bf16[64,1152]{1,0:T(8,128)(2,1)S(1)} collective-permute-done((bf16[64,1152]{1,0:T(8,128)(2,1)S(1)}, bf16[64,1152]{1,0:T(8,128)(2,1)S(1)}, u32[]{:S(2)}, u32[]{:S(2)}) %collective-permute-start.10) | collective-permute-done | bytes 147488 | tf_op jit(solution)/shard_map/ppermute | solution.py:33
  34.6 1.5 %collective-permute-start.9 = (bf16[64,1152]{1,0:T(8,128)(2,1)S(1)}, bf16[64,1152]{1,0:T(8,128)(2,1)S(1)}, u32[]{:S(2)}, u32[]{:S(2)}) collective-permute-start(bf16[64,1152]{1,0:T(8,128)(2,1)S(1)} %get-tuple-element.38.refs_6_), channel_id=1, source_target_pairs={{0,24},{1,25},{8,0},{9,1},{16,8},{17,9},{24,16},{25,17},{32,56},{3... | collective-permute-start | bytes 442376 | tf_op jit(solution)/shard_map/ppermute | solution.py:33
  37.0 4.0 %collective-permute-done.9.refs_8_ = bf16[64,1152]{1,0:T(8,128)(2,1)S(1)} collective-permute-done((bf16[64,1152]{1,0:T(8,128)(2,1)S(1)}, bf16[64,1152]{1,0:T(8,128)(2,1)S(1)}, u32[]{:S(2)}, u32[]{:S(2)}) %collective-permute-start.9) | collective-permute-done | bytes 147488 | tf_op jit(solution)/shard_map/ppermute | solution.py:33
  41.3 1.0 copy-done.7
  42.3 1.3 copy-done.8
  43.6 8.7 %other_rows.1 = (f32[512,1152]{1,0:T(8,128)}, bf16[4,1024,256]{2,1,0:T(8,128)(2,1)S(1)}, bf16[1024,1152]{1,0:T(8,128)(2,1)S(1)}, bf16[1024,1152]{1,0:T(8,128)(2,1)S(1)}, f32[3,8,1024]{2,1,0:T(8,128)S(1)}) custom-call(f32[2]{0:T(128)S(1)} %pad_maximum_fusion.7.refs_0_, s32[6]{0:T(128)S(1)} %stack.32.refs_1_, bf16[512,1152]{1,0:T(8,128)(2,1)S(1)} %copy-done.8, ...), custom_call_target="tpu_custom_call" | custom-call | flops 2415919104 | bytes 7077888 | tf_op jit(solution)/shard_map/other_rows/pallas_call | solution.py:196
  52.5 4.8 %own_rows.1 = (f32[512,1152]{1,0:T(8,128)S(1)}, bf16[4,1024,256]{2,1,0:T(8,128)(2,1)S(1)}, bf16[1024,1152]{1,0:T(8,128)(2,1)S(1)}, f32[8,128]{1,0:T(8,128)S(1)}) custom-call(f32[2]{0:T(128)S(1)} %pad_maximum_fusion.7.refs_0_, s32[6]{0:T(128)S(1)} %stack.32.refs_1_, bf16[512,1152]{1,0:T(8,128)(2,1)S(1)} %copy-done.6, ...), custom_call_target="tpu_custom_call", output_to_operand_aliasing={{1}: (5, {}), {2}: (6, {})} | custom-call | flops 2415919104 | bytes 7077888 | tf_op jit(solution)/shard_map/own_rows/pallas_call | solution.py:213
  57.3 1.4 %copy-done.2 = f32[512,1152]{1,0:T(8,128)} copy-done((f32[512,1152]{1,0:T(8,128)}, f32[512,1152]{1,0:T(8,128)S(1)}, u32[]{:S(2)}) %copy-start.2) | copy-done | bytes 2359320
  58.7 1.4 %copy-done.3 = bf16[4,1024,256]{2,1,0:T(8,128)(2,1)} copy-done((bf16[4,1024,256]{2,1,0:T(8,128)(2,1)}, bf16[4,1024,256]{2,1,0:T(8,128)(2,1)S(1)}, u32[]{:S(2)}) %copy-start.3) | copy-done | bytes 2097176
  62.3 2.7 %collective-permute-done.13 = f32[4,128]{1,0:T(4,128)S(1)} collective-permute-done((f32[4,128]{1,0:T(4,128)S(1)}, f32[4,128]{1,0:T(4,128)S(1)}, u32[]{:S(2)}, u32[]{:S(2)}) %collective-permute-start.13) | collective-permute-done | bytes 2080 | tf_op jit(solution)/shard_map/ppermute | solution.py:265
  65.0 1.6 %collective-permute-start.14 = (f32[4,128]{1,0:T(4,128)S(1)}, f32[4,128]{1,0:T(4,128)S(1)}, u32[]{:S(2)}, u32[]{:S(2)}) collective-permute-start(f32[4,128]{1,0:T(4,128)S(1)} %add.191), channel_id=1, source_target_pairs={{0,16},{1,17},{2,18},{3,19},{4,20},{5,21},{6,22},{7,23},{8,24},{9,... | collective-permute-start | bytes 6152 | tf_op jit(solution)/shard_map/ppermute | solution.py:265
  66.7 3.4 %collective-permute-done.14 = f32[4,128]{1,0:T(4,128)S(1)} collective-permute-done((f32[4,128]{1,0:T(4,128)S(1)}, f32[4,128]{1,0:T(4,128)S(1)}, u32[]{:S(2)}, u32[]{:S(2)}) %collective-permute-start.14) | collective-permute-done | bytes 2080 | tf_op jit(solution)/shard_map/ppermute | solution.py:265
  70.2 2.7 %fusion.3 = (f16[128,1152]{1,0:T(8,128)(2,1)S(1)}, f16[128,1152]{1,0:T(8,128)(2,1)S(1)}, f16[128,1152]{1,0:T(8,128)(2,1)S(1)}, f16[128,1152]{1,0:T(8,128)(2,1)S(1)}) fusion(f32[512,1152]{1,0:T(8,128)} %collective-permute-done.11, f32[512,1152]{1,0:T(8,128)} %copy-done.2), kind=kLoop, calls=%fused_computation.15 | loop fusion | flops 1179648 | bytes 5898240 | tf_op jit(solution)/shard_map/convert_element_type | solution.py:260
  73.1 1.7 %collective-permute-start.15 = (f16[136,1152]{1,0:T(8,128)(2,1)S(1)}, f16[136,1152]{1,0:T(8,128)(2,1)S(1)}, u32[]{:S(2)}, u32[]{:S(2)}) collective-permute-start(f16[136,1152]{1,0:T(8,128)(2,1)S(1)} %get-tuple-element.79), channel_id=1, source_target_pairs={{0,32},{1,33},{8,40},{9,41},{16,48},{17,49},{24,56},{25,57},{32,64... | collective-permute-start | bytes 940040 | tf_op jit(solution)/shard_map/ppermute | solution.py:33
  74.8 1.7 %collective-permute-start.16 = (f16[136,1152]{1,0:T(8,128)(2,1)S(1)}, f16[136,1152]{1,0:T(8,128)(2,1)S(1)}, u32[]{:S(2)}, u32[]{:S(2)}) collective-permute-start(f16[136,1152]{1,0:T(8,128)(2,1)S(1)} %get-tuple-element.78), channel_id=1, source_target_pairs={{0,96},{1,97},{8,104},{9,105},{16,112},{17,113},{24,120},{25,121},... | collective-permute-start | bytes 940040 | tf_op jit(solution)/shard_map/ppermute | solution.py:33
  76.4 2.0 %collective-permute-start.17 = (f16[136,1152]{1,0:T(8,128)(2,1)S(1)}, f16[136,1152]{1,0:T(8,128)(2,1)S(1)}, u32[]{:S(2)}, u32[]{:S(2)}) collective-permute-start(f16[136,1152]{1,0:T(8,128)(2,1)S(1)} %get-tuple-element.77), channel_id=1, source_target_pairs={{0,64},{1,65},{8,72},{9,73},{16,80},{17,81},{24,88},{25,89},{32,96... | collective-permute-start | bytes 940040 | tf_op jit(solution)/shard_map/ppermute | solution.py:33
  79.3 0.9 convolution_convert_fusion.1
  80.2 3.4 %collective-permute-done.15 = f16[136,1152]{1,0:T(8,128)(2,1)S(1)} collective-permute-done((f16[136,1152]{1,0:T(8,128)(2,1)S(1)}, f16[136,1152]{1,0:T(8,128)(2,1)S(1)}, u32[]{:S(2)}, u32[]{:S(2)}) %collective-permute-start.15) | collective-permute-done | bytes 313376 | tf_op jit(solution)/shard_map/ppermute | solution.py:33
  83.6 4.3 %collective-permute-done.16 = f16[136,1152]{1,0:T(8,128)(2,1)S(1)} collective-permute-done((f16[136,1152]{1,0:T(8,128)(2,1)S(1)}, f16[136,1152]{1,0:T(8,128)(2,1)S(1)}, u32[]{:S(2)}, u32[]{:S(2)}) %collective-permute-start.16) | collective-permute-done | bytes 313376 | tf_op jit(solution)/shard_map/ppermute | solution.py:33
  87.9 1.8 %collective-permute-done.17 = f16[136,1152]{1,0:T(8,128)(2,1)S(1)} collective-permute-done((f16[136,1152]{1,0:T(8,128)(2,1)S(1)}, f16[136,1152]{1,0:T(8,128)(2,1)S(1)}, u32[]{:S(2)}, u32[]{:S(2)}) %collective-permute-start.17) | collective-permute-done | bytes 313376 | tf_op jit(solution)/shard_map/ppermute | solution.py:33
  90.0 4.7 %collective-permute-start.18 = (f16[136,1152]{1,0:T(8,128)(2,1)S(1)}, f16[136,1152]{1,0:T(8,128)(2,1)S(1)}, u32[]{:S(2)}, u32[]{:S(2)}) collective-permute-start(f16[136,1152]{1,0:T(8,128)(2,1)S(1)} %pad_maximum_fusion.3), channel_id=1, source_target_pairs={{0,128},{1,129},{8,136},{9,137},{16,144},{17,145},{24,152},{25,153... | collective-permute-start | bytes 940040 | tf_op jit(solution)/shard_map/ppermute | solution.py:33
  96.3 2.4 %collective-permute-start.20 = (f16[256,1152]{1,0:T(8,128)(2,1)S(1)}, f16[256,1152]{1,0:T(8,128)(2,1)S(1)}, u32[]{:S(2)}, u32[]{:S(2)}) collective-permute-start(f16[256,1152]{1,0:T(8,128)(2,1)S(1)} %convolution_convert_fusion.1), channel_id=1, source_target_pairs={{0,8},{1,9},{8,16},{9,17},{16,24},{17,25},{24,0},{25,1},{32,40},{3... | collective-permute-start | bytes 1769480 | tf_op jit(solution)/shard_map/ppermute | solution.py:33
  99.6 7.6 %collective-permute-done.18 = f16[136,1152]{1,0:T(8,128)(2,1)S(1)} collective-permute-done((f16[136,1152]{1,0:T(8,128)(2,1)S(1)}, f16[136,1152]{1,0:T(8,128)(2,1)S(1)}, u32[]{:S(2)}, u32[]{:S(2)}) %collective-permute-start.18) | collective-permute-done | bytes 313376 | tf_op jit(solution)/shard_map/ppermute | solution.py:33
  107.5 0.9 collective-permute-start.22
  108.5 2.4 %collective-permute-start.23 = (f16[128,1152]{1,0:T(8,128)(2,1)S(1)}, f16[128,1152]{1,0:T(8,128)(2,1)S(1)}, u32[]{:S(2)}, u32[]{:S(2)}) collective-permute-start(f16[128,1152]{1,0:T(8,128)(2,1)S(1)} %subtract_convert_fusion), channel_id=1, source_target_pairs={{0,96},{1,97},{8,104},{9,105},{16,112},{17,113},{24,120},{25,121},... | collective-permute-start | bytes 884744 | tf_op jit(solution)/shard_map/ppermute | solution.py:33
  111.1 2.4 %collective-permute-done.21 = f16[256,1152]{1,0:T(8,128)(2,1)S(1)} collective-permute-done((f16[256,1152]{1,0:T(8,128)(2,1)S(1)}, f16[256,1152]{1,0:T(8,128)(2,1)S(1)}, u32[]{:S(2)}, u32[]{:S(2)}) %collective-permute-start.21) | collective-permute-done | bytes 589856 | tf_op jit(solution)/shard_map/ppermute | solution.py:33
  114.2 5.1 %collective-permute-done.20 = f16[256,1152]{1,0:T(8,128)(2,1)S(1)} collective-permute-done((f16[256,1152]{1,0:T(8,128)(2,1)S(1)}, f16[256,1152]{1,0:T(8,128)(2,1)S(1)}, u32[]{:S(2)}, u32[]{:S(2)}) %collective-permute-start.20) | collective-permute-done | bytes 589856 | tf_op jit(solution)/shard_map/ppermute | solution.py:33
  119.4 2.6 %collective-permute-done.19 = f16[256,1152]{1,0:T(8,128)(2,1)S(1)} collective-permute-done((f16[256,1152]{1,0:T(8,128)(2,1)S(1)}, f16[256,1152]{1,0:T(8,128)(2,1)S(1)}, u32[]{:S(2)}, u32[]{:S(2)}) %collective-permute-start.19) | collective-permute-done | bytes 589856 | tf_op jit(solution)/shard_map/ppermute | solution.py:33
  123.4 1.4 collective-permute-start.25
  124.8 1.5 %collective-permute-start.26 = (f16[72,1152]{1,0:T(8,128)(2,1)S(1)}, f16[72,1152]{1,0:T(8,128)(2,1)S(1)}, u32[]{:S(2)}, u32[]{:S(2)}) collective-permute-start(f16[72,1152]{1,0:T(8,128)(2,1)S(1)} %get-tuple-element.75), channel_id=1, source_target_pairs={{0,2},{1,3},{8,10},{9,11},{16,18},{17,19},{24,26},{25,27},{32,34},... | collective-permute-start | bytes 497672 | tf_op jit(solution)/shard_map/ppermute | solution.py:33
  126.4 2.2 %collective-permute-start.28 = (f16[32,1152]{1,0:T(8,128)(2,1)S(1)}, f16[32,1152]{1,0:T(8,128)(2,1)S(1)}, u32[]{:S(2)}, u32[]{:S(2)}) collective-permute-start(f16[32,1152]{1,0:T(8,128)(2,1)S(1)} %get-tuple-element.71), channel_id=1, source_target_pairs={{0,4},{1,5},{8,12},{9,13},{16,20},{17,21},{24,28},{25,29},{32,36},... | collective-permute-start | bytes 221192 | tf_op jit(solution)/shard_map/ppermute | solution.py:33
  128.7 1.7 %convert_multiply_fusion = f32[512,1152]{1,0:T(8,128)} fusion(f16[512,1152]{1,0:T(8,128)(2,1)S(1)} %constant_dynamic-update-slice_fusion, f32[512]{0:T(512)S(1)} %get-tuple-element.80), kind=kLoop, calls=%fused_computation.4 | loop fusion | flops 1179648 | bytes 3540992 | tf_op jit(solution)/shard_map/mul | solution.py:299
  130.4 5.2 %collective-permute-done.28 = f16[32,1152]{1,0:T(8,128)(2,1)S(1)} collective-permute-done((f16[32,1152]{1,0:T(8,128)(2,1)S(1)}, f16[32,1152]{1,0:T(8,128)(2,1)S(1)}, u32[]{:S(2)}, u32[]{:S(2)}) %collective-permute-start.28) | collective-permute-done | bytes 73760 | tf_op jit(solution)/shard_map/ppermute | solution.py:33
  (82 shorter events, 11.9 us)
Async XLA Ops:
  0.6 1.0 copy-start
  1.6 2.9 %copy-start.9 = (f32[512,1152]{1,0:T(8,128)S(1)}, f32[512,1152]{1,0:T(8,128)}, u32[]{:S(2)}) copy-start(f32[512,1152]{1,0:T(8,128)} %param.4) | copy-start | bytes 7077892
  6.2 35.1 %collective-permute-start = (bf16[512,1152]{1,0:T(8,128)(2,1)S(1)}, bf16[512,1152]{1,0:T(8,128)(2,1)S(1)}, u32[]{:S(2)}, u32[]{:S(2)}) collective-permute-start(bf16[512,1152]{1,0:T(8,128)(2,1)S(1)} %get-tuple-element.65.refs_2_), channel_id=1, source_target_pairs={{0,1},{1,0},{8,9},{9,8},{16,17},{17,16},{24,25},{25,24},{32,33},{3... | collective-permute-start | bytes 3538952 | tf_op jit(solution)/shard_map/ppermute | solution.py:33
  6.2 1.1 copy-start.5
  7.2 9.3 %collective-permute-start.4 = (bf16[32,1152]{1,0:T(8,128)(2,1)S(1)}, bf16[32,1152]{1,0:T(8,128)(2,1)S(1)}, u32[]{:S(2)}, u32[]{:S(2)}) collective-permute-start(bf16[32,1152]{1,0:T(8,128)(2,1)S(1)} %get-tuple-element.35), channel_id=1, source_target_pairs={{0,4},{1,5},{8,12},{9,13},{16,20},{17,21},{24,28},{25,29},{32,36},... | collective-permute-start | bytes 221192 | tf_op jit(solution)/shard_map/ppermute | solution.py:33
  10.5 11.3 %collective-permute-start.1 = (bf16[64,1152]{1,0:T(8,128)(2,1)S(1)}, bf16[64,1152]{1,0:T(8,128)(2,1)S(1)}, u32[]{:S(2)}, u32[]{:S(2)}) collective-permute-start(bf16[64,1152]{1,0:T(8,128)(2,1)S(1)} %get-tuple-element.34.refs_0_), channel_id=1, source_target_pairs={{0,8},{1,9},{8,16},{9,17},{16,24},{17,25},{24,0},{25,1},{32,40},{3... | collective-permute-start | bytes 442376 | tf_op jit(solution)/shard_map/ppermute | solution.py:33
  11.0 10.8 %collective-permute-start.2 = (bf16[64,1152]{1,0:T(8,128)(2,1)S(1)}, bf16[64,1152]{1,0:T(8,128)(2,1)S(1)}, u32[]{:S(2)}, u32[]{:S(2)}) collective-permute-start(bf16[64,1152]{1,0:T(8,128)(2,1)S(1)} %get-tuple-element.34.refs_0_), channel_id=1, source_target_pairs={{0,24},{1,25},{8,0},{9,1},{16,8},{17,9},{24,16},{25,17},{32,56},{3... | collective-permute-start | bytes 442376 | tf_op jit(solution)/shard_map/ppermute | solution.py:33
  12.5 9.3 %collective-permute-start.3 = (bf16[64,1152]{1,0:T(8,128)(2,1)S(1)}, bf16[64,1152]{1,0:T(8,128)(2,1)S(1)}, u32[]{:S(2)}, u32[]{:S(2)}) collective-permute-start(bf16[64,1152]{1,0:T(8,128)(2,1)S(1)} %get-tuple-element.34.refs_0_), channel_id=1, source_target_pairs={{0,16},{1,17},{8,24},{9,25},{16,0},{17,1},{24,8},{25,9},{32,48},{3... | collective-permute-start | bytes 442376 | tf_op jit(solution)/shard_map/ppermute | solution.py:33
  16.6 5.3 %collective-permute-start.5 = (bf16[32,1152]{1,0:T(8,128)(2,1)S(1)}, bf16[32,1152]{1,0:T(8,128)(2,1)S(1)}, u32[]{:S(2)}, u32[]{:S(2)}) collective-permute-start(bf16[32,1152]{1,0:T(8,128)(2,1)S(1)} %get-tuple-element.36), channel_id=1, source_target_pairs={{0,132},{1,133},{8,140},{9,141},{16,148},{17,149},{24,156},{25,157... | collective-permute-start | bytes 221192 | tf_op jit(solution)/shard_map/ppermute | solution.py:33
  22.9 18.1 %collective-permute-start.6 = (bf16[256,1152]{1,0:T(8,128)(2,1)S(1)}, bf16[256,1152]{1,0:T(8,128)(2,1)}, u32[]{:S(2)}, u32[]{:S(2)}) collective-permute-start(bf16[256,1152]{1,0:T(8,128)(2,1)S(1)} %get-tuple-element.37.refs_3_), channel_id=1, source_target_pairs={{0,2},{1,3},{8,10},{9,11},{16,18},{17,19},{24,26},{25,27},{32,34},... | collective-permute-start | bytes 1769480 | tf_op jit(solution)/shard_map/ppermute | solution.py:33
  25.9 15.4 %collective-permute-start.7 = (bf16[256,1152]{1,0:T(8,128)(2,1)S(1)}, bf16[256,1152]{1,0:T(8,128)(2,1)}, u32[]{:S(2)}, u32[]{:S(2)}) collective-permute-start(bf16[256,1152]{1,0:T(8,128)(2,1)S(1)} %get-tuple-element.37.refs_3_), channel_id=1, source_target_pairs={{0,134},{1,135},{8,142},{9,143},{16,150},{17,151},{24,158},{25,159... | collective-permute-start | bytes 1769480 | tf_op jit(solution)/shard_map/ppermute | solution.py:33
  27.9 6.7 %collective-permute-start.10 = (bf16[64,1152]{1,0:T(8,128)(2,1)S(1)}, bf16[64,1152]{1,0:T(8,128)(2,1)S(1)}, u32[]{:S(2)}, u32[]{:S(2)}) collective-permute-start(bf16[64,1152]{1,0:T(8,128)(2,1)S(1)} %get-tuple-element.38.refs_6_), channel_id=1, source_target_pairs={{0,16},{1,17},{8,24},{9,25},{16,0},{17,1},{24,8},{25,9},{32,48},{3... | collective-permute-start | bytes 442376 | tf_op jit(solution)/shard_map/ppermute | solution.py:33
  29.3 7.6 %collective-permute-start.8 = (bf16[64,1152]{1,0:T(8,128)(2,1)S(1)}, bf16[64,1152]{1,0:T(8,128)(2,1)S(1)}, u32[]{:S(2)}, u32[]{:S(2)}) collective-permute-start(bf16[64,1152]{1,0:T(8,128)(2,1)S(1)} %get-tuple-element.38.refs_6_), channel_id=1, source_target_pairs={{0,8},{1,9},{8,16},{9,17},{16,24},{17,25},{24,0},{25,1},{32,40},{3... | collective-permute-start | bytes 442376 | tf_op jit(solution)/shard_map/ppermute | solution.py:33
  34.6 6.4 %collective-permute-start.9 = (bf16[64,1152]{1,0:T(8,128)(2,1)S(1)}, bf16[64,1152]{1,0:T(8,128)(2,1)S(1)}, u32[]{:S(2)}, u32[]{:S(2)}) collective-permute-start(bf16[64,1152]{1,0:T(8,128)(2,1)S(1)} %get-tuple-element.38.refs_6_), channel_id=1, source_target_pairs={{0,24},{1,25},{8,0},{9,1},{16,8},{17,9},{24,16},{25,17},{32,56},{3... | collective-permute-start | bytes 442376 | tf_op jit(solution)/shard_map/ppermute | solution.py:33
  37.0 15.5 %copy-start.6 = (bf16[512,1152]{1,0:T(8,128)(2,1)S(1)}, bf16[512,1152]{1,0:T(8,128)(2,1)}, u32[]{:S(2)}) copy-start(bf16[512,1152]{1,0:T(8,128)(2,1)} %copy-done.5) | copy-start | bytes 3538948
  41.3 1.0 copy-start.7
  42.3 1.3 copy-start.8
  52.3 17.8 %collective-permute-start.11 = (f32[512,1152]{1,0:T(8,128)}, f32[512,1152]{1,0:T(8,128)}, u32[]{:S(2)}, u32[]{:S(2)}) collective-permute-start(f32[512,1152]{1,0:T(8,128)} %get-tuple-element.46), channel_id=1, source_target_pairs={{0,1},{1,0},{8,9},{9,8},{16,17},{17,16},{24,25},{25,24},{32,33},{3... | collective-permute-start | bytes 7077896 | tf_op jit(solution)/shard_map/ppermute | solution.py:33
  52.5 8.2 %copy-start.1 = (f32[64,1152]{1,0:T(8,128)S(1)}, f32[64,1152]{1,0:T(8,128)}, u32[]{:S(2)}) copy-start(f32[64,1152]{1,0:T(8,128)} %text_ref.1) | copy-start | bytes 884740
  57.3 1.4 %copy-start.2 = (f32[512,1152]{1,0:T(8,128)}, f32[512,1152]{1,0:T(8,128)S(1)}, u32[]{:S(2)}) copy-start(f32[512,1152]{1,0:T(8,128)S(1)} %get-tuple-element.45) | copy-start | bytes 7077892
  58.7 1.4 %copy-start.3 = (bf16[4,1024,256]{2,1,0:T(8,128)(2,1)}, bf16[4,1024,256]{2,1,0:T(8,128)(2,1)S(1)}, u32[]{:S(2)}) copy-start(bf16[4,1024,256]{2,1,0:T(8,128)(2,1)S(1)} %get-tuple-element.49) | copy-start | bytes 6291460
  60.1 1.3 collective-permute-start.12
  61.4 3.6 %collective-permute-start.13 = (f32[4,128]{1,0:T(4,128)S(1)}, f32[4,128]{1,0:T(4,128)S(1)}, u32[]{:S(2)}, u32[]{:S(2)}) collective-permute-start(f32[4,128]{1,0:T(4,128)S(1)} %slice_add_fusion.4), channel_id=1, source_target_pairs={{0,8},{1,9},{2,10},{3,11},{4,12},{5,13},{6,14},{7,15},{8,0},{9,1},... | collective-permute-start | bytes 6152 | tf_op jit(solution)/shard_map/ppermute | solution.py:265
  65.0 5.1 %collective-permute-start.14 = (f32[4,128]{1,0:T(4,128)S(1)}, f32[4,128]{1,0:T(4,128)S(1)}, u32[]{:S(2)}, u32[]{:S(2)}) collective-permute-start(f32[4,128]{1,0:T(4,128)S(1)} %add.191), channel_id=1, source_target_pairs={{0,16},{1,17},{2,18},{3,19},{4,20},{5,21},{6,22},{7,23},{8,24},{9,... | collective-permute-start | bytes 6152 | tf_op jit(solution)/shard_map/ppermute | solution.py:265
  70.2 8.2 %copy-start.4 = (bf16[4,1024,256]{2,1,0:T(8,128)(2,1)S(1)}, bf16[4,1024,256]{2,1,0:T(8,128)(2,1)}, u32[]{:S(2)}) copy-start(bf16[4,1024,256]{2,1,0:T(8,128)(2,1)} %copy-done.3) | copy-start | bytes 6291460
  73.1 10.5 %collective-permute-start.15 = (f16[136,1152]{1,0:T(8,128)(2,1)S(1)}, f16[136,1152]{1,0:T(8,128)(2,1)S(1)}, u32[]{:S(2)}, u32[]{:S(2)}) collective-permute-start(f16[136,1152]{1,0:T(8,128)(2,1)S(1)} %get-tuple-element.79), channel_id=1, source_target_pairs={{0,32},{1,33},{8,40},{9,41},{16,48},{17,49},{24,56},{25,57},{32,64... | collective-permute-start | bytes 940040 | tf_op jit(solution)/shard_map/ppermute | solution.py:33
  74.8 13.1 %collective-permute-start.16 = (f16[136,1152]{1,0:T(8,128)(2,1)S(1)}, f16[136,1152]{1,0:T(8,128)(2,1)S(1)}, u32[]{:S(2)}, u32[]{:S(2)}) collective-permute-start(f16[136,1152]{1,0:T(8,128)(2,1)S(1)} %get-tuple-element.78), channel_id=1, source_target_pairs={{0,96},{1,97},{8,104},{9,105},{16,112},{17,113},{24,120},{25,121},... | collective-permute-start | bytes 940040 | tf_op jit(solution)/shard_map/ppermute | solution.py:33
  76.4 13.3 %collective-permute-start.17 = (f16[136,1152]{1,0:T(8,128)(2,1)S(1)}, f16[136,1152]{1,0:T(8,128)(2,1)S(1)}, u32[]{:S(2)}, u32[]{:S(2)}) collective-permute-start(f16[136,1152]{1,0:T(8,128)(2,1)S(1)} %get-tuple-element.77), channel_id=1, source_target_pairs={{0,64},{1,65},{8,72},{9,73},{16,80},{17,81},{24,88},{25,89},{32,96... | collective-permute-start | bytes 940040 | tf_op jit(solution)/shard_map/ppermute | solution.py:33
  90.0 17.2 %collective-permute-start.18 = (f16[136,1152]{1,0:T(8,128)(2,1)S(1)}, f16[136,1152]{1,0:T(8,128)(2,1)S(1)}, u32[]{:S(2)}, u32[]{:S(2)}) collective-permute-start(f16[136,1152]{1,0:T(8,128)(2,1)S(1)} %pad_maximum_fusion.3), channel_id=1, source_target_pairs={{0,128},{1,129},{8,136},{9,137},{16,144},{17,145},{24,152},{25,153... | collective-permute-start | bytes 940040 | tf_op jit(solution)/shard_map/ppermute | solution.py:33
  95.6 11.6 %copy-start.10 = (f32[512,1152]{1,0:T(8,128)S(1)}, f32[512,1152]{1,0:T(8,128)}, u32[]{:S(2)}) copy-start(f32[512,1152]{1,0:T(8,128)} %get-tuple-element.66) | copy-start | bytes 7077892
  95.6 17.9 %collective-permute-start.21 = (f16[256,1152]{1,0:T(8,128)(2,1)S(1)}, f16[256,1152]{1,0:T(8,128)(2,1)S(1)}, u32[]{:S(2)}, u32[]{:S(2)}) collective-permute-start(f16[256,1152]{1,0:T(8,128)(2,1)S(1)} %convolution_convert_fusion), channel_id=1, source_target_pairs={{0,16},{1,17},{8,24},{9,25},{16,0},{17,1},{24,8},{25,9},{32,48},{3... | collective-permute-start | bytes 1769480 | tf_op jit(solution)/shard_map/ppermute | solution.py:33
  96.3 23.1 %collective-permute-start.20 = (f16[256,1152]{1,0:T(8,128)(2,1)S(1)}, f16[256,1152]{1,0:T(8,128)(2,1)S(1)}, u32[]{:S(2)}, u32[]{:S(2)}) collective-permute-start(f16[256,1152]{1,0:T(8,128)(2,1)S(1)} %convolution_convert_fusion.1), channel_id=1, source_target_pairs={{0,8},{1,9},{8,16},{9,17},{16,24},{17,25},{24,0},{25,1},{32,40},{3... | collective-permute-start | bytes 1769480 | tf_op jit(solution)/shard_map/ppermute | solution.py:33
  98.7 23.2 %collective-permute-start.19 = (f16[256,1152]{1,0:T(8,128)(2,1)S(1)}, f16[256,1152]{1,0:T(8,128)(2,1)S(1)}, u32[]{:S(2)}, u32[]{:S(2)}) collective-permute-start(f16[256,1152]{1,0:T(8,128)(2,1)S(1)} %convolution_convert_fusion.2), channel_id=1, source_target_pairs={{0,24},{1,25},{8,0},{9,1},{16,8},{17,9},{24,16},{25,17},{32,56},{3... | collective-permute-start | bytes 1769480 | tf_op jit(solution)/shard_map/ppermute | solution.py:33
  107.5 15.2 %collective-permute-start.22 = (f16[128,1152]{1,0:T(8,128)(2,1)S(1)}, f16[128,1152]{1,0:T(8,128)(2,1)S(1)}, u32[]{:S(2)}, u32[]{:S(2)}) collective-permute-start(f16[128,1152]{1,0:T(8,128)(2,1)S(1)} %subtract_convert_fusion), channel_id=1, source_target_pairs={{0,32},{1,33},{8,40},{9,41},{16,48},{17,49},{24,56},{25,57},{32,64... | collective-permute-start | bytes 884744 | tf_op jit(solution)/shard_map/ppermute | solution.py:33
  108.5 17.9 %collective-permute-start.23 = (f16[128,1152]{1,0:T(8,128)(2,1)S(1)}, f16[128,1152]{1,0:T(8,128)(2,1)S(1)}, u32[]{:S(2)}, u32[]{:S(2)}) collective-permute-start(f16[128,1152]{1,0:T(8,128)(2,1)S(1)} %subtract_convert_fusion), channel_id=1, source_target_pairs={{0,96},{1,97},{8,104},{9,105},{16,112},{17,113},{24,120},{25,121},... | collective-permute-start | bytes 884744 | tf_op jit(solution)/shard_map/ppermute | solution.py:33
  113.5 15.2 %collective-permute-start.24 = (f16[128,1152]{1,0:T(8,128)(2,1)S(1)}, f16[128,1152]{1,0:T(8,128)(2,1)S(1)}, u32[]{:S(2)}, u32[]{:S(2)}) collective-permute-start(f16[128,1152]{1,0:T(8,128)(2,1)S(1)} %subtract_convert_fusion), channel_id=1, source_target_pairs={{0,64},{1,65},{8,72},{9,73},{16,80},{17,81},{24,88},{25,89},{32,96... | collective-permute-start | bytes 884744 | tf_op jit(solution)/shard_map/ppermute | solution.py:33
  123.2 12.3 %collective-permute-start.27 = (f16[40,1152]{1,0:T(8,128)(2,1)S(1)}, f16[40,1152]{1,0:T(8,128)(2,1)S(1)}, u32[]{:S(2)}, u32[]{:S(2)}) collective-permute-start(f16[40,1152]{1,0:T(8,128)(2,1)S(1)} %pad_maximum_fusion.6), channel_id=1, source_target_pairs={{0,132},{1,133},{8,140},{9,141},{16,148},{17,149},{24,156},{25,157... | collective-permute-start | bytes 276488 | tf_op jit(solution)/shard_map/ppermute | solution.py:33
  123.4 12.1 %collective-permute-start.25 = (f16[72,1152]{1,0:T(8,128)(2,1)S(1)}, f16[72,1152]{1,0:T(8,128)(2,1)S(1)}, u32[]{:S(2)}, u32[]{:S(2)}) collective-permute-start(f16[72,1152]{1,0:T(8,128)(2,1)S(1)} %get-tuple-element.76), channel_id=1, source_target_pairs={{0,134},{1,135},{8,142},{9,143},{16,150},{17,151},{24,158},{25,159... | collective-permute-start | bytes 497672 | tf_op jit(solution)/shard_map/ppermute | solution.py:33
  124.8 10.8 %collective-permute-start.26 = (f16[72,1152]{1,0:T(8,128)(2,1)S(1)}, f16[72,1152]{1,0:T(8,128)(2,1)S(1)}, u32[]{:S(2)}, u32[]{:S(2)}) collective-permute-start(f16[72,1152]{1,0:T(8,128)(2,1)S(1)} %get-tuple-element.75), channel_id=1, source_target_pairs={{0,2},{1,3},{8,10},{9,11},{16,18},{17,19},{24,26},{25,27},{32,34},... | collective-permute-start | bytes 497672 | tf_op jit(solution)/shard_map/ppermute | solution.py:33
  126.4 9.2 %collective-permute-start.28 = (f16[32,1152]{1,0:T(8,128)(2,1)S(1)}, f16[32,1152]{1,0:T(8,128)(2,1)S(1)}, u32[]{:S(2)}, u32[]{:S(2)}) collective-permute-start(f16[32,1152]{1,0:T(8,128)(2,1)S(1)} %get-tuple-element.71), channel_id=1, source_target_pairs={{0,4},{1,5},{8,12},{9,13},{16,20},{17,21},{24,28},{25,29},{32,36},... | collective-permute-start | bytes 221192 | tf_op jit(solution)/shard_map/ppermute | solution.py:33

commit v5 on v4

--- a/solution.py
+++ b/solution.py
@@ -256,13 +256,14 @@
 
     quarter = count // 4
     received = move(grad_other, swap=1)
+    total = total[:4]
+    total += move(total, swap=1)
+    total = ring_sum(total, move(total, dx=1), move(total, dx=-1), move(total, dx=2))
+    grad_own, received, total = lax.optimization_barrier((grad_own, received, total))
     parts = [
         (grad_own[k * quarter : (k + 1) * quarter] + received[k * quarter : (k + 1) * quarter]).astype(SEND)
         for k in range(4)
     ]
-    total = total[:4]
-    for bit in (0, 3, 4):
-        total += lax.ppermute(total, AXES, [(i, i ^ (1 << bit)) for i in range(256)])
     own_sums = sums_rows(total, width)
     arrived = [move(jnp.concatenate([part, own_sums]), dy=dy) for part, dy in zip(parts[1:], (1, -1, 2))]
 

time: 138 us -> 137 us (level)
    ppermute x26 -> x30, waiting for transfers between devices: 46 us -> 53.2 us  [move(): return lax.ppermute(value, AXES, shifted(**shift))]
    ppermute x3 -> x0, waiting for transfers between devices: 6.89 us -> none  [per_device(): total += lax.ppermute(total, AXES, [(i, i ^ 1 << bit) for i in range(256)])]
    ppermute x3 -> x0, starting transfers between devices: 2.94 us -> none  [per_device(): total += lax.ppermute(total, AXES, [(i, i ^ 1 << bit) for i in range(256)])]
    ppermute x26 -> x30, starting transfers between devices: 41.8 us -> 44.7 us  [move(): return lax.ppermute(value, AXES, shifted(**shift))]
  transfers between devices with their start and end apart: 29 -> 30, of which waited for: 17 -> 18; matrix products, arithmetic and copies ran while one was open for 5% -> 5% of each run, Pallas kernels for 4% -> 4%
where the time goes in v5:
time: 137 us
  waiting for transfers between devices  53.2 us (39%)
  starting transfers between devices  44.7 us (33%)
  Pallas kernels  14.4 us (11%)
  other arithmetic  11.3 us (8%)
  local copies, waits for them, and re-layouts  7.85 us (6%)
  matrix products  3.51 us (3%)
  between operations  2.3 us (2%)
    ppermute x30, waiting for transfers between devices, move(): return lax.ppermute(value, AXES, shifted(**shift))  53.2 us
    ppermute x30, starting transfers between devices, move(): return lax.ppermute(value, AXES, shifted(**shift))  44.7 us
    pallas_call x1, Pallas kernels, pair_terms(): pl.pallas_call(lambda *refs: pair_kernel(0, *refs), grid=(1,), in_specs=[...  8.4 us
    unnamed x22, local copies, waits for them, and re-layouts  7.19 us
    pallas_call x1, Pallas kernels, pair_terms(): pl.pallas_call(lambda *refs: pair_kernel(1, *refs), grid=(1,), in_specs=[...  4.82 us
    dot_general x4, matrix products, per_device(): lax.dot_general(coef[k], copies, (((0,), (0,)), ((), ())), preferred_elem...  3.51 us
  transfers between devices with their start and end apart: 30, of which 18 were waited for; matrix products, arithmetic and copies ran while one was open for 5% of the time, Pallas kernels for 4%

profile of v5, /device:TPU:6, one launch (start us, length us, event | category | flops | bytes accessed | tf_op | source)
XLA Modules:
  0.0 137.2 jit_solution(6708002100757399962)
XLA Ops:
  0.6 1.0 copy-done
  1.7 2.0 %multiply_reduce_fusion = f32[512]{0:T(512)S(1)} fusion(f32[512,1152]{1,0:T(8,128)} %param.4), kind=kLoop, calls=%fused_computation.5 | loop fusion | flops 1179136 | bytes 2361344 | tf_op jit(solution)/shard_map/reduce_sum | solution.py:53
  4.5 1.7 %fusion.20 = (bf16[512,1152]{1,0:T(8,128)(2,1)S(1)}, f32[512,1152]{1,0:T(8,128)}) fusion(f32[512,1152]{1,0:T(8,128)S(1)} %copy-done.9, f32[512]{0:T(512)S(1)} %get-tuple-element.85), kind=kLoop, calls=%fused_computation.67 | loop fusion | flops 1179648 | bytes 5900288 | tf_op jit(solution)/shard_map/convert_element_type | solution.py:248
  6.2 1.1 copy-done.5
  7.2 3.3 %collective-permute-start.4 = (bf16[32,1152]{1,0:T(8,128)(2,1)S(1)}, bf16[32,1152]{1,0:T(8,128)(2,1)S(1)}, u32[]{:S(2)}, u32[]{:S(2)}) collective-permute-start(bf16[32,1152]{1,0:T(8,128)(2,1)S(1)} %get-tuple-element.38), channel_id=1, source_target_pairs={{0,4},{1,5},{8,12},{9,13},{16,20},{17,21},{24,28},{25,29},{32,36},... | collective-permute-start | bytes 221192 | tf_op jit(solution)/shard_map/ppermute | solution.py:33
  11.0 1.5 %collective-permute-start.2 = (bf16[64,1152]{1,0:T(8,128)(2,1)S(1)}, bf16[64,1152]{1,0:T(8,128)(2,1)S(1)}, u32[]{:S(2)}, u32[]{:S(2)}) collective-permute-start(bf16[64,1152]{1,0:T(8,128)(2,1)S(1)} %get-tuple-element.37.refs_0_), channel_id=1, source_target_pairs={{0,24},{1,25},{8,0},{9,1},{16,8},{17,9},{24,16},{25,17},{32,56},{3... | collective-permute-start | bytes 442376 | tf_op jit(solution)/shard_map/ppermute | solution.py:33
  12.5 1.4 %collective-permute-start.3 = (bf16[64,1152]{1,0:T(8,128)(2,1)S(1)}, bf16[64,1152]{1,0:T(8,128)(2,1)S(1)}, u32[]{:S(2)}, u32[]{:S(2)}) collective-permute-start(bf16[64,1152]{1,0:T(8,128)(2,1)S(1)} %get-tuple-element.37.refs_0_), channel_id=1, source_target_pairs={{0,16},{1,17},{8,24},{9,25},{16,0},{17,1},{24,8},{25,9},{32,48},{3... | collective-permute-start | bytes 442376 | tf_op jit(solution)/shard_map/ppermute | solution.py:33
  13.9 2.6 %collective-permute-done.4.refs_4_ = bf16[32,1152]{1,0:T(8,128)(2,1)S(1)} collective-permute-done((bf16[32,1152]{1,0:T(8,128)(2,1)S(1)}, bf16[32,1152]{1,0:T(8,128)(2,1)S(1)}, u32[]{:S(2)}, u32[]{:S(2)}) %collective-permute-start.4) | collective-permute-done | bytes 73760 | tf_op jit(solution)/shard_map/ppermute | solution.py:33
  16.6 2.6 %collective-permute-start.5 = (bf16[32,1152]{1,0:T(8,128)(2,1)S(1)}, bf16[32,1152]{1,0:T(8,128)(2,1)S(1)}, u32[]{:S(2)}, u32[]{:S(2)}) collective-permute-start(bf16[32,1152]{1,0:T(8,128)(2,1)S(1)} %get-tuple-element.39), channel_id=1, source_target_pairs={{0,132},{1,133},{8,140},{9,141},{16,148},{17,149},{24,156},{25,157... | collective-permute-start | bytes 221192 | tf_op jit(solution)/shard_map/ppermute | solution.py:33
  19.2 2.6 %collective-permute-done.5.refs_5_ = bf16[32,1152]{1,0:T(8,128)(2,1)S(1)} collective-permute-done((bf16[32,1152]{1,0:T(8,128)(2,1)S(1)}, bf16[32,1152]{1,0:T(8,128)(2,1)S(1)}, u32[]{:S(2)}, u32[]{:S(2)}) %collective-permute-start.5) | collective-permute-done | bytes 73760 | tf_op jit(solution)/shard_map/ppermute | solution.py:33
  21.8 1.0 join.1
  22.9 3.0 %collective-permute-start.6 = (bf16[256,1152]{1,0:T(8,128)(2,1)S(1)}, bf16[256,1152]{1,0:T(8,128)(2,1)}, u32[]{:S(2)}, u32[]{:S(2)}) collective-permute-start(bf16[256,1152]{1,0:T(8,128)(2,1)S(1)} %get-tuple-element.40.refs_3_), channel_id=1, source_target_pairs={{0,2},{1,3},{8,10},{9,11},{16,18},{17,19},{24,26},{25,27},{32,34},... | collective-permute-start | bytes 1769480 | tf_op jit(solution)/shard_map/ppermute | solution.py:33
  25.9 2.1 %collective-permute-start.7 = (bf16[256,1152]{1,0:T(8,128)(2,1)S(1)}, bf16[256,1152]{1,0:T(8,128)(2,1)}, u32[]{:S(2)}, u32[]{:S(2)}) collective-permute-start(bf16[256,1152]{1,0:T(8,128)(2,1)S(1)} %get-tuple-element.40.refs_3_), channel_id=1, source_target_pairs={{0,134},{1,135},{8,142},{9,143},{16,150},{17,151},{24,158},{25,159... | collective-permute-start | bytes 1769480 | tf_op jit(solution)/shard_map/ppermute | solution.py:33
  27.9 1.4 %collective-permute-start.10 = (bf16[64,1152]{1,0:T(8,128)(2,1)S(1)}, bf16[64,1152]{1,0:T(8,128)(2,1)S(1)}, u32[]{:S(2)}, u32[]{:S(2)}) collective-permute-start(bf16[64,1152]{1,0:T(8,128)(2,1)S(1)} %get-tuple-element.41.refs_6_), channel_id=1, source_target_pairs={{0,16},{1,17},{8,24},{9,25},{16,0},{17,1},{24,8},{25,9},{32,48},{3... | collective-permute-start | bytes 442376 | tf_op jit(solution)/shard_map/ppermute | solution.py:33
  29.3 2.1 %collective-permute-start.8 = (bf16[64,1152]{1,0:T(8,128)(2,1)S(1)}, bf16[64,1152]{1,0:T(8,128)(2,1)}, u32[]{:S(2)}, u32[]{:S(2)}) collective-permute-start(bf16[64,1152]{1,0:T(8,128)(2,1)S(1)} %get-tuple-element.41.refs_6_), channel_id=1, source_target_pairs={{0,8},{1,9},{8,16},{9,17},{16,24},{17,25},{24,0},{25,1},{32,40},{3... | collective-permute-start | bytes 442376 | tf_op jit(solution)/shard_map/ppermute | solution.py:33
  31.4 3.2 %collective-permute-done.10.refs_9_ = bf16[64,1152]{1,0:T(8,128)(2,1)S(1)} collective-permute-done((bf16[64,1152]{1,0:T(8,128)(2,1)S(1)}, bf16[64,1152]{1,0:T(8,128)(2,1)S(1)}, u32[]{:S(2)}, u32[]{:S(2)}) %collective-permute-start.10) | collective-permute-done | bytes 147488 | tf_op jit(solution)/shard_map/ppermute | solution.py:33
  34.6 1.5 %collective-permute-start.9 = (bf16[64,1152]{1,0:T(8,128)(2,1)S(1)}, bf16[64,1152]{1,0:T(8,128)(2,1)}, u32[]{:S(2)}, u32[]{:S(2)}) collective-permute-start(bf16[64,1152]{1,0:T(8,128)(2,1)S(1)} %get-tuple-element.41.refs_6_), channel_id=1, source_target_pairs={{0,24},{1,25},{8,0},{9,1},{16,8},{17,9},{24,16},{25,17},{32,56},{3... | collective-permute-start | bytes 442376 | tf_op jit(solution)/shard_map/ppermute | solution.py:33
  37.0 4.1 %collective-permute-done.9.refs_8_ = bf16[64,1152]{1,0:T(8,128)(2,1)} collective-permute-done((bf16[64,1152]{1,0:T(8,128)(2,1)S(1)}, bf16[64,1152]{1,0:T(8,128)(2,1)}, u32[]{:S(2)}, u32[]{:S(2)}) %collective-permute-start.9) | collective-permute-done | bytes 147488 | tf_op jit(solution)/shard_map/ppermute | solution.py:33
  41.3 1.0 copy-done.7
  42.3 1.3 copy-done.8
  43.6 8.4 %other_rows.1 = (f32[512,1152]{1,0:T(8,128)}, bf16[4,1024,256]{2,1,0:T(8,128)(2,1)S(1)}, bf16[1024,1152]{1,0:T(8,128)(2,1)S(1)}, bf16[1024,1152]{1,0:T(8,128)(2,1)S(1)}, f32[3,8,1024]{2,1,0:T(8,128)S(1)}) custom-call(f32[2]{0:T(128)S(1)} %pad_maximum_fusion.7.refs_0_, s32[6]{0:T(128)S(1)} %stack.32.refs_1_, bf16[512,1152]{1,0:T(8,128)(2,1)S(1)} %copy-done.8, ...), custom_call_target="tpu_custom_call" | custom-call | flops 2415919104 | bytes 7077888 | tf_op jit(solution)/shard_map/other_rows/pallas_call | solution.py:196
  52.2 4.8 %own_rows.1 = (f32[512,1152]{1,0:T(8,128)S(1)}, bf16[4,1024,256]{2,1,0:T(8,128)(2,1)S(1)}, bf16[1024,1152]{1,0:T(8,128)(2,1)S(1)}, f32[8,128]{1,0:T(8,128)S(1)}) custom-call(f32[2]{0:T(128)S(1)} %pad_maximum_fusion.7.refs_0_, s32[6]{0:T(128)S(1)} %stack.32.refs_1_, bf16[512,1152]{1,0:T(8,128)(2,1)S(1)} %copy-done.6, ...), custom_call_target="tpu_custom_call", output_to_operand_aliasing={{1}: (5, {}), {2}: (6, {})} | custom-call | flops 2415919104 | bytes 7077888 | tf_op jit(solution)/shard_map/own_rows/pallas_call | solution.py:213
  57.1 1.4 %copy-done.2 = f32[512,1152]{1,0:T(8,128)} copy-done((f32[512,1152]{1,0:T(8,128)}, f32[512,1152]{1,0:T(8,128)S(1)}, u32[]{:S(2)}) %copy-start.2) | copy-done | bytes 2359320
  58.5 1.4 %copy-done.3 = bf16[4,1024,256]{2,1,0:T(8,128)(2,1)} copy-done((bf16[4,1024,256]{2,1,0:T(8,128)(2,1)}, bf16[4,1024,256]{2,1,0:T(8,128)(2,1)S(1)}, u32[]{:S(2)}) %copy-start.3) | copy-done | bytes 2097176
  61.2 1.6 %collective-permute-start.13 = (f32[4,128]{1,0:T(4,128)S(1)}, f32[4,128]{1,0:T(4,128)S(1)}, u32[]{:S(2)}, u32[]{:S(2)}) collective-permute-start(f32[4,128]{1,0:T(4,128)S(1)} %slice_add_fusion), channel_id=1, source_target_pairs={{0,16},{1,17},{8,24},{9,25},{16,0},{17,1},{24,8},{25,9},{32,48},{3... | collective-permute-start | bytes 6152 | tf_op jit(solution)/shard_map/ppermute | solution.py:33
  62.9 1.9 %collective-permute-start.14 = (f32[4,128]{1,0:T(4,128)S(1)}, f32[4,128]{1,0:T(4,128)S(1)}, u32[]{:S(2)}, u32[]{:S(2)}) collective-permute-start(f32[4,128]{1,0:T(4,128)S(1)} %slice_add_fusion), channel_id=1, source_target_pairs={{0,8},{1,9},{8,16},{9,17},{16,24},{17,25},{24,0},{25,1},{32,40},{3... | collective-permute-start | bytes 6152 | tf_op jit(solution)/shard_map/ppermute | solution.py:33
  64.9 1.4 %collective-permute-done.13 = f32[4,128]{1,0:T(4,128)S(1)} collective-permute-done((f32[4,128]{1,0:T(4,128)S(1)}, f32[4,128]{1,0:T(4,128)S(1)}, u32[]{:S(2)}, u32[]{:S(2)}) %collective-permute-start.13) | collective-permute-done | bytes 2080 | tf_op jit(solution)/shard_map/ppermute | solution.py:33
  66.5 3.1 %collective-permute-done.15 = f32[4,128]{1,0:T(4,128)S(1)} collective-permute-done((f32[4,128]{1,0:T(4,128)S(1)}, f32[4,128]{1,0:T(4,128)S(1)}, u32[]{:S(2)}, u32[]{:S(2)}) %collective-permute-start.15) | collective-permute-done | bytes 2080 | tf_op jit(solution)/shard_map/ppermute | solution.py:33
  69.6 2.7 %add_convert_fusion.5 = (f16[128,1152]{1,0:T(8,128)(2,1)S(1)}, f16[128,1152]{1,0:T(8,128)(2,1)S(1)}, f16[128,1152]{1,0:T(8,128)(2,1)S(1)}, f16[128,1152]{1,0:T(8,128)(2,1)S(1)}) fusion(f32[512,1152]{1,0:T(8,128)} %collective-permute-done.11, f32[512,1152]{1,0:T(8,128)} %copy-done.2), kind=kLoop, calls=%fused_computation.15 | loop fusion | flops 1179648 | bytes 5898240 | tf_op jit(solution)/shard_map/convert_element_type | solution.py:264
  72.5 1.6 %collective-permute-start.16 = (f16[136,1152]{1,0:T(8,128)(2,1)S(1)}, f16[136,1152]{1,0:T(8,128)(2,1)S(1)}, u32[]{:S(2)}, u32[]{:S(2)}) collective-permute-start(f16[136,1152]{1,0:T(8,128)(2,1)S(1)} %get-tuple-element.83), channel_id=1, source_target_pairs={{0,32},{1,33},{8,40},{9,41},{16,48},{17,49},{24,56},{25,57},{32,64... | collective-permute-start | bytes 940040 | tf_op jit(solution)/shard_map/ppermute | solution.py:33
  74.2 1.7 %collective-permute-start.17 = (f16[136,1152]{1,0:T(8,128)(2,1)S(1)}, f16[136,1152]{1,0:T(8,128)(2,1)S(1)}, u32[]{:S(2)}, u32[]{:S(2)}) collective-permute-start(f16[136,1152]{1,0:T(8,128)(2,1)S(1)} %get-tuple-element.82), channel_id=1, source_target_pairs={{0,96},{1,97},{8,104},{9,105},{16,112},{17,113},{24,120},{25,121},... | collective-permute-start | bytes 940040 | tf_op jit(solution)/shard_map/ppermute | solution.py:33
  75.9 1.9 %collective-permute-start.18 = (f16[136,1152]{1,0:T(8,128)(2,1)S(1)}, f16[136,1152]{1,0:T(8,128)(2,1)S(1)}, u32[]{:S(2)}, u32[]{:S(2)}) collective-permute-start(f16[136,1152]{1,0:T(8,128)(2,1)S(1)} %get-tuple-element.81), channel_id=1, source_target_pairs={{0,64},{1,65},{8,72},{9,73},{16,80},{17,81},{24,88},{25,89},{32,96... | collective-permute-start | bytes 940040 | tf_op jit(solution)/shard_map/ppermute | solution.py:33
  79.6 3.4 %collective-permute-done.16 = f16[136,1152]{1,0:T(8,128)(2,1)S(1)} collective-permute-done((f16[136,1152]{1,0:T(8,128)(2,1)S(1)}, f16[136,1152]{1,0:T(8,128)(2,1)S(1)}, u32[]{:S(2)}, u32[]{:S(2)}) %collective-permute-start.16) | collective-permute-done | bytes 313376 | tf_op jit(solution)/shard_map/ppermute | solution.py:33
  83.0 5.1 %collective-permute-done.17 = f16[136,1152]{1,0:T(8,128)(2,1)S(1)} collective-permute-done((f16[136,1152]{1,0:T(8,128)(2,1)S(1)}, f16[136,1152]{1,0:T(8,128)(2,1)S(1)}, u32[]{:S(2)}, u32[]{:S(2)}) %collective-permute-start.17) | collective-permute-done | bytes 313376 | tf_op jit(solution)/shard_map/ppermute | solution.py:33
  88.1 1.6 %collective-permute-done.18 = f16[136,1152]{1,0:T(8,128)(2,1)S(1)} collective-permute-done((f16[136,1152]{1,0:T(8,128)(2,1)S(1)}, f16[136,1152]{1,0:T(8,128)(2,1)S(1)}, u32[]{:S(2)}, u32[]{:S(2)}) %collective-permute-start.18) | collective-permute-done | bytes 313376 | tf_op jit(solution)/shard_map/ppermute | solution.py:33
  90.0 4.3 %collective-permute-start.19 = (f16[136,1152]{1,0:T(8,128)(2,1)S(1)}, f16[136,1152]{1,0:T(8,128)(2,1)S(1)}, u32[]{:S(2)}, u32[]{:S(2)}) collective-permute-start(f16[136,1152]{1,0:T(8,128)(2,1)S(1)} %pad_maximum_fusion.3), channel_id=1, source_target_pairs={{0,128},{1,129},{8,136},{9,137},{16,144},{17,145},{24,152},{25,153... | collective-permute-start | bytes 940040 | tf_op jit(solution)/shard_map/ppermute | solution.py:33
  95.3 1.8 %collective-permute-start.21 = (f16[256,1152]{1,0:T(8,128)(2,1)S(1)}, f16[256,1152]{1,0:T(8,128)(2,1)S(1)}, u32[]{:S(2)}, u32[]{:S(2)}) collective-permute-start(f16[256,1152]{1,0:T(8,128)(2,1)S(1)} %convolution_convert_fusion.1), channel_id=1, source_target_pairs={{0,8},{1,9},{8,16},{9,17},{16,24},{17,25},{24,0},{25,1},{32,40},{3... | collective-permute-start | bytes 1769480 | tf_op jit(solution)/shard_map/ppermute | solution.py:33
  98.3 9.5 %collective-permute-done.19 = f16[136,1152]{1,0:T(8,128)(2,1)S(1)} collective-permute-done((f16[136,1152]{1,0:T(8,128)(2,1)S(1)}, f16[136,1152]{1,0:T(8,128)(2,1)S(1)}, u32[]{:S(2)}, u32[]{:S(2)}) %collective-permute-start.19) | collective-permute-done | bytes 313376 | tf_op jit(solution)/shard_map/ppermute | solution.py:33
  109.1 2.4 %collective-permute-start.24 = (f16[128,1152]{1,0:T(8,128)(2,1)S(1)}, f16[128,1152]{1,0:T(8,128)(2,1)S(1)}, u32[]{:S(2)}, u32[]{:S(2)}) collective-permute-start(f16[128,1152]{1,0:T(8,128)(2,1)S(1)} %subtract_convert_fusion), channel_id=1, source_target_pairs={{0,96},{1,97},{8,104},{9,105},{16,112},{17,113},{24,120},{25,121},... | collective-permute-start | bytes 884744 | tf_op jit(solution)/shard_map/ppermute | solution.py:33
  111.7 1.3 collective-permute-done.22
  113.8 6.2 %collective-permute-done.21 = f16[256,1152]{1,0:T(8,128)(2,1)S(1)} collective-permute-done((f16[256,1152]{1,0:T(8,128)(2,1)S(1)}, f16[256,1152]{1,0:T(8,128)(2,1)S(1)}, u32[]{:S(2)}, u32[]{:S(2)}) %collective-permute-start.21) | collective-permute-done | bytes 589856 | tf_op jit(solution)/shard_map/ppermute | solution.py:33
  120.0 2.1 %collective-permute-done.20 = f16[256,1152]{1,0:T(8,128)(2,1)S(1)} collective-permute-done((f16[256,1152]{1,0:T(8,128)(2,1)S(1)}, f16[256,1152]{1,0:T(8,128)(2,1)S(1)}, u32[]{:S(2)}, u32[]{:S(2)}) %collective-permute-start.20) | collective-permute-done | bytes 589856 | tf_op jit(solution)/shard_map/ppermute | solution.py:33
  122.1 1.3 collective-permute-done.23
  124.1 1.3 collective-permute-start.26
  125.4 1.5 %collective-permute-start.27 = (f16[72,1152]{1,0:T(8,128)(2,1)S(1)}, f16[72,1152]{1,0:T(8,128)(2,1)S(1)}, u32[]{:S(2)}, u32[]{:S(2)}) collective-permute-start(f16[72,1152]{1,0:T(8,128)(2,1)S(1)} %get-tuple-element.79), channel_id=1, source_target_pairs={{0,2},{1,3},{8,10},{9,11},{16,18},{17,19},{24,26},{25,27},{32,34},... | collective-permute-start | bytes 497672 | tf_op jit(solution)/shard_map/ppermute | solution.py:33
  127.0 2.2 %collective-permute-start.29 = (f16[32,1152]{1,0:T(8,128)(2,1)S(1)}, f16[32,1152]{1,0:T(8,128)(2,1)S(1)}, u32[]{:S(2)}, u32[]{:S(2)}) collective-permute-start(f16[32,1152]{1,0:T(8,128)(2,1)S(1)} %get-tuple-element.75), channel_id=1, source_target_pairs={{0,4},{1,5},{8,12},{9,13},{16,20},{17,21},{24,28},{25,29},{32,36},... | collective-permute-start | bytes 221192 | tf_op jit(solution)/shard_map/ppermute | solution.py:33
  129.4 1.7 %convert_multiply_fusion = f32[512,1152]{1,0:T(8,128)} fusion(f16[512,1152]{1,0:T(8,128)(2,1)S(1)} %constant_dynamic-update-slice_fusion, f32[512]{0:T(512)S(1)} %get-tuple-element.84), kind=kLoop, calls=%fused_computation.4 | loop fusion | flops 1179648 | bytes 3540992 | tf_op jit(solution)/shard_map/mul | solution.py:300
  131.0 4.4 %collective-permute-done.29 = f16[32,1152]{1,0:T(8,128)(2,1)S(1)} collective-permute-done((f16[32,1152]{1,0:T(8,128)(2,1)S(1)}, f16[32,1152]{1,0:T(8,128)(2,1)S(1)}, u32[]{:S(2)}, u32[]{:S(2)}) %collective-permute-start.29) | collective-permute-done | bytes 73760 | tf_op jit(solution)/shard_map/ppermute | solution.py:33
  (84 shorter events, 12.1 us)
Async XLA Ops:
  0.6 1.0 copy-start
  1.6 2.9 %copy-start.9 = (f32[512,1152]{1,0:T(8,128)S(1)}, f32[512,1152]{1,0:T(8,128)}, u32[]{:S(2)}) copy-start(f32[512,1152]{1,0:T(8,128)} %param.4) | copy-start | bytes 7077892
  6.2 35.1 %collective-permute-start = (bf16[512,1152]{1,0:T(8,128)(2,1)S(1)}, bf16[512,1152]{1,0:T(8,128)(2,1)S(1)}, u32[]{:S(2)}, u32[]{:S(2)}) collective-permute-start(bf16[512,1152]{1,0:T(8,128)(2,1)S(1)} %get-tuple-element.69.refs_2_), channel_id=1, source_target_pairs={{0,1},{1,0},{8,9},{9,8},{16,17},{17,16},{24,25},{25,24},{32,33},{3... | collective-permute-start | bytes 3538952 | tf_op jit(solution)/shard_map/ppermute | solution.py:33
  6.2 1.1 copy-start.5
  7.2 9.3 %collective-permute-start.4 = (bf16[32,1152]{1,0:T(8,128)(2,1)S(1)}, bf16[32,1152]{1,0:T(8,128)(2,1)S(1)}, u32[]{:S(2)}, u32[]{:S(2)}) collective-permute-start(bf16[32,1152]{1,0:T(8,128)(2,1)S(1)} %get-tuple-element.38), channel_id=1, source_target_pairs={{0,4},{1,5},{8,12},{9,13},{16,20},{17,21},{24,28},{25,29},{32,36},... | collective-permute-start | bytes 221192 | tf_op jit(solution)/shard_map/ppermute | solution.py:33
  10.5 11.3 %collective-permute-start.1 = (bf16[64,1152]{1,0:T(8,128)(2,1)S(1)}, bf16[64,1152]{1,0:T(8,128)(2,1)S(1)}, u32[]{:S(2)}, u32[]{:S(2)}) collective-permute-start(bf16[64,1152]{1,0:T(8,128)(2,1)S(1)} %get-tuple-element.37.refs_0_), channel_id=1, source_target_pairs={{0,8},{1,9},{8,16},{9,17},{16,24},{17,25},{24,0},{25,1},{32,40},{3... | collective-permute-start | bytes 442376 | tf_op jit(solution)/shard_map/ppermute | solution.py:33
  11.0 10.8 %collective-permute-start.2 = (bf16[64,1152]{1,0:T(8,128)(2,1)S(1)}, bf16[64,1152]{1,0:T(8,128)(2,1)S(1)}, u32[]{:S(2)}, u32[]{:S(2)}) collective-permute-start(bf16[64,1152]{1,0:T(8,128)(2,1)S(1)} %get-tuple-element.37.refs_0_), channel_id=1, source_target_pairs={{0,24},{1,25},{8,0},{9,1},{16,8},{17,9},{24,16},{25,17},{32,56},{3... | collective-permute-start | bytes 442376 | tf_op jit(solution)/shard_map/ppermute | solution.py:33
  12.5 9.3 %collective-permute-start.3 = (bf16[64,1152]{1,0:T(8,128)(2,1)S(1)}, bf16[64,1152]{1,0:T(8,128)(2,1)S(1)}, u32[]{:S(2)}, u32[]{:S(2)}) collective-permute-start(bf16[64,1152]{1,0:T(8,128)(2,1)S(1)} %get-tuple-element.37.refs_0_), channel_id=1, source_target_pairs={{0,16},{1,17},{8,24},{9,25},{16,0},{17,1},{24,8},{25,9},{32,48},{3... | collective-permute-start | bytes 442376 | tf_op jit(solution)/shard_map/ppermute | solution.py:33
  16.6 5.3 %collective-permute-start.5 = (bf16[32,1152]{1,0:T(8,128)(2,1)S(1)}, bf16[32,1152]{1,0:T(8,128)(2,1)S(1)}, u32[]{:S(2)}, u32[]{:S(2)}) collective-permute-start(bf16[32,1152]{1,0:T(8,128)(2,1)S(1)} %get-tuple-element.39), channel_id=1, source_target_pairs={{0,132},{1,133},{8,140},{9,141},{16,148},{17,149},{24,156},{25,157... | collective-permute-start | bytes 221192 | tf_op jit(solution)/shard_map/ppermute | solution.py:33
  22.9 18.2 %collective-permute-start.6 = (bf16[256,1152]{1,0:T(8,128)(2,1)S(1)}, bf16[256,1152]{1,0:T(8,128)(2,1)}, u32[]{:S(2)}, u32[]{:S(2)}) collective-permute-start(bf16[256,1152]{1,0:T(8,128)(2,1)S(1)} %get-tuple-element.40.refs_3_), channel_id=1, source_target_pairs={{0,2},{1,3},{8,10},{9,11},{16,18},{17,19},{24,26},{25,27},{32,34},... | collective-permute-start | bytes 1769480 | tf_op jit(solution)/shard_map/ppermute | solution.py:33
  25.9 15.4 %collective-permute-start.7 = (bf16[256,1152]{1,0:T(8,128)(2,1)S(1)}, bf16[256,1152]{1,0:T(8,128)(2,1)}, u32[]{:S(2)}, u32[]{:S(2)}) collective-permute-start(bf16[256,1152]{1,0:T(8,128)(2,1)S(1)} %get-tuple-element.40.refs_3_), channel_id=1, source_target_pairs={{0,134},{1,135},{8,142},{9,143},{16,150},{17,151},{24,158},{25,159... | collective-permute-start | bytes 1769480 | tf_op jit(solution)/shard_map/ppermute | solution.py:33
  27.9 6.7 %collective-permute-start.10 = (bf16[64,1152]{1,0:T(8,128)(2,1)S(1)}, bf16[64,1152]{1,0:T(8,128)(2,1)S(1)}, u32[]{:S(2)}, u32[]{:S(2)}) collective-permute-start(bf16[64,1152]{1,0:T(8,128)(2,1)S(1)} %get-tuple-element.41.refs_6_), channel_id=1, source_target_pairs={{0,16},{1,17},{8,24},{9,25},{16,0},{17,1},{24,8},{25,9},{32,48},{3... | collective-permute-start | bytes 442376 | tf_op jit(solution)/shard_map/ppermute | solution.py:33
  29.3 7.6 %collective-permute-start.8 = (bf16[64,1152]{1,0:T(8,128)(2,1)S(1)}, bf16[64,1152]{1,0:T(8,128)(2,1)}, u32[]{:S(2)}, u32[]{:S(2)}) collective-permute-start(bf16[64,1152]{1,0:T(8,128)(2,1)S(1)} %get-tuple-element.41.refs_6_), channel_id=1, source_target_pairs={{0,8},{1,9},{8,16},{9,17},{16,24},{17,25},{24,0},{25,1},{32,40},{3... | collective-permute-start | bytes 442376 | tf_op jit(solution)/shard_map/ppermute | solution.py:33
  34.6 6.5 %collective-permute-start.9 = (bf16[64,1152]{1,0:T(8,128)(2,1)S(1)}, bf16[64,1152]{1,0:T(8,128)(2,1)}, u32[]{:S(2)}, u32[]{:S(2)}) collective-permute-start(bf16[64,1152]{1,0:T(8,128)(2,1)S(1)} %get-tuple-element.41.refs_6_), channel_id=1, source_target_pairs={{0,24},{1,25},{8,0},{9,1},{16,8},{17,9},{24,16},{25,17},{32,56},{3... | collective-permute-start | bytes 442376 | tf_op jit(solution)/shard_map/ppermute | solution.py:33
  37.0 15.2 %copy-start.1 = (f32[64,1152]{1,0:T(8,128)S(1)}, f32[64,1152]{1,0:T(8,128)}, u32[]{:S(2)}) copy-start(f32[64,1152]{1,0:T(8,128)} %text_ref.1) | copy-start | bytes 884740
  37.0 15.3 %copy-start.6 = (bf16[512,1152]{1,0:T(8,128)(2,1)S(1)}, bf16[512,1152]{1,0:T(8,128)(2,1)}, u32[]{:S(2)}) copy-start(bf16[512,1152]{1,0:T(8,128)(2,1)} %copy-done.5) | copy-start | bytes 3538948
  41.3 1.0 copy-start.7
  42.3 1.3 copy-start.8
  52.0 17.5 %collective-permute-start.11 = (f32[512,1152]{1,0:T(8,128)}, f32[512,1152]{1,0:T(8,128)}, u32[]{:S(2)}, u32[]{:S(2)}) collective-permute-start(f32[512,1152]{1,0:T(8,128)} %get-tuple-element.49), channel_id=1, source_target_pairs={{0,1},{1,0},{8,9},{9,8},{16,17},{17,16},{24,25},{25,24},{32,33},{3... | collective-permute-start | bytes 7077896 | tf_op jit(solution)/shard_map/ppermute | solution.py:33
  57.1 1.4 %copy-start.2 = (f32[512,1152]{1,0:T(8,128)}, f32[512,1152]{1,0:T(8,128)S(1)}, u32[]{:S(2)}) copy-start(f32[512,1152]{1,0:T(8,128)S(1)} %get-tuple-element.51) | copy-start | bytes 7077892
  58.5 1.4 %copy-start.3 = (bf16[4,1024,256]{2,1,0:T(8,128)(2,1)}, bf16[4,1024,256]{2,1,0:T(8,128)(2,1)S(1)}, u32[]{:S(2)}) copy-start(bf16[4,1024,256]{2,1,0:T(8,128)(2,1)S(1)} %get-tuple-element.55) | copy-start | bytes 6291460
  59.9 1.3 collective-permute-start.12
  61.2 5.1 %collective-permute-start.13 = (f32[4,128]{1,0:T(4,128)S(1)}, f32[4,128]{1,0:T(4,128)S(1)}, u32[]{:S(2)}, u32[]{:S(2)}) collective-permute-start(f32[4,128]{1,0:T(4,128)S(1)} %slice_add_fusion), channel_id=1, source_target_pairs={{0,16},{1,17},{8,24},{9,25},{16,0},{17,1},{24,8},{25,9},{32,48},{3... | collective-permute-start | bytes 6152 | tf_op jit(solution)/shard_map/ppermute | solution.py:33
  62.9 3.6 %collective-permute-start.14 = (f32[4,128]{1,0:T(4,128)S(1)}, f32[4,128]{1,0:T(4,128)S(1)}, u32[]{:S(2)}, u32[]{:S(2)}) collective-permute-start(f32[4,128]{1,0:T(4,128)S(1)} %slice_add_fusion), channel_id=1, source_target_pairs={{0,8},{1,9},{8,16},{9,17},{16,24},{17,25},{24,0},{25,1},{32,40},{3... | collective-permute-start | bytes 6152 | tf_op jit(solution)/shard_map/ppermute | solution.py:33
  64.8 4.8 %collective-permute-start.15 = (f32[4,128]{1,0:T(4,128)S(1)}, f32[4,128]{1,0:T(4,128)S(1)}, u32[]{:S(2)}, u32[]{:S(2)}) collective-permute-start(f32[4,128]{1,0:T(4,128)S(1)} %slice_add_fusion), channel_id=1, source_target_pairs={{0,24},{1,25},{8,0},{9,1},{16,8},{17,9},{24,16},{25,17},{32,56},{3... | collective-permute-start | bytes 6152 | tf_op jit(solution)/shard_map/ppermute | solution.py:33
  69.6 8.3 %copy-start.4 = (bf16[4,1024,256]{2,1,0:T(8,128)(2,1)S(1)}, bf16[4,1024,256]{2,1,0:T(8,128)(2,1)}, u32[]{:S(2)}) copy-start(bf16[4,1024,256]{2,1,0:T(8,128)(2,1)} %copy-done.3) | copy-start | bytes 6291460
  72.5 10.5 %collective-permute-start.16 = (f16[136,1152]{1,0:T(8,128)(2,1)S(1)}, f16[136,1152]{1,0:T(8,128)(2,1)S(1)}, u32[]{:S(2)}, u32[]{:S(2)}) collective-permute-start(f16[136,1152]{1,0:T(8,128)(2,1)S(1)} %get-tuple-element.83), channel_id=1, source_target_pairs={{0,32},{1,33},{8,40},{9,41},{16,48},{17,49},{24,56},{25,57},{32,64... | collective-permute-start | bytes 940040 | tf_op jit(solution)/shard_map/ppermute | solution.py:33
  74.2 14.0 %collective-permute-start.17 = (f16[136,1152]{1,0:T(8,128)(2,1)S(1)}, f16[136,1152]{1,0:T(8,128)(2,1)S(1)}, u32[]{:S(2)}, u32[]{:S(2)}) collective-permute-start(f16[136,1152]{1,0:T(8,128)(2,1)S(1)} %get-tuple-element.82), channel_id=1, source_target_pairs={{0,96},{1,97},{8,104},{9,105},{16,112},{17,113},{24,120},{25,121},... | collective-permute-start | bytes 940040 | tf_op jit(solution)/shard_map/ppermute | solution.py:33
  75.9 13.8 %collective-permute-start.18 = (f16[136,1152]{1,0:T(8,128)(2,1)S(1)}, f16[136,1152]{1,0:T(8,128)(2,1)S(1)}, u32[]{:S(2)}, u32[]{:S(2)}) collective-permute-start(f16[136,1152]{1,0:T(8,128)(2,1)S(1)} %get-tuple-element.81), channel_id=1, source_target_pairs={{0,64},{1,65},{8,72},{9,73},{16,80},{17,81},{24,88},{25,89},{32,96... | collective-permute-start | bytes 940040 | tf_op jit(solution)/shard_map/ppermute | solution.py:33
  90.0 17.8 %collective-permute-start.19 = (f16[136,1152]{1,0:T(8,128)(2,1)S(1)}, f16[136,1152]{1,0:T(8,128)(2,1)S(1)}, u32[]{:S(2)}, u32[]{:S(2)}) collective-permute-start(f16[136,1152]{1,0:T(8,128)(2,1)S(1)} %pad_maximum_fusion.3), channel_id=1, source_target_pairs={{0,128},{1,129},{8,136},{9,137},{16,144},{17,145},{24,152},{25,153... | collective-permute-start | bytes 940040 | tf_op jit(solution)/shard_map/ppermute | solution.py:33
  95.2 12.6 %copy-start.10 = (f32[512,1152]{1,0:T(8,128)S(1)}, f32[512,1152]{1,0:T(8,128)}, u32[]{:S(2)}) copy-start(f32[512,1152]{1,0:T(8,128)} %get-tuple-element.70) | copy-start | bytes 7077892
  95.2 17.9 %collective-permute-start.22 = (f16[256,1152]{1,0:T(8,128)(2,1)S(1)}, f16[256,1152]{1,0:T(8,128)(2,1)S(1)}, u32[]{:S(2)}, u32[]{:S(2)}) collective-permute-start(f16[256,1152]{1,0:T(8,128)(2,1)S(1)} %convolution_convert_fusion), channel_id=1, source_target_pairs={{0,16},{1,17},{8,24},{9,25},{16,0},{17,1},{24,8},{25,9},{32,48},{3... | collective-permute-start | bytes 1769480 | tf_op jit(solution)/shard_map/ppermute | solution.py:33
  95.3 24.7 %collective-permute-start.21 = (f16[256,1152]{1,0:T(8,128)(2,1)S(1)}, f16[256,1152]{1,0:T(8,128)(2,1)S(1)}, u32[]{:S(2)}, u32[]{:S(2)}) collective-permute-start(f16[256,1152]{1,0:T(8,128)(2,1)S(1)} %convolution_convert_fusion.1), channel_id=1, source_target_pairs={{0,8},{1,9},{8,16},{9,17},{16,24},{17,25},{24,0},{25,1},{32,40},{3... | collective-permute-start | bytes 1769480 | tf_op jit(solution)/shard_map/ppermute | solution.py:33
  97.1 25.0 %collective-permute-start.20 = (f16[256,1152]{1,0:T(8,128)(2,1)S(1)}, f16[256,1152]{1,0:T(8,128)(2,1)S(1)}, u32[]{:S(2)}, u32[]{:S(2)}) collective-permute-start(f16[256,1152]{1,0:T(8,128)(2,1)S(1)} %convolution_convert_fusion.2), channel_id=1, source_target_pairs={{0,24},{1,25},{8,0},{9,1},{16,8},{17,9},{24,16},{25,17},{32,56},{3... | collective-permute-start | bytes 1769480 | tf_op jit(solution)/shard_map/ppermute | solution.py:33
  108.2 15.2 %collective-permute-start.23 = (f16[128,1152]{1,0:T(8,128)(2,1)S(1)}, f16[128,1152]{1,0:T(8,128)(2,1)S(1)}, u32[]{:S(2)}, u32[]{:S(2)}) collective-permute-start(f16[128,1152]{1,0:T(8,128)(2,1)S(1)} %subtract_convert_fusion), channel_id=1, source_target_pairs={{0,32},{1,33},{8,40},{9,41},{16,48},{17,49},{24,56},{25,57},{32,64... | collective-permute-start | bytes 884744 | tf_op jit(solution)/shard_map/ppermute | solution.py:33
  109.1 17.9 %collective-permute-start.24 = (f16[128,1152]{1,0:T(8,128)(2,1)S(1)}, f16[128,1152]{1,0:T(8,128)(2,1)S(1)}, u32[]{:S(2)}, u32[]{:S(2)}) collective-permute-start(f16[128,1152]{1,0:T(8,128)(2,1)S(1)} %subtract_convert_fusion), channel_id=1, source_target_pairs={{0,96},{1,97},{8,104},{9,105},{16,112},{17,113},{24,120},{25,121},... | collective-permute-start | bytes 884744 | tf_op jit(solution)/shard_map/ppermute | solution.py:33
  113.1 16.3 %collective-permute-start.25 = (f16[128,1152]{1,0:T(8,128)(2,1)S(1)}, f16[128,1152]{1,0:T(8,128)(2,1)S(1)}, u32[]{:S(2)}, u32[]{:S(2)}) collective-permute-start(f16[128,1152]{1,0:T(8,128)(2,1)S(1)} %subtract_convert_fusion), channel_id=1, source_target_pairs={{0,64},{1,65},{8,72},{9,73},{16,80},{17,81},{24,88},{25,89},{32,96... | collective-permute-start | bytes 884744 | tf_op jit(solution)/shard_map/ppermute | solution.py:33
  123.9 11.5 %collective-permute-start.28 = (f16[40,1152]{1,0:T(8,128)(2,1)S(1)}, f16[40,1152]{1,0:T(8,128)(2,1)S(1)}, u32[]{:S(2)}, u32[]{:S(2)}) collective-permute-start(f16[40,1152]{1,0:T(8,128)(2,1)S(1)} %pad_maximum_fusion.6), channel_id=1, source_target_pairs={{0,132},{1,133},{8,140},{9,141},{16,148},{17,149},{24,156},{25,157... | collective-permute-start | bytes 276488 | tf_op jit(solution)/shard_map/ppermute | solution.py:33
  124.1 11.4 %collective-permute-start.26 = (f16[72,1152]{1,0:T(8,128)(2,1)S(1)}, f16[72,1152]{1,0:T(8,128)(2,1)S(1)}, u32[]{:S(2)}, u32[]{:S(2)}) collective-permute-start(f16[72,1152]{1,0:T(8,128)(2,1)S(1)} %get-tuple-element.80), channel_id=1, source_target_pairs={{0,134},{1,135},{8,142},{9,143},{16,150},{17,151},{24,158},{25,159... | collective-permute-start | bytes 497672 | tf_op jit(solution)/shard_map/ppermute | solution.py:33
  125.4 10.1 %collective-permute-start.27 = (f16[72,1152]{1,0:T(8,128)(2,1)S(1)}, f16[72,1152]{1,0:T(8,128)(2,1)S(1)}, u32[]{:S(2)}, u32[]{:S(2)}) collective-permute-start(f16[72,1152]{1,0:T(8,128)(2,1)S(1)} %get-tuple-element.79), channel_id=1, source_target_pairs={{0,2},{1,3},{8,10},{9,11},{16,18},{17,19},{24,26},{25,27},{32,34},... | collective-permute-start | bytes 497672 | tf_op jit(solution)/shard_map/ppermute | solution.py:33
  127.0 8.4 %collective-permute-start.29 = (f16[32,1152]{1,0:T(8,128)(2,1)S(1)}, f16[32,1152]{1,0:T(8,128)(2,1)S(1)}, u32[]{:S(2)}, u32[]{:S(2)}) collective-permute-start(f16[32,1152]{1,0:T(8,128)(2,1)S(1)} %get-tuple-element.75), channel_id=1, source_target_pairs={{0,4},{1,5},{8,12},{9,13},{16,20},{17,21},{24,28},{25,29},{32,36},... | collective-permute-start | bytes 221192 | tf_op jit(solution)/shard_map/ppermute | solution.py:33
